TPU v7x, 32 devices: a whole 2x2x4 slice. The times are simulated.
32 devices in a mesh: seq: 4 (over x, core), shard: 8 (over z, y).
Axes of the slice: x: 2, y: 2, z: 4, core: 2. Of those that a mesh axis runs over, the one named last changes fastest.
Arguments:
- inputs: bfloat16 [8, 512, 2048], P('shard', 'seq'), may hold values from -6 to 6
- seq_ids: int32 [8, 512], P('shard', 'seq'), may hold values from 0 to 2, as said below
- routes: int32 [8, 512, 8], P('shard', 'seq'), may hold values from 0 to 31, all different within a row; in each aligned block of 128 rows (0 to 127, 128 to 255, ..., all dimensions but the last counted through in order) at most 40 rows name the same one
- norm1_gain: bfloat16 [2048], P('shard'), may hold values from 0.5 to 1.5
- w_query: bfloat16 [2048, 4096], P('shard'), may hold values from -0.125 to 0.125
- key_weight: bfloat16 [2048, 512], P('shard'), may hold values from -0.125 to 0.125
- value_weight: bfloat16 [2048, 512], P('shard'), may hold values from -0.125 to 0.125
- q_gain: bfloat16 [128], P('shard'), may hold values from 0.796875 to 1.59375
- k_gain: bfloat16 [128], P('shard'), may hold values from 0.5 to 1.5
- w_out: bfloat16 [4096, 2048], P('shard'), may hold values from -1.5 to 1.5
- norm2_gain: bfloat16 [2048], P('shard'), may hold values from 0.5 to 1.5
- w_router: bfloat16 [2048, 32], P('shard'), may hold values from -0.0625 to 0.0625
- w_gate: bfloat16 [32, 2048, 768], P(('seq', 'shard')), may hold values from -0.125 to 0.125
- w_up: bfloat16 [32, 2048, 768], P(('seq', 'shard')), may hold values from -0.125 to 0.125
- w_down: bfloat16 [32, 768, 2048], P(('seq', 'shard')), may hold values from -0.875 to 0.875
- cotangent: bfloat16 [8, 512, 2048], P('shard', 'seq'), may hold values from -6 to 6
Outputs:
- output: bfloat16 [8, 512, 2048], P('shard', 'seq')
- grad_inputs: float32 [8, 512, 2048], P('shard', 'seq')
- grad_norm1_gain: float32 [2048], P('shard')
- grad_w_query: float32 [2048, 4096], P('shard')
- grad_w_key: float32 [2048, 512], P('shard')
- grad_w_value: float32 [2048, 512], P('shard')
- grad_q_gain: float32 [128], P('shard')
- grad_k_gain: float32 [128], P('shard')
- grad_w_out: float32 [4096, 2048], P('shard')
- grad_norm2_gain: float32 [2048], P('shard')
- grad_w_router: float32 [2048, 32], P('shard')
- grad_w_gate: float32 [32, 2048, 768], P(('seq', 'shard'))
- grad_w_up: float32 [32, 2048, 768], P(('seq', 'shard'))
- grad_w_down: float32 [32, 768, 2048], P(('seq', 'shard'))
Inputs may be any that keep to these rules, and one draw needn't show every extreme that they name: `seq_ids`: along each row the ids form three runs 0, 1, 2 in this order; the run of 0 has 1 to 64 tokens, the run of 2 has 1 to 64 tokens. `routes`: among the 128 tokens of one device no expert is named more than 40 times; some expert is named exactly 40 times.
All inputs are finite; a program needn't handle non-finite values.
Results may differ from a plain program's by a relative error of at most 0.024.
Values may be sent and summed in bfloat16 or wider, within the bound.
No kernel may reach another device: no remote copies, remote signals or barrier semaphores. Data moves between devices by JAX's collectives and lax.ppermute only.
A program may use at most 256 MiB of HBM per device.

v0:
```python
import jax
import jax.numpy as jnp
from jax import lax
from jax.sharding import PartitionSpec as P

HQ = 32
KEY_VALUE_HEADS = 4
HEAD_DIMENSION = 128
TOPK = 8


EPSILON = 1e-06
ROPE_BASE = 1000000.0
NEGATIVE = -1e30
EXACT_PRECISION = lax.Precision.HIGHEST


def rope_tables(positions, head_size):
    half_size = head_size // 2
    inverse = ROPE_BASE ** (-2.0 * jnp.arange(half_size, dtype=jnp.float32) / head_size)
    angles = positions.astype(jnp.float32)[:, None] * inverse[None, :]
    return (jnp.cos(angles), jnp.sin(angles))


def apply_rotary(values, cosine_table, sine_values):
    half_size = values.shape[-1] // 2
    first_half = values[..., :half_size]
    second_half = values[..., half_size:]
    cos_b = cosine_table[:, None, :]
    sin_b = sine_values[:, None, :]
    return jnp.concatenate(
        [first_half * cos_b - second_half * sin_b, second_half * cos_b + first_half * sin_b],
        axis=-1,
    )


def root_mean_scale(values):
    return lax.rsqrt(jnp.mean(values * values, axis=-1, keepdims=True) + EPSILON)


def rms_back(grad_out, values, gain):
    factor = root_mean_scale(values)
    normed = values * factor
    grad_norm = grad_out * gain
    grad_values = factor * (
        grad_norm - normed * jnp.mean(grad_norm * normed, axis=-1, keepdims=True)
    )
    return (grad_values, grad_out * normed)


def block_mask(row_ids, first_row, block_rows, key_count):
    query_pos = first_row + jnp.arange(block_rows)
    key_pos = jnp.arange(key_count)
    causal = key_pos[None, :] <= query_pos[:, None]
    same_doc = row_ids[first_row : first_row + block_rows][:, None] == row_ids[None, :key_count]
    return causal & same_doc


def block_scores(queries, keys, row_ids, first_row, block_rows):
    last_row = first_row + block_rows
    scores = jnp.einsum(
        "qhd,kd->hqk",
        queries[first_row:last_row],
        keys[:last_row],
        preferred_element_type=jnp.float32,
    ) * queries.shape[-1] ** (-0.5)
    allowed = block_mask(row_ids, first_row, block_rows, last_row)
    return jnp.where(allowed[None], scores, NEGATIVE)


def attend_forward(queries, keys, values, row_ids, block_rows):
    length = keys.shape[0]
    outputs = []
    totals = []
    for first_row in range(0, length, block_rows):
        last_row = first_row + block_rows
        scores = block_scores(queries, keys, row_ids, first_row, block_rows)
        highest = jnp.max(scores, axis=-1, keepdims=True)
        exp_terms = jnp.exp(scores - highest)
        row_total = jnp.sum(exp_terms, axis=-1, keepdims=True)
        weights_bf = (exp_terms / row_total).astype(jnp.bfloat16)
        outputs.append(
            jnp.einsum(
                "hqk,kd->qhd", weights_bf, values[:last_row], preferred_element_type=jnp.float32
            ).astype(jnp.bfloat16)
        )
        totals.append((highest + jnp.log(row_total))[..., 0])
    return (jnp.concatenate(outputs, axis=0), jnp.concatenate(totals, axis=1))


def attend_backward(queries, keys, values, grad_heads, log_totals, row_ids, block_rows):
    length = keys.shape[0]
    scale_factor = queries.shape[-1] ** (-0.5)
    grad_keys = jnp.zeros(keys.shape, jnp.float32)
    grad_values = jnp.zeros(values.shape, jnp.float32)
    grad_parts = []
    for first_row in range(0, length, block_rows):
        last_row = first_row + block_rows
        query_block = queries[first_row:last_row]
        grad_block = grad_heads[first_row:last_row]
        scores = block_scores(queries, keys, row_ids, first_row, block_rows)
        weights_full = jnp.exp(scores - log_totals[:, first_row:last_row, None])
        grad_weights = jnp.einsum(
            "qhd,kd->hqk", grad_block, values[:last_row], preferred_element_type=jnp.float32
        )
        centre = jnp.sum(weights_full * grad_weights, axis=-1, keepdims=True)
        grad_scores = (weights_full * (grad_weights - centre)).astype(jnp.bfloat16)
        grad_parts.append(
            (
                jnp.einsum(
                    "hqk,kd->qhd", grad_scores, keys[:last_row], preferred_element_type=jnp.float32
                )
                * scale_factor
            ).astype(jnp.bfloat16)
        )
        grad_keys = grad_keys.at[:last_row].add(
            jnp.einsum("hqk,qhd->kd", grad_scores, query_block, preferred_element_type=jnp.float32)
            * scale_factor
        )
        grad_values = grad_values.at[:last_row].add(
            jnp.einsum(
                "hqk,qhd->kd",
                weights_full.astype(jnp.bfloat16),
                grad_block,
                preferred_element_type=jnp.float32,
            )
        )
    return (
        jnp.concatenate(grad_parts, axis=0),
        grad_keys.astype(jnp.bfloat16),
        grad_values.astype(jnp.bfloat16),
    )


def per_device(
    inputs,
    seq_ids,
    routes,
    norm1_gain,
    w_query,
    key_weight,
    value_weight,
    q_gain,
    k_gain,
    w_out,
    norm2_gain,
    w_router,
    w_gate,
    w_up,
    w_down,
    cotangent,
):
    token_count = inputs.shape[1]
    model_width = inputs.shape[2]
    sequence_count = lax.axis_size("seq")
    shard_count = lax.axis_size("shard")
    devices = sequence_count * shard_count
    heads_here = HQ // sequence_count
    replica_count = sequence_count // KEY_VALUE_HEADS
    length = token_count * sequence_count
    block_rows = min(512, length)
    capacity = max(2, token_count * TOPK * 5 // (4 * devices))
    x_first = inputs[0].astype(jnp.float32)
    grad_final = cotangent[0].astype(jnp.float32)
    (
        gain_one,
        query_full,
        key_full,
        value_full,
        qgain_full,
        kgain_full,
        out_full,
        gain_two,
        router_full,
    ) = (
        lax.all_gather(norm1_gain, "shard", axis=0, tiled=True),
        lax.all_gather(w_query, "shard", axis=0, tiled=True),
        lax.all_gather(key_weight, "shard", axis=0, tiled=True),
        lax.all_gather(value_weight, "shard", axis=0, tiled=True),
        lax.all_gather(q_gain, "shard", axis=0, tiled=True),
        lax.all_gather(k_gain, "shard", axis=0, tiled=True),
        lax.all_gather(w_out, "shard", axis=0, tiled=True),
        lax.all_gather(norm2_gain, "shard", axis=0, tiled=True),
        lax.all_gather(w_router, "shard", axis=0, tiled=True),
    )
    normed_one = x_first * root_mean_scale(x_first)
    first_hidden = (normed_one * gain_one).astype(jnp.bfloat16)
    q_raw = jnp.dot(first_hidden, query_full, preferred_element_type=jnp.float32).reshape(
        token_count, HQ, HEAD_DIMENSION
    )
    key_projected = jnp.dot(first_hidden, key_full, preferred_element_type=jnp.float32).reshape(
        token_count, KEY_VALUE_HEADS, HEAD_DIMENSION
    )
    value_projected = jnp.dot(first_hidden, value_full, preferred_element_type=jnp.float32).reshape(
        token_count, KEY_VALUE_HEADS, HEAD_DIMENSION
    )
    positions = lax.axis_index("seq") * token_count + jnp.arange(token_count, dtype=jnp.int32)
    cosine_table, sine_values = rope_tables(positions, HEAD_DIMENSION)
    q_rot = apply_rotary(
        q_raw * root_mean_scale(q_raw) * qgain_full, cosine_table, sine_values
    ).astype(jnp.bfloat16)
    k_rot = apply_rotary(
        key_projected * root_mean_scale(key_projected) * kgain_full, cosine_table, sine_values
    ).astype(jnp.bfloat16)
    v_low = value_projected.astype(jnp.bfloat16)
    q_send = q_rot.reshape(token_count, sequence_count, heads_here * HEAD_DIMENSION)
    k_send = jnp.repeat(k_rot, replica_count, axis=1)
    v_send = jnp.repeat(v_low, replica_count, axis=1)
    q_heads, k_heads, v_heads = (
        lax.all_to_all(q_send, "seq", split_axis=1, concat_axis=0, tiled=True),
        lax.all_to_all(k_send, "seq", split_axis=1, concat_axis=0, tiled=True),
        lax.all_to_all(v_send, "seq", split_axis=1, concat_axis=0, tiled=True),
    )
    q_heads = q_heads.reshape(length, heads_here, HEAD_DIMENSION)
    k_heads = k_heads.reshape(length, HEAD_DIMENSION)
    v_heads = v_heads.reshape(length, HEAD_DIMENSION)
    row_ids = lax.all_gather(seq_ids, "seq", axis=1, tiled=True)[0]
    attended, log_totals = attend_forward(q_heads, k_heads, v_heads, row_ids, block_rows)
    attn_tok = lax.all_to_all(
        attended.reshape(length, 1, heads_here * HEAD_DIMENSION),
        "seq",
        split_axis=0,
        concat_axis=1,
        tiled=True,
    ).reshape(token_count, HQ * HEAD_DIMENSION)
    x_second = x_first + jnp.dot(attn_tok, out_full, preferred_element_type=jnp.float32)
    normed_two = x_second * root_mean_scale(x_second)
    hidden_two = (normed_two * gain_two).astype(jnp.bfloat16)
    logits = jnp.dot(hidden_two, router_full, preferred_element_type=jnp.float32)
    experts = logits.shape[1]
    tok_routes = routes[0]
    route_pick = tok_routes[:, :, None] == jnp.arange(experts, dtype=jnp.int32)[None, None, :]
    chosen = jnp.sum(jnp.where(route_pick, logits[:, None, :], 0.0), axis=-1)
    gate_probs = jax.nn.softmax(chosen, axis=-1)
    route_hits = route_pick.reshape(-1, experts).astype(jnp.int32)
    slot_rank = jnp.sum(route_hits * (jnp.cumsum(route_hits, axis=0) - 1), axis=-1)
    slot_index = tok_routes.reshape(-1) * capacity + slot_rank
    owner_tok = jnp.arange(token_count * TOPK, dtype=jnp.int32) // TOPK
    owner_table = jnp.zeros((experts * capacity,), jnp.int32).at[slot_index].set(owner_tok)
    filled = jnp.zeros((experts * capacity,), jnp.bool_).at[slot_index].set(True)
    send_rows = jnp.where(
        filled[:, None], hidden_two[owner_table], jnp.zeros((), jnp.bfloat16)
    ).reshape(experts, capacity, model_width)
    rows_in = lax.all_to_all(
        send_rows, ("seq", "shard"), split_axis=0, concat_axis=0, tiled=True
    ).reshape(-1, model_width)
    gate_local = w_gate[0]
    up_local = w_up[0]
    down_local = w_down[0]
    gate_pre = jnp.dot(rows_in, gate_local, preferred_element_type=jnp.float32)
    up_pre = jnp.dot(rows_in, up_local, preferred_element_type=jnp.float32)
    gate_sigmoid = jax.nn.sigmoid(gate_pre)
    gate_silu = gate_pre * gate_sigmoid
    hidden = (gate_silu * up_pre).astype(jnp.bfloat16)
    expert_out = (
        jnp.dot(hidden, down_local, preferred_element_type=jnp.float32)
        .astype(jnp.bfloat16)
        .reshape(devices, capacity, model_width)
    )
    returned = lax.all_to_all(
        expert_out, ("seq", "shard"), split_axis=0, concat_axis=0, tiled=True
    ).reshape(-1, model_width)
    picked = returned[slot_index].reshape(token_count, TOPK, model_width).astype(jnp.float32)
    mixture = jnp.sum(gate_probs[:, :, None] * picked, axis=1)
    result = (x_second + mixture).astype(jnp.bfloat16)
    (
        gain_one,
        query_full,
        key_full,
        value_full,
        qgain_full,
        kgain_full,
        out_full,
        gain_two,
        router_full,
    ) = (
        lax.all_gather(norm1_gain, "shard", axis=0, tiled=True),
        lax.all_gather(w_query, "shard", axis=0, tiled=True),
        lax.all_gather(key_weight, "shard", axis=0, tiled=True),
        lax.all_gather(value_weight, "shard", axis=0, tiled=True),
        lax.all_gather(q_gain, "shard", axis=0, tiled=True),
        lax.all_gather(k_gain, "shard", axis=0, tiled=True),
        lax.all_gather(w_out, "shard", axis=0, tiled=True),
        lax.all_gather(norm2_gain, "shard", axis=0, tiled=True),
        lax.all_gather(w_router, "shard", axis=0, tiled=True),
    )
    grad_gates = jnp.sum(grad_final[:, None, :] * picked, axis=-1)
    grad_picked = (
        (gate_probs[:, :, None] * grad_final[:, None, :])
        .astype(jnp.bfloat16)
        .reshape(-1, model_width)
    )
    back_rows = (
        jnp.zeros((experts * capacity, model_width), jnp.bfloat16)
        .at[slot_index]
        .set(grad_picked)
        .reshape(experts, capacity, model_width)
    )
    grad_rows = lax.all_to_all(
        back_rows, ("seq", "shard"), split_axis=0, concat_axis=0, tiled=True
    ).reshape(-1, model_width)
    grad_hidden = jnp.dot(grad_rows, down_local.T, preferred_element_type=jnp.float32)
    grad_down = jnp.einsum("rf,rd->fd", hidden, grad_rows, preferred_element_type=jnp.float32)
    grad_gate_pre = (
        grad_hidden * up_pre * gate_sigmoid * (1.0 + gate_pre * (1.0 - gate_sigmoid))
    ).astype(jnp.bfloat16)
    grad_up_pre = (grad_hidden * gate_silu).astype(jnp.bfloat16)
    grad_gate = jnp.einsum("rd,rf->df", rows_in, grad_gate_pre, preferred_element_type=jnp.float32)
    grad_up = jnp.einsum("rd,rf->df", rows_in, grad_up_pre, preferred_element_type=jnp.float32)
    grad_in = (
        (
            jnp.dot(grad_gate_pre, gate_local.T, preferred_element_type=jnp.float32)
            + jnp.dot(grad_up_pre, up_local.T, preferred_element_type=jnp.float32)
        )
        .astype(jnp.bfloat16)
        .reshape(devices, capacity, model_width)
    )
    grad_back = lax.all_to_all(
        grad_in, ("seq", "shard"), split_axis=0, concat_axis=0, tiled=True
    ).reshape(-1, model_width)
    grad_two = jnp.sum(
        grad_back[slot_index].reshape(token_count, TOPK, model_width).astype(jnp.float32), axis=1
    )
    grad_chosen = gate_probs * (
        grad_gates - jnp.sum(gate_probs * grad_gates, axis=-1, keepdims=True)
    )
    grad_logits = jnp.sum(jnp.where(route_pick, grad_chosen[:, :, None], 0.0), axis=1)
    router_float = router_full.astype(jnp.float32)
    grad_two = grad_two + jnp.dot(grad_logits, router_float.T, precision=EXACT_PRECISION)
    grad_router = jnp.dot(hidden_two.astype(jnp.float32).T, grad_logits, precision=EXACT_PRECISION)
    grad_x_norm, norm_terms = rms_back(grad_two, x_second, gain_two)
    grad_gain_two = jnp.sum(norm_terms, axis=0)
    grad_second = grad_final + grad_x_norm
    grad_attn = grad_second.astype(jnp.bfloat16)
    grad_attended = (
        jnp.dot(grad_attn, out_full.T, preferred_element_type=jnp.float32)
        .astype(jnp.bfloat16)
        .reshape(token_count, sequence_count, heads_here * HEAD_DIMENSION)
    )
    grad_heads = lax.all_to_all(
        grad_attended, "seq", split_axis=1, concat_axis=0, tiled=True
    ).reshape(length, heads_here, HEAD_DIMENSION)
    grad_q_heads, grad_k_heads, grad_v_heads = attend_backward(
        q_heads, k_heads, v_heads, grad_heads, log_totals, row_ids, block_rows
    )
    grad_q_tok, gradient_key_token, gradient_value_token = (
        lax.all_to_all(
            grad_q_heads.reshape(length, 1, heads_here * HEAD_DIMENSION),
            "seq",
            split_axis=0,
            concat_axis=1,
            tiled=True,
        ),
        lax.all_to_all(
            grad_k_heads.reshape(length, 1, HEAD_DIMENSION),
            "seq",
            split_axis=0,
            concat_axis=1,
            tiled=True,
        ),
        lax.all_to_all(
            grad_v_heads.reshape(length, 1, HEAD_DIMENSION),
            "seq",
            split_axis=0,
            concat_axis=1,
            tiled=True,
        ),
    )
    grad_q_rot = grad_q_tok.reshape(token_count, HQ, HEAD_DIMENSION).astype(jnp.float32)
    grad_k_rot = jnp.sum(
        gradient_key_token.astype(jnp.float32).reshape(
            token_count, KEY_VALUE_HEADS, replica_count, HEAD_DIMENSION
        ),
        axis=2,
    )
    gradient_value_summed = jnp.sum(
        gradient_value_token.astype(jnp.float32).reshape(
            token_count, KEY_VALUE_HEADS, replica_count, HEAD_DIMENSION
        ),
        axis=2,
    )
    grad_q_norm, q_terms = rms_back(
        apply_rotary(grad_q_rot, cosine_table, -sine_values), q_raw, qgain_full
    )
    gradient_key_normed, k_terms = rms_back(
        apply_rotary(grad_k_rot, cosine_table, -sine_values), key_projected, kgain_full
    )
    grad_qgain = jnp.sum(q_terms, axis=(0, 1))
    grad_kgain = jnp.sum(k_terms, axis=(0, 1))
    grad_q_raw = grad_q_norm.reshape(token_count, HQ * HEAD_DIMENSION).astype(jnp.bfloat16)
    gradient_key_unrotated = gradient_key_normed.reshape(
        token_count, KEY_VALUE_HEADS * HEAD_DIMENSION
    ).astype(jnp.bfloat16)
    gradient_value_projected = gradient_value_summed.reshape(
        token_count, KEY_VALUE_HEADS * HEAD_DIMENSION
    ).astype(jnp.bfloat16)
    grad_one = (
        jnp.dot(grad_q_raw, query_full.T, preferred_element_type=jnp.float32)
        + jnp.dot(gradient_key_unrotated, key_full.T, preferred_element_type=jnp.float32)
        + jnp.dot(gradient_value_projected, value_full.T, preferred_element_type=jnp.float32)
    )
    grad_x_first, first_terms = rms_back(grad_one, x_first, gain_one)
    grad_gain_one = jnp.sum(first_terms, axis=0)
    grad_inputs = grad_second + grad_x_first
    grad_query = jnp.einsum(
        "td,tf->df", first_hidden, grad_q_raw, preferred_element_type=jnp.float32
    )
    grad_key = jnp.einsum(
        "td,tf->df", first_hidden, gradient_key_unrotated, preferred_element_type=jnp.float32
    )
    grad_value = jnp.einsum(
        "td,tf->df", first_hidden, gradient_value_projected, preferred_element_type=jnp.float32
    )
    grad_out_w = jnp.einsum("tf,td->fd", attn_tok, grad_attn, preferred_element_type=jnp.float32)
    (
        part_one,
        part_query,
        part_key,
        part_value,
        part_qgain,
        part_kgain,
        part_out,
        part_two,
        part_router,
    ) = (
        lax.psum_scatter(
            grad_gain_one.astype(jnp.bfloat16), "shard", scatter_dimension=0, tiled=True
        ).astype(jnp.float32),
        lax.psum_scatter(
            grad_query.astype(jnp.bfloat16), "shard", scatter_dimension=0, tiled=True
        ).astype(jnp.float32),
        lax.psum_scatter(
            grad_key.astype(jnp.bfloat16), "shard", scatter_dimension=0, tiled=True
        ).astype(jnp.float32),
        lax.psum_scatter(
            grad_value.astype(jnp.bfloat16), "shard", scatter_dimension=0, tiled=True
        ).astype(jnp.float32),
        lax.psum_scatter(
            grad_qgain.astype(jnp.bfloat16), "shard", scatter_dimension=0, tiled=True
        ).astype(jnp.float32),
        lax.psum_scatter(
            grad_kgain.astype(jnp.bfloat16), "shard", scatter_dimension=0, tiled=True
        ).astype(jnp.float32),
        lax.psum_scatter(
            grad_out_w.astype(jnp.bfloat16), "shard", scatter_dimension=0, tiled=True
        ).astype(jnp.float32),
        lax.psum_scatter(
            grad_gain_two.astype(jnp.bfloat16), "shard", scatter_dimension=0, tiled=True
        ).astype(jnp.float32),
        lax.psum_scatter(
            grad_router.astype(jnp.bfloat16), "shard", scatter_dimension=0, tiled=True
        ).astype(jnp.float32),
    )
    sum_one, sum_query, sum_key, sum_value, sum_qgain, sum_kgain, sum_out, sum_two, sum_router = (
        lax.psum(part_one.astype(jnp.bfloat16), "seq").astype(jnp.float32),
        lax.psum(part_query.astype(jnp.bfloat16), "seq").astype(jnp.float32),
        lax.psum(part_key.astype(jnp.bfloat16), "seq").astype(jnp.float32),
        lax.psum(part_value.astype(jnp.bfloat16), "seq").astype(jnp.float32),
        lax.psum(part_qgain.astype(jnp.bfloat16), "seq").astype(jnp.float32),
        lax.psum(part_kgain.astype(jnp.bfloat16), "seq").astype(jnp.float32),
        lax.psum(part_out.astype(jnp.bfloat16), "seq").astype(jnp.float32),
        lax.psum(part_two.astype(jnp.bfloat16), "seq").astype(jnp.float32),
        lax.psum(part_router.astype(jnp.bfloat16), "seq").astype(jnp.float32),
    )
    return (
        result[None],
        grad_inputs[None],
        sum_one,
        sum_query,
        sum_key,
        sum_value,
        sum_qgain,
        sum_kgain,
        sum_out,
        sum_two,
        sum_router,
        grad_gate[None],
        grad_up[None],
        grad_down[None],
    )


def solution(mesh):
    in_specs = (
        P("shard", "seq", None),
        P("shard", "seq"),
        P("shard", "seq", None),
        P("shard"),
        P("shard", None),
        P("shard", None),
        P("shard", None),
        P("shard"),
        P("shard"),
        P("shard", None),
        P("shard"),
        P("shard", None),
        P(("seq", "shard"), None, None),
        P(("seq", "shard"), None, None),
        P(("seq", "shard"), None, None),
        P("shard", "seq", None),
    )
    out_specs = (
        P("shard", "seq", None),
        P("shard", "seq", None),
        P("shard"),
        P("shard", None),
        P("shard", None),
        P("shard", None),
        P("shard"),
        P("shard"),
        P("shard", None),
        P("shard"),
        P("shard", None),
        P(("seq", "shard"), None, None),
        P(("seq", "shard"), None, None),
        P(("seq", "shard"), None, None),
    )
    return jax.shard_map(
        per_device, mesh=mesh, in_specs=in_specs, out_specs=out_specs, check_vma=False
    )
```

profile of v0, /device:TPU:5, one launch (start us, length us, event | category | flops | bytes accessed | tf_op | source)
XLA Modules:
  0.0 2104.2 jit_solution(9218490821074823771)
XLA Ops:
  10.1 14.0 all-gather
  25.9 17.5 all-reduce.7
  46.2 12.4 all-gather.9.cloned.1.call-done
  71.6 216.5 %all-gather.11.cloned.1.call-done = bf16[2048,4096]{1,0:T(8,128)(2,1)} async-done(((bf16[256,4096]{1,0:T(8,128)(2,1)}), bf16[2048,4096]{1,0:T(8,128)(2,1)}) %all-gather.11.cloned.1.call-update) | async-done | bytes 16777232 | tf_op jit(solution)/shard_map/all_gather | solution.py:177
  288.1 22.6 %copy.186 = bf16[4096,2048]{1,0:T(8,128)(2,1)} copy(bf16[4096,2048]{0,1:T(8,128)(2,1)} %bitcast.260) | data formatting | bytes 33554432 | tf_op jit(solution)/shard_map/dot_general | solution.py:188
  329.2 13.5 all-gather.1
  344.1 9.0 reduce-window.6
  429.0 136.8 %all-gather.13.cloned.1.call-done = bf16[4096,2048]{1,0:T(8,128)(2,1)} async-done(((bf16[512,2048]{1,0:T(8,128)(2,1)}), bf16[4096,2048]{1,0:T(8,128)(2,1)}) %all-gather.13.cloned.1.call-update) | async-done | bytes 16777232 | tf_op jit(solution)/shard_map/all_gather | solution.py:182
  576.4 11.9 gather_fusion
  599.1 128.6 %all_gather.48 = bf16[2048,32]{0,1:T(8,128)(2,1)S(1)} all-gather(bf16[256,32]{0,1:T(8,128)(2,1)S(1)} %copy-done.42), channel_id=1, replica_groups=mesh['seq'=4,'shard'=8] {'shard'}, dimensions={0}, use_global_device_ids=true | all-gather | bytes 147456 | tf_op jit(solution)/shard_map/all_gather | solution.py:184
  731.5 10.7 scatter_custom_fusion.2
  742.2 12.3 all-to-all-start.6
  754.5 9.8 fusion.25
  773.0 98.2 %all-to-all-done.6 = bf16[32,40,2048]{2,1,0:T(8,128)(2,1)} async-done(((bf16[32,40,2048]{2,1,0:T(8,128)(2,1)}), bf16[32,40,2048]{2,1,0:T(8,128)(2,1)}, u32[]{:S(2)}, u32[]{:S(2)}) %all-to-all-start.6) | async-done | bytes 5242912 | tf_op jit(solution)/shard_map/all_to_all | solution.py:299
  871.2 11.7 multiply_convert_fusion
  910.3 109.2 %all-to-all-done.7 = bf16[32,40,2048]{2,1,0:T(8,128)(2,1)} async-done(((bf16[32,40,2048]{2,1,0:T(8,128)(2,1)}), bf16[32,40,2048]{2,1,0:T(8,128)(2,1)}, u32[]{:S(2)}, u32[]{:S(2)}) %all-to-all-start.7) | async-done | bytes 5242912 | tf_op jit(solution)/shard_map/all_to_all | solution.py:318
  1026.0 12.0 gather_fusion.2
  1043.0 99.4 %all-to-all-done.5 = bf16[32,40,2048]{2,1,0:T(8,128)(2,1)} async-done(((bf16[32,40,2048]{2,1,0:T(8,128)(2,1)}), bf16[32,40,2048]{2,1,0:T(8,128)(2,1)}, u32[]{:S(2)}, u32[]{:S(2)}) %all-to-all-start.5) | async-done | bytes 5242912 | tf_op jit(solution)/shard_map/all_to_all | solution.py:260
  1142.5 12.1 gather_fusion.1
  1164.9 11.7 convolution_convert_fusion.3
  1181.3 13.5 all-to-all-done.8
  1249.2 17.6 all_to_all.130
  1278.9 9.4 convolution_convert_fusion.1
  1308.6 10.2 convolution_bitcast_fusion
  1318.8 36.4 %reduce-scatter.10.cloned.1.call-done = bf16[256,512]{1,0:T(8,128)(2,1)} async-done(((bf16[2048,512]{1,0:T(8,128)(2,1)}), bf16[256,512]{1,0:T(8,128)(2,1)}) %reduce-scatter.10.cloned.1.call-update) | async-done | bytes 262160 | tf_op jit(solution)/shard_map/reduce_scatter | solution.py:435
  1355.2 287.1 %reduce-scatter.12.cloned.1.call-done = bf16[512,2048]{1,0:T(8,128)(2,1)} async-done(((bf16[4096,2048]{1,0:T(8,128)(2,1)}), bf16[512,2048]{1,0:T(8,128)(2,1)}) %reduce-scatter.12.cloned.1.call-update) | async-done | bytes 2097168 | tf_op jit(solution)/shard_map/reduce_scatter | solution.py:444
  1642.3 286.1 %reduce-scatter.6.cloned.1.call-done = bf16[256,4096]{1,0:T(8,128)(2,1)} async-done(((bf16[2048,4096]{1,0:T(8,128)(2,1)}), bf16[256,4096]{1,0:T(8,128)(2,1)}) %reduce-scatter.6.cloned.1.call-update) | async-done | bytes 2097168 | tf_op jit(solution)/shard_map/reduce_scatter | solution.py:429
  1928.5 11.5 fusion.94
  1943.6 14.5 all-reduce.6
  1958.4 32.2 %reduce-scatter.14.cloned.1.call-done = bf16[256,32]{0,1:T(8,128)(2,1)} async-done(((bf16[2048,32]{0,1:T(8,128)(2,1)}), bf16[256,32]{0,1:T(8,128)(2,1)}) %reduce-scatter.14.cloned.1.call-update) | async-done | bytes 16400 | tf_op jit(solution)/shard_map/reduce_scatter | solution.py:450
  1990.6 13.5 all-reduce.8
  2008.3 80.4 %all-reduce.12.cloned.1.call-done = (bf16[256,4096]{1,0:T(8,128)(2,1)}, bf16[256,512]{1,0:T(8,128)(2,1)}, bf16[256,512]{1,0:T(8,128)(2,1)}, bf16[512,2048]{1,0:T(8,128)(2,1)}) async-done(((bf16[256,4096]{1,0:T(8,128)(2,1)}, bf16[256,512]{1,0:T(8,128)(2,1)}, bf16[256,512]{1,0:T(8,128)(2,1)}, bf16[512,2048]{1,0:T(8,128)(2,1)}), (bf16[256,4096]{1,0:T(8,128)(2,1)}, bf16[256,512]{1,0:T(8,128)(2,1)}, ...) | async-done | bytes 4718608 | tf_op jit(solution)/shard_map/psum | solution.py:456
  (310 shorter events, 304.2 us)
Async XLA Ops:
  7.2 864.0 %copy-start = (bf16[1,768,2048]{2,1,0:T(8,128)(2,1)S(1)}, bf16[1,768,2048]{2,1,0:T(8,128)(2,1)}, u32[]{:S(2)}) copy-start(bf16[1,768,2048]{2,1,0:T(8,128)(2,1)} %param.38) | copy-start | bytes 9437188
  7.2 18.4 copy-start.56
  7.2 36.7 %copy-start.35 = (s32[1,128,8]{1,2,0:T(8,128)S(1)}, s32[1,128,8]{1,2,0:T(8,128)}, u32[]{:S(2)}) copy-start(s32[1,128,8]{1,2,0:T(8,128)} %param.26) | copy-start | bytes 12292
  7.3 51.4 %all-gather.9.cloned.1.call-start = ((), (), s32[]{:S(2)}) async-start(), calls=%async_computation.18 | async-start | bytes 2359296 | tf_op jit(solution)/shard_map/all_gather | solution.py:178
  8.0 280.1 %all-gather.11.cloned.1.call-start = ((), (), s32[]{:S(2)}) async-start(), calls=%async_computation.19 | async-start | bytes 18874368 | tf_op jit(solution)/shard_map/all_gather | solution.py:177
  8.7 355.9 %all-gather.7.cloned.1.call-start = ((), (), s32[]{:S(2)}) async-start(), calls=%async_computation.17 | async-start | bytes 2359296 | tf_op jit(solution)/shard_map/all_gather | solution.py:179
  9.5 556.4 %all-gather.13.cloned.1.call-start = ((), (), s32[]{:S(2)}) async-start(), calls=%async_computation.20 | async-start | bytes 18874368 | tf_op jit(solution)/shard_map/all_gather | solution.py:182
  24.1 344.5 %copy-start.25 = (f32[8,1,256]{2,1,0:T(1,128)}, f32[8,1,256]{2,1,0:T(1,128)S(1)}, u32[]{:S(2)}) copy-start(f32[8,1,256]{2,1,0:T(1,128)S(1)} %convert_element_type.355) | copy-start | bytes 24580
  43.4 22.5 %copy-start.45 = (f32[128]{0:T(128)}, f32[128]{0:T(128)S(1)}, u32[]{:S(2)}) copy-start(f32[128]{0:T(128)S(1)} %convert_element_type.281) | copy-start | bytes 1540
  45.4 323.2 %copy-start.39 = (f32[128]{0:T(128)}, f32[128]{0:T(128)S(1)}, u32[]{:S(2)}) copy-start(f32[128]{0:T(128)S(1)} %add_rsqrt_fusion.3) | copy-start | bytes 1540
  46.2 273.3 %copy-start.23 = (f32[128,64]{0,1:T(8,128)}, f32[128,64]{0,1:T(8,128)S(1)}, u32[]{:S(2)}) copy-start(f32[128,64]{0,1:T(8,128)S(1)} %get-tuple-element.94) | copy-start | bytes 98308
  66.7 256.5 %all-to-all-start.1 = ((bf16[128,4,128]{0,2,1:T(8,128)(2,1)}), bf16[128,4,128]{0,2,1:T(8,128)(2,1)S(1)}, u32[]{:S(2)}, u32[]{:S(2)}) async-start(bf16[128,4,128]{0,2,1:T(8,128)(2,1)} %pad_maximum_fusion.3), calls=%async_computation.1 | async-start | bytes 262144 | tf_op jit(solution)/shard_map/all_to_all | solution.py:211
  319.8 34.2 %copy-start.50 = (s32[1,128]{1,0:T(1,128)S(1)}, s32[1,128]{1,0:T(1,128)}, u32[]{:S(2)}) copy-start(s32[1,128]{1,0:T(1,128)} %param.25) | copy-start | bytes 1540
  323.1 20.3 copy-start.27
  323.1 49.8 %all-to-all-start.2 = ((bf16[128,4,1024]{2,0,1:T(8,128)(2,1)}), bf16[128,4,1024]{2,0,1:T(8,128)(2,1)}, u32[]{:S(2)}, u32[]{:S(2)}) async-start(bf16[128,4,1024]{2,0,1:T(8,128)(2,1)} %copy.187), calls=%async_computation.2 | async-start | bytes 2097152 | tf_op jit(solution)/shard_map/all_to_all | solution.py:210
  372.9 12.5 all-to-all-start
  401.4 18.2 all-to-all-start.3
  593.6 137.6 %copy-start.36 = (s32[1,128,8]{1,2,0:T(8,128)S(1)}, s32[1,128,8]{1,2,0:T(8,128)}, u32[]{:S(2)}) copy-start(s32[1,128,8]{1,2,0:T(8,128)} %param.26) | copy-start | bytes 12292
  593.6 148.6 %all-to-all-start.4 = ((bf16[32,40,2048]{2,1,0:T(8,128)(2,1)}), bf16[32,40,2048]{2,1,0:T(8,128)(2,1)}, u32[]{:S(2)}, u32[]{:S(2)}) async-start(bf16[32,40,2048]{2,1,0:T(8,128)(2,1)} %broadcast_select_fusion), calls=%async_computation.4 | async-start | bytes 10485760 | tf_op jit(solution)/shard_map/all_to_all | solution.py:244
  742.2 129.0 %all-to-all-start.6 = ((bf16[32,40,2048]{2,1,0:T(8,128)(2,1)}), bf16[32,40,2048]{2,1,0:T(8,128)(2,1)}, u32[]{:S(2)}, u32[]{:S(2)}) async-start(bf16[32,40,2048]{2,1,0:T(8,128)(2,1)} %bitcast.262), calls=%async_computation.6 | async-start | bytes 10485760 | tf_op jit(solution)/shard_map/all_to_all | solution.py:299
  896.7 122.8 %all-to-all-start.7 = ((bf16[32,40,2048]{2,1,0:T(8,128)(2,1)}), bf16[32,40,2048]{2,1,0:T(8,128)(2,1)}, u32[]{:S(2)}, u32[]{:S(2)}) async-start(bf16[32,40,2048]{2,1,0:T(8,128)(2,1)} %bitcast.273), calls=%async_computation.7 | async-start | bytes 10485760 | tf_op jit(solution)/shard_map/all_to_all | solution.py:318
  1019.5 123.0 %all-to-all-start.5 = ((bf16[32,40,2048]{2,1,0:T(8,128)(2,1)}), bf16[32,40,2048]{2,1,0:T(8,128)(2,1)}, u32[]{:S(2)}, u32[]{:S(2)}) async-start(bf16[32,40,2048]{2,1,0:T(8,128)(2,1)} %bitcast.272), calls=%async_computation.5 | async-start | bytes 10485760 | tf_op jit(solution)/shard_map/all_to_all | solution.py:260
  1164.9 69.4 %copy-start.10 = (f32[128,2048]{1,0:T(8,128)}, f32[128,2048]{1,0:T(8,128)S(1)}, u32[]{:S(2)}) copy-start(f32[128,2048]{1,0:T(8,128)S(1)} %get-tuple-element.86) | copy-start | bytes 3145732
  1177.7 17.0 all-to-all-start.8
  1181.2 137.6 %reduce-scatter.8.cloned.1.call-start = ((), (), s32[]{:S(2)}) async-start(), calls=%async_computation.22 | async-start | bytes 2359296 | tf_op jit(solution)/shard_map/reduce_scatter | solution.py:432
  1218.8 136.4 %reduce-scatter.10.cloned.1.call-start = ((), (), s32[]{:S(2)}) async-start(), calls=%async_computation.23 | async-start | bytes 2359296 | tf_op jit(solution)/shard_map/reduce_scatter | solution.py:435
  1234.2 408.1 %reduce-scatter.12.cloned.1.call-start = ((), (), s32[]{:S(2)}) async-start(), calls=%async_computation.24 | async-start | bytes 18874368 | tf_op jit(solution)/shard_map/reduce_scatter | solution.py:444
  1242.5 685.9 %reduce-scatter.6.cloned.1.call-start = ((), (), s32[]{:S(2)}) async-start(), calls=%async_computation.21 | async-start | bytes 18874368 | tf_op jit(solution)/shard_map/reduce_scatter | solution.py:429
  1288.4 702.2 %reduce-scatter.14.cloned.1.call-start = ((), (), s32[]{:S(2)}) async-start(), calls=%async_computation.25 | async-start | bytes 147456 | tf_op jit(solution)/shard_map/reduce_scatter | solution.py:450
  1308.4 780.3 %all-reduce.12.cloned.1.call-start = ((), (), s32[]{:S(2)}) async-start(), calls=%async_computation.26 | async-start | bytes 9437184 | tf_op jit(solution)/shard_map/psum | solution.py:456
  1318.8 609.7 %copy-start.13 = (bf16[128,32,128]{0,2,1:T(8,128)(2,1)S(1)}, bf16[128,32,128]{0,2,1:T(8,128)(2,1)}, u32[]{:S(2)}) copy-start(bf16[128,32,128]{0,2,1:T(8,128)(2,1)} %multiply_convert_fusion.3) | copy-start | bytes 3145732
  1940.0 67.0 %copy-start.11 = (f32[128,2048]{1,0:T(8,128)S(1)}, f32[128,2048]{1,0:T(8,128)}, u32[]{:S(2)}) copy-start(f32[128,2048]{1,0:T(8,128)} %copy-done.10) | copy-start | bytes 3145732
  (49 other events, 356.7 us)
Sparse Core Ops, SparseCore 0:
  10.2 48.3 all-gather.8
  60.8 227.2 all-gather.10
  290.2 46.7 all-gather.6
  339.0 226.8 all-gather.12
  1218.9 66.0 reduce-scatter.7
  1288.5 66.6 reduce-scatter.9
  1359.0 283.3 reduce-scatter.11
  1646.6 281.7 reduce-scatter.5
  1932.3 58.2 reduce-scatter.13
  1993.0 95.5 all-reduce.11
where the time goes:
time: 2110 us; the launch traced here: 2100 us
  waiting for transfers between devices  1420 us (67%)
  blocking collectives  242 us (11%)
  matrix products  176 us (8%)
  local copies, waits for them, and re-layouts  120 us (6%)
  other arithmetic  78.3 us (4%)
  starting transfers between devices  53.7 us (3%)
    reduce_scatter x1, waiting for transfers between devices, per_device(): lax.psum_scatter(grad_out_w.astype(jnp.bfloat16), 'shard', scatter_dimens...  287 us
    reduce_scatter x1, waiting for transfers between devices, per_device(): lax.psum_scatter(grad_query.astype(jnp.bfloat16), 'shard', scatter_dimens...  286 us
    all_gather x1, waiting for transfers between devices, per_device(): lax.all_gather(w_query, 'shard', axis=0, tiled=True)  216 us
    all_gather x1, waiting for transfers between devices, per_device(): lax.all_gather(w_out, 'shard', axis=0, tiled=True)  137 us
    all_gather x1, blocking collectives, per_device(): lax.all_gather(w_router, 'shard', axis=0, tiled=True)  129 us
    all_to_all x1, waiting for transfers between devices, per_device(): lax.all_to_all(grad_in, ('seq', 'shard'), split_axis=0, concat_axis=0, ti...  109 us
    all_to_all x1, waiting for transfers between devices, per_device(): lax.all_to_all(expert_out, ('seq', 'shard'), split_axis=0, concat_axis=0,...  99.4 us
    all_to_all x1, waiting for transfers between devices, per_device(): lax.all_to_all(back_rows, ('seq', 'shard'), split_axis=0, concat_axis=0,...  98.2 us
  transfers between devices with their start and end apart: 19, of which 13 were waited for; matrix products, arithmetic and copies ran while one was open for 12% of the time, Pallas kernels for 0%

commit v1 on v0

v1 whole, which is shorter than its diff:
```python
import jax
import jax.numpy as jnp
import numpy as np
from jax import lax
from jax.sharding import PartitionSpec as P

HQ = 32
KEY_VALUE_HEADS = 4
HEAD_DIMENSION = 128
TOPK = 8

EPSILON = 1e-06
ROPE_BASE = 1000000.0
NEGATIVE = -1e30
EXACT_PRECISION = lax.Precision.HIGHEST
BF = jnp.bfloat16
F32 = jnp.float32


def ring_order(count):
    width = 4 if count >= 16 else 2
    if count % width or count // width < 2:
        return list(range(count))
    depth = count // width
    order = [z * width for z in range(depth)]
    for turn, z in enumerate(reversed(range(depth))):
        columns = range(1, width) if turn % 2 == 0 else range(width - 1, 0, -1)
        order += [z * width + y for y in columns]
    return order


class Ring:
    def __init__(self, count):
        self.n = count
        self.order = ring_order(count)
        place = [0] * count
        for i, d in enumerate(self.order):
            place[d] = i
        self.up = [(self.order[i], self.order[(i + 1) % count]) for i in range(count)]
        self.down = [(b, a) for a, b in self.up]
        me = jnp.asarray(place, jnp.int32)[lax.axis_index("shard")]
        table = jnp.asarray(self.order, jnp.int32)
        self.index = [table[(me + r) % count] for r in range(count)]

    def forward(self, value):
        return lax.ppermute(value, "shard", self.up)

    def backward(self, value):
        return lax.ppermute(value, "shard", self.down)

    def gather(self, value):
        n, half = self.n, self.n // 2
        blocks = [None] * n
        blocks[0] = value
        for j in range(1, half):
            blocks[n - j] = self.forward(blocks[(n - j + 1) % n])
            blocks[j] = self.backward(blocks[j - 1])
        cut = value.shape[0] // 2 // 16 * 16
        top = self.forward(blocks[(half + 1) % n][:cut])
        bottom = self.backward(blocks[half - 1][cut:])
        blocks[half] = jnp.concatenate([top, bottom], axis=0)
        return blocks

    def reduce(self, part):
        n, half = self.n, self.n // 2
        far = part(half)
        rows = far.shape[0]
        cut = rows // 2 // 16 * 16
        top = self.forward(far[:cut].astype(BF)).astype(F32)
        bottom = self.backward(far[cut:].astype(BF)).astype(F32)
        ahead = jnp.pad(top, ((0, rows - cut), (0, 0)))
        behind = jnp.pad(bottom, ((cut, 0), (0, 0)))
        for j in range(half - 1, 0, -1):
            ahead = self.forward((part(j) + ahead).astype(BF)).astype(F32)
            behind = self.backward((part(n - j) + behind).astype(BF)).astype(F32)
        return part(0) + ahead + behind

    def chunks(self):
        n, half = self.n, self.n // 2
        if half < 2:
            return [[0], [1]]
        near = [[j, n - j] for j in range(1, half - 1)]
        return [[0]] + near + [[half - 1, n - half + 1, half]]


def swap(value, bit, count):
    return lax.ppermute(value, "seq", [(i, i ^ bit) for i in range(count)])


def seq_gather(value, count):
    have = {0: value}
    bit = count // 2
    while bit:
        keys = sorted(have)
        got = swap(jnp.stack([have[k] for k in keys]), bit, count)
        for i, k in enumerate(keys):
            have[k ^ bit] = got[i]
        bit //= 2
    return [have[k] for k in range(count)]


def seq_reduce(parts, count):
    have = dict(enumerate(parts))
    bit = 1
    while bit < count:
        keys = [k for k in sorted(have) if k & bit]
        got = swap(jnp.stack([have[k].astype(BF) for k in keys]), bit, count)
        for i, k in enumerate(keys):
            have[k ^ bit] = have[k ^ bit] + got[i].astype(F32)
            del have[k]
        bit *= 2
    return have[0]


def tree_sum(values):
    values = list(values)
    while len(values) > 1:
        values = [values[i] + values[i + 1] for i in range(0, len(values), 2)]
    return values[0]


def after(value, *others):
    return lax.optimization_barrier((value,) + others)[0]


def matmul(a, b):
    return jnp.dot(a, b, preferred_element_type=F32)


def matmul_nt(a, b):
    return lax.dot_general(a, b, (((1,), (1,)), ((), ())), preferred_element_type=F32)


def matmul_tn(a, b):
    return lax.dot_general(a, b, (((0,), (0,)), ((), ())), preferred_element_type=F32)


def apply_rotary(values, cosine_table, sine_values):
    half_size = values.shape[-1] // 2
    first_half = values[..., :half_size]
    second_half = values[..., half_size:]
    cos_b = cosine_table[:, None, :]
    sin_b = sine_values[:, None, :]
    return jnp.concatenate(
        [first_half * cos_b - second_half * sin_b, second_half * cos_b + first_half * sin_b],
        axis=-1,
    )


def root_mean_scale(values):
    return lax.rsqrt(jnp.mean(values * values, axis=-1, keepdims=True) + EPSILON)


def rms_back(grad_out, values, gain):
    factor = root_mean_scale(values)
    normed = values * factor
    grad_norm = grad_out * gain
    grad_values = factor * (
        grad_norm - normed * jnp.mean(grad_norm * normed, axis=-1, keepdims=True)
    )
    return (grad_values, grad_out * normed)


def attend_scores(queries, keys, allowed):
    scores = jnp.einsum("qhd,kd->hqk", queries, keys, preferred_element_type=F32)
    scores = scores * queries.shape[-1] ** (-0.5)
    return jnp.where(allowed[None], scores, NEGATIVE)


def attend_forward(queries, keys, values, allowed):
    scores = attend_scores(queries, keys, allowed)
    highest = jnp.max(scores, axis=-1, keepdims=True)
    exp_terms = jnp.exp(scores - highest)
    row_total = jnp.sum(exp_terms, axis=-1, keepdims=True)
    weights_bf = (exp_terms / row_total).astype(BF)
    out = jnp.einsum("hqk,kd->qhd", weights_bf, values, preferred_element_type=F32)
    return out.astype(BF), highest + jnp.log(row_total)


def attend_backward(queries, keys, values, grad_heads, log_totals, allowed):
    scale = queries.shape[-1] ** (-0.5)
    weights = jnp.exp(attend_scores(queries, keys, allowed) - log_totals)
    grad_weights = jnp.einsum("qhd,kd->hqk", grad_heads, values, preferred_element_type=F32)
    centre = jnp.sum(weights * grad_weights, axis=-1, keepdims=True)
    grad_scores = (weights * (grad_weights - centre)).astype(BF)
    grad_q = jnp.einsum("hqk,kd->qhd", grad_scores, keys, preferred_element_type=F32) * scale
    grad_k = jnp.einsum("hqk,qhd->kd", grad_scores, queries, preferred_element_type=F32) * scale
    grad_v = jnp.einsum(
        "hqk,qhd->kd", weights.astype(BF), grad_heads, preferred_element_type=F32
    )
    return grad_q.astype(BF), grad_k.astype(BF), grad_v.astype(BF)


def per_device(
    inputs,
    seq_ids,
    routes,
    norm1_gain,
    w_query,
    key_weight,
    value_weight,
    q_gain,
    k_gain,
    w_out,
    norm2_gain,
    w_router,
    w_gate,
    w_up,
    w_down,
    cotangent,
):
    tokens = inputs.shape[1]
    width = inputs.shape[2]
    S = lax.axis_size("seq")
    N = lax.axis_size("shard")
    s = lax.axis_index("seq")
    d = lax.axis_index("shard")
    ring = Ring(N)
    heads = HQ // S
    replicas = S // KEY_VALUE_HEADS
    HD = HEAD_DIMENSION
    length = tokens * S
    experts = S * N
    cap = max(2, tokens * TOPK * 5 // (4 * experts))
    slab = width // N
    q_cols = heads * HD
    cols = q_cols + 2 * HD
    kv_at = (s // replicas) * HD

    pieces = [
        norm1_gain,
        norm2_gain,
        q_gain,
        k_gain,
        w_router.reshape(-1),
        routes.astype(BF).reshape(-1),
    ]
    sizes = [p.shape[0] for p in pieces]
    starts = np.cumsum([0] + sizes)
    extra = -(-int(starts[-1]) // (8 * cols)) * 8
    packed = jnp.concatenate(pieces + [jnp.zeros((extra * cols - int(starts[-1]),), BF)])
    block = jnp.concatenate(
        [
            lax.dynamic_slice(w_query, (0, s * q_cols), (slab, q_cols)),
            lax.dynamic_slice(key_weight, (0, kv_at), (slab, HD)),
            lax.dynamic_slice(value_weight, (0, kv_at), (slab, HD)),
        ],
        axis=1,
    )
    block = jnp.concatenate([block, packed.reshape(extra, cols)], axis=0)
    x_row = jnp.stack(seq_gather(inputs[0], S))
    ids = jnp.stack(seq_gather(seq_ids[0], S)).reshape(length)

    blocks = ring.gather(block)
    w_qkv = jnp.zeros((width, cols), BF)
    small = jnp.zeros((N, extra * cols), BF)
    route_blocks = []
    for r in range(N):
        w_qkv = lax.dynamic_update_slice(w_qkv, blocks[r][:slab], (ring.index[r] * slab, 0))
        flat = blocks[r][slab:].reshape(1, -1)
        small = lax.dynamic_update_slice(small, flat, (ring.index[r], 0))
        route_blocks.append(flat[0, int(starts[5]) : int(starts[6])].reshape(tokens, TOPK))

    def unpack(i):
        return small[:, int(starts[i]) : int(starts[i + 1])]

    gain_one, gain_two = unpack(0).reshape(-1), unpack(1).reshape(-1)
    qgain, kgain = unpack(2).reshape(-1), unpack(3).reshape(-1)
    router = unpack(4).reshape(width, experts)

    rows_out = w_out.shape[0] // S
    piece = lax.dynamic_slice(w_out, (s * rows_out, 0), (rows_out, width))
    spread = [((g % S) * N + g // S, g) for g in range(S * N)]
    piece = lax.ppermute(piece, ("seq", "shard"), spread)
    piece = after(piece, blocks[N // 2])
    out_blocks = ring.gather(piece)
    w_o = jnp.zeros((q_cols, width), BF)
    for r in range(N):
        w_o = lax.dynamic_update_slice(w_o, out_blocks[r], (ring.index[r] * rows_out, 0))

    grad_low = cotangent[0]
    dy_blocks = ring.gather(after(grad_low, out_blocks[N // 2]))

    x_all = x_row.reshape(length, width).astype(F32)
    factor_one = root_mean_scale(x_all)
    h1 = (x_all * factor_one * gain_one).astype(BF)
    qkv = matmul(h1, w_qkv)
    q_raw = qkv[:, :q_cols].reshape(length, heads, HD)
    k_raw = qkv[:, q_cols : q_cols + HD].reshape(length, 1, HD)
    v_low = qkv[:, q_cols + HD :].astype(BF)
    sources = jnp.arange(S, dtype=jnp.int32) ^ s
    positions = (sources[:, None] * tokens + jnp.arange(tokens, dtype=jnp.int32)).reshape(-1)
    inverse = ROPE_BASE ** (-2.0 * jnp.arange(HD // 2, dtype=F32) / HD)
    angles = positions.astype(F32)[:, None] * inverse[None, :]
    cosine_table, sine_values = jnp.cos(angles), jnp.sin(angles)
    q_rot = apply_rotary(q_raw * root_mean_scale(q_raw) * qgain, cosine_table, sine_values)
    k_rot = apply_rotary(k_raw * root_mean_scale(k_raw) * kgain, cosine_table, sine_values)
    q_rot = q_rot.astype(BF)
    k_rot = k_rot.astype(BF).reshape(length, HD)
    allowed = (positions[None, :] <= positions[:, None]) & (ids[:, None] == ids[None, :])
    attended, log_totals = attend_forward(q_rot, k_rot, v_low, allowed)
    attended = attended.reshape(length, q_cols)

    out_part = matmul(attended, w_o).reshape(S, tokens, width)
    x_first = inputs[0].astype(F32)
    x_second = x_first + seq_reduce([out_part[k] for k in range(S)], S)
    normed_two = x_second * root_mean_scale(x_second)
    h2 = (normed_two * gain_two).astype(BF)

    my_experts = ((jnp.arange(S, dtype=jnp.int32) ^ s) * N + d).astype(F32)
    route_all = jnp.stack(route_blocks).astype(F32)
    hits = jnp.any(
        route_all[:, None, :, :] == my_experts[None, :, None, None], axis=-1
    )
    before = jnp.asarray(np.triu(np.ones((tokens, tokens), np.float32), 1), BF)
    ranks = jnp.einsum("rkt,tu->rku", hits.astype(BF), before, preferred_element_type=F32)
    ranks = jnp.where(hits, ranks, -1.0)
    chosen = (
        ranks[:, :, None, :] == jnp.arange(cap, dtype=F32)[None, None, :, None]
    ).astype(BF)
    chunks = ring.chunks()

    def select(c):
        m = len(c)
        table = jnp.stack([chosen[r] for r in c], axis=1)
        eye = jnp.eye(m, dtype=BF)
        wide = table[:, :, :, None, :] * eye[None, :, None, :, None]
        return wide.reshape(S * m * cap, m * tokens)

    tables = [select(c) for c in chunks]

    def exchange(rows):
        size = rows.shape[0] // S
        got = [rows[:size]]
        for k in range(1, S):
            got.append(swap(rows[k * size : (k + 1) * size], k, S))
        return jnp.concatenate(got, axis=0)

    def dispatch(token_blocks):
        result = []
        for c, table in zip(chunks, tables):
            source = jnp.concatenate([token_blocks[r] for r in c], axis=0)
            result.append(exchange(matmul(table, source).astype(BF)))
        return result

    dy_rows = dispatch(dy_blocks)
    down_w, gate_w, up_w = w_down[0], w_gate[0], w_up[0]
    pulled = [matmul_nt(rows, down_w) for rows in dy_rows]

    h2_blocks = ring.gather(h2)
    h2_rows = dispatch(h2_blocks)

    logits = [matmul(block, router) for block in h2_blocks]
    expert_ids = jnp.arange(experts, dtype=F32)

    def gates_of(r):
        pick = route_all[r][:, :, None] == expert_ids[None, None, :]
        taken = jnp.sum(jnp.where(pick, logits[r][:, None, :], 0.0), axis=-1)
        return jax.nn.softmax(taken, axis=-1), pick

    gate_list = [gates_of(r) for r in range(N)]
    gate_here = jnp.stack(
        [
            jnp.sum(
                jnp.where(
                    route_all[r][:, :, None] == my_experts[None, None, :],
                    gate_list[r][0][:, :, None],
                    0.0,
                ),
                axis=1,
            )
            for r in range(N)
        ]
    )
    slot_gates = jnp.sum(
        chosen.astype(F32) * jnp.transpose(gate_here, (0, 2, 1))[:, :, None, :], axis=-1
    )
    slot_gates = jnp.transpose(slot_gates, (1, 0, 2))
    slot_gates = jnp.stack(
        [slot_gates[0]] + [swap(slot_gates[k], k, S) for k in range(1, S)]
    )

    def of_chunk(values, c):
        return jnp.stack([values[:, r] for r in c], axis=1).reshape(-1)

    y_rows, back_rows, gate_terms = [], [], []
    weighted_hidden, weighted_gate, weighted_up = [], [], []
    for i, c in enumerate(chunks):
        rows, pull = h2_rows[i], pulled[i]
        g = matmul(rows, gate_w)
        u = matmul(rows, up_w)
        sig = jax.nn.sigmoid(g)
        silu = g * sig
        hidden = (silu * u).astype(BF)
        dg = pull * u * sig * (1.0 + g * (1.0 - sig))
        du = pull * silu
        back_rows.append(
            (matmul_nt(dg.astype(BF), gate_w) + matmul_nt(du.astype(BF), up_w)).astype(BF)
        )
        gate_terms.append(jnp.sum(pull * hidden.astype(F32), axis=-1))
        y_rows.append(matmul(hidden, down_w).astype(BF))
        weight = of_chunk(slot_gates, c)[:, None]
        weighted_hidden.append((hidden.astype(F32) * weight).astype(BF))
        weighted_gate.append((dg * weight).astype(BF))
        weighted_up.append((du * weight).astype(BF))

    def combine_table(i):
        c = chunks[i]
        m = len(c)
        gates = jnp.stack([gate_here[r] for r in c])
        scale = jnp.broadcast_to(
            jnp.transpose(gates, (2, 0, 1))[:, None, None], (S, m, cap, m, tokens)
        ).reshape(S * m * cap, m * tokens)
        return (tables[i].astype(F32) * scale).astype(BF)

    mixers = [combine_table(i) for i in range(len(chunks))]

    term_slots = jnp.zeros((N, S, cap), F32)
    terms = {}
    for i, c in enumerate(chunks):
        parts = gate_terms[i].reshape(S, len(c), cap)
        for j, r in enumerate(c):
            terms[r] = parts[:, j]
    terms = jnp.stack([terms[r] for r in range(N)], axis=1)
    terms = jnp.stack([terms[0]] + [swap(terms[k], k, S) for k in range(1, S)])
    term_tokens = jnp.einsum(
        "rkct,krc->rtk", chosen.astype(F32), terms, precision=EXACT_PRECISION
    )
    lanes = -(-experts // 128) * 128
    column = (
        my_experts[:, None] == jnp.arange(lanes, dtype=F32)[None, :]
    ).astype(F32)
    term_columns = jnp.einsum("rtk,ke->rte", term_tokens, column, precision=EXACT_PRECISION)

    def combine(expert_rows):
        sums = {}
        for i in reversed(range(len(chunks))):
            c = chunks[i]
            returned = exchange(expert_rows[i])
            mixed = matmul_tn(mixers[i], returned)
            for j, r in enumerate(c):
                sums[r] = mixed[j * tokens : (j + 1) * tokens]
        return sums

    back_sums = combine(back_rows)
    with_terms = ring.reduce(
        lambda r: jnp.concatenate([back_sums[r], term_columns[r]], axis=1)
    )

    y_rows[-1] = after(y_rows[-1], with_terms)
    y_sums = combine(y_rows)
    mixture = ring.reduce(lambda r: y_sums[r])
    result = (x_second + mixture).astype(BF)

    grad_final = grad_low.astype(F32)
    gate_probs, pick = gate_list[0]
    columns = with_terms[:, width : width + experts]
    grad_gates = jnp.sum(jnp.where(pick, columns[:, None, :], 0.0), axis=-1)
    grad_chosen = gate_probs * (
        grad_gates - jnp.sum(gate_probs * grad_gates, axis=-1, keepdims=True)
    )
    grad_logits = jnp.sum(jnp.where(pick, grad_chosen[:, :, None], 0.0), axis=1)
    grad_two = with_terms[:, :width] + jnp.dot(
        grad_logits, router.astype(F32).T, precision=EXACT_PRECISION
    )
    grad_router = jnp.dot(h2.astype(F32).T, grad_logits, precision=EXACT_PRECISION)
    grad_x_norm, norm_terms = rms_back(grad_two, x_second, gain_two)
    grad_gain_two = jnp.sum(norm_terms, axis=0)
    grad_second = grad_final + grad_x_norm
    grad_attn = jnp.stack(seq_gather(grad_second.astype(BF), S)).reshape(length, width)

    grad_heads = matmul_nt(grad_attn, w_o).astype(BF).reshape(length, heads, HD)
    out_sum = ring.reduce(
        lambda r: matmul_tn(
            lax.dynamic_slice(attended, (0, ring.index[r] * rows_out), (length, rows_out)),
            grad_attn,
        )
    ).astype(BF)
    out_sum = lax.ppermute(out_sum, ("seq", "shard"), [(b, a) for a, b in spread])
    out_sum = seq_gather(out_sum, S)
    grad_out_w = jnp.zeros((S * rows_out, width), F32)
    for k in range(S):
        grad_out_w = lax.dynamic_update_slice(
            grad_out_w, out_sum[k].astype(F32), (sources[k] * rows_out, 0)
        )

    grad_q, grad_k, grad_v = attend_backward(
        q_rot, k_rot, v_low, grad_heads, log_totals, allowed
    )
    grad_k, grad_v = grad_k.astype(F32), grad_v.astype(F32)
    bit = 1
    while bit < replicas:
        both = jnp.stack([grad_k, grad_v])
        both = both + swap(both.astype(BF), bit, S).astype(F32)
        grad_k, grad_v = both[0], both[1]
        bit *= 2
    grad_q_norm, q_terms = rms_back(
        apply_rotary(grad_q.astype(F32), cosine_table, -sine_values), q_raw, qgain
    )
    grad_k_norm, k_terms = rms_back(
        apply_rotary(grad_k.reshape(length, 1, HD), cosine_table, -sine_values), k_raw, kgain
    )
    grad_qgain = jnp.sum(q_terms, axis=(0, 1))
    grad_kgain = jnp.sum(k_terms, axis=(0, 1)) / replicas
    grad_q_raw = grad_q_norm.reshape(length, q_cols).astype(BF)
    grad_k_raw = grad_k_norm.reshape(length, HD).astype(BF)
    grad_v_raw = grad_v.astype(BF)
    grad_qkv = jnp.concatenate([grad_q_raw, grad_k_raw, grad_v_raw], axis=1)
    if replicas > 1:
        shared = jnp.concatenate(
            [grad_q_raw, grad_k_raw / replicas, grad_v_raw / replicas], axis=1
        )
    else:
        shared = grad_qkv
    grad_one_part = matmul_nt(shared, w_qkv)
    grad_gain_one = jnp.sum(grad_one_part * (x_all * factor_one), axis=0)

    small_grads = jnp.concatenate(
        [
            grad_gain_one.reshape(N, -1),
            grad_gain_two.reshape(N, -1),
            grad_qgain.reshape(N, -1),
            grad_kgain.reshape(N, -1),
            grad_router.reshape(N, -1),
        ],
        axis=1,
    )
    rest = extra * cols - small_grads.shape[1]
    small_grads = jnp.pad(small_grads, ((0, 0), (0, rest))).reshape(N, extra, cols)

    def grad_block(r):
        part = matmul_tn(
            lax.dynamic_slice(h1, (0, ring.index[r] * slab), (length, slab)), grad_qkv
        )
        tail = lax.dynamic_index_in_dim(small_grads, ring.index[r], 0, keepdims=False)
        return jnp.concatenate([part, tail], axis=0)

    qkv_sum = seq_gather(ring.reduce(grad_block).astype(BF), S)
    grad_query = jnp.zeros((slab, S * q_cols), F32)
    grad_key = jnp.zeros((slab, KEY_VALUE_HEADS * HD), F32)
    grad_value = jnp.zeros((slab, KEY_VALUE_HEADS * HD), F32)
    for k in range(S):
        full = qkv_sum[k][:slab].astype(F32)
        at = (sources[k] // replicas) * HD
        grad_query = lax.dynamic_update_slice(
            grad_query, full[:, :q_cols], (0, sources[k] * q_cols)
        )
        grad_key = lax.dynamic_update_slice(grad_key, full[:, q_cols : q_cols + HD], (0, at))
        grad_value = lax.dynamic_update_slice(grad_value, full[:, q_cols + HD :], (0, at))
    tail = tree_sum([qkv_sum[k][slab:].astype(F32) for k in range(S)]).reshape(-1)

    def tail_part(i):
        return tail[int(starts[i]) : int(starts[i + 1])]

    grad_one = seq_reduce(list(grad_one_part.reshape(S, tokens, width)), S)
    grad_x_first, _ = rms_back(grad_one, x_first, gain_one)
    grad_inputs = grad_second + grad_x_first

    def over_rows(left, right):
        return matmul_tn(jnp.concatenate(left, axis=0), jnp.concatenate(right, axis=0))

    grad_gate = over_rows(h2_rows, weighted_gate)
    grad_up = over_rows(h2_rows, weighted_up)
    grad_down = over_rows(weighted_hidden, dy_rows)

    return (
        result[None],
        grad_inputs[None],
        tail_part(0),
        grad_query,
        grad_key,
        grad_value,
        tail_part(2),
        tail_part(3),
        grad_out_w,
        tail_part(1),
        tail_part(4).reshape(slab, experts),
        grad_gate[None],
        grad_up[None],
        grad_down[None],
    )


def solution(mesh):
    in_specs = (
        P("shard", "seq", None),
        P("shard", "seq"),
        P("shard", "seq", None),
        P("shard"),
        P("shard", None),
        P("shard", None),
        P("shard", None),
        P("shard"),
        P("shard"),
        P("shard", None),
        P("shard"),
        P("shard", None),
        P(("seq", "shard"), None, None),
        P(("seq", "shard"), None, None),
        P(("seq", "shard"), None, None),
        P("shard", "seq", None),
    )
    out_specs = (
        P("shard", "seq", None),
        P("shard", "seq", None),
        P("shard"),
        P("shard", None),
        P("shard", None),
        P("shard", None),
        P("shard"),
        P("shard"),
        P("shard", None),
        P("shard"),
        P("shard", None),
        P(("seq", "shard"), None, None),
        P(("seq", "shard"), None, None),
        P(("seq", "shard"), None, None),
    )
    return jax.shard_map(
        per_device, mesh=mesh, in_specs=in_specs, out_specs=out_specs, check_vma=False
    )
```

time: 2110 us -> 925 us (0.44)
  waiting for transfers between devices: 1420 us -> 299 us
  blocking collectives: 242 us -> 0 us
  starting transfers between devices: 53.7 us -> 145 us
  local copies, waits for them, and re-layouts: 120 us -> 172 us
  between operations: 17.6 us -> 42.2 us
    reduce_scatter x5 -> x0, waiting for transfers between devices: 642 us -> none  [the longest x1 287 us: per_device(): lax.psum_scatter(grad_out_w.astype(jnp.bfloat16), 'shard', scatter_dimens...]
    all_gather x4 -> x0, waiting for transfers between devices: 366 us -> none  [the longest x1 216 us: per_device(): lax.all_gather(w_query, 'shard', axis=0, tiled=True)]
    all_to_all x9 -> x0, waiting for transfers between devices: 325 us -> none  [the longest x1 109 us: per_device(): lax.all_to_all(grad_in, ('seq', 'shard'), split_axis=0, concat_axis=0, ti...]
    ppermute x0 -> x134, waiting for transfers between devices: none -> 299 us  [the longest x68 162 us: swap(): return lax.ppermute(value, 'seq', [(i, i ^ bit) for i in range(count)])]
    all_gather x4 -> x0, blocking collectives: 165 us -> none  [the longest x1 129 us: per_device(): lax.all_gather(w_router, 'shard', axis=0, tiled=True)]
    ppermute x0 -> x134, starting transfers between devices: none -> 145 us  [the longest x68 85.1 us: swap(): return lax.ppermute(value, 'seq', [(i, i ^ bit) for i in range(count)])]
    psum x1 -> x0, waiting for transfers between devices: 80.4 us -> none  [per_device(): lax.psum(part_query.astype(jnp.bfloat16), 'seq').astype(jnp.float32)]
    all_to_all x9 -> x0, starting transfers between devices: 53.1 us -> none  [the longest x1 12.3 us: per_device(): lax.all_to_all(back_rows, ('seq', 'shard'), split_axis=0, concat_axis=0,...]
  transfers between devices with their start and end apart: 19 -> 134, of which waited for: 13 -> 53; matrix products, arithmetic and copies ran while one was open for 12% -> 40% of each run, Pallas kernels for 0% -> 0%
where the time goes in v1:
time: 925 us; the launch traced here: 914 us
  waiting for transfers between devices  299 us (32%)
  matrix products  174 us (19%)
  local copies, waits for them, and re-layouts  172 us (19%)
  starting transfers between devices  145 us (16%)
  other arithmetic  83 us (9%)
  between operations  42.2 us (5%)
    ppermute x68, waiting for transfers between devices, swap(): return lax.ppermute(value, 'seq', [(i, i ^ bit) for i in range(count)])  162 us
    ppermute x68, starting transfers between devices, swap(): return lax.ppermute(value, 'seq', [(i, i ^ bit) for i in range(count)])  85.1 us
    ppermute x32, waiting for transfers between devices, forward(): return lax.ppermute(value, 'shard', self.up)  62.7 us
    dot_general x30, matrix products, matmul(): return jnp.dot(a, b, preferred_element_type=F32)  60.8 us
    unnamed x546, local copies, waits for them, and re-layouts  58.6 us
    dot_general x27, matrix products, matmul_tn(): lax.dot_general(a, b, (((0,), (0,)), ((), ())), preferred_element_type=F32)  50.4 us
    ppermute x32, waiting for transfers between devices, backward(): return lax.ppermute(value, 'shard', self.down)  47.1 us
    dot_general x14, matrix products, matmul_nt(): lax.dot_general(a, b, (((1,), (1,)), ((), ())), preferred_element_type=F32)  42.4 us
  transfers between devices with their start and end apart: 134, of which 53 were waited for; matrix products, arithmetic and copies ran while one was open for 40% of the time, Pallas kernels for 0%

profile of v1, /device:TPU:5, one launch (start us, length us, event | category | flops | bytes accessed | tf_op | source)
XLA Modules:
  0.0 914.1 jit_solution(8951706100063961687)
XLA Ops:
  81.6 10.2 %collective-permute-done.3 = bf16[264,1280]{1,0:T(8,128)(2,1)} collective-permute-done((bf16[264,1280]{1,0:T(8,128)(2,1)}, bf16[264,1280]{1,0:T(8,128)(2,1)}, u32[]{:S(2)}, u32[]{:S(2)}) %collective-permute-start.3) | collective-permute-done | bytes 675872 | tf_op jit(solution)/shard_map/ppermute | solution.py:49
  104.9 7.9 collective-permute-done.4
  154.3 6.1 fusion.511
  225.6 9.8 %collective-permute-start.52 = (bf16[40,2048]{1,0:T(8,128)(2,1)S(1)}, bf16[40,2048]{1,0:T(8,128)(2,1)S(1)}, u32[]{:S(2)}, u32[]{:S(2)}) collective-permute-start(bf16[40,2048]{1,0:T(8,128)(2,1)S(1)} %get-tuple-element.233), channel_id=1, source_target_pairs={{0,8},{8,0},{16,24},{24,16},{1,9},{9,1},{17,25},{25,17},{2,10},{10... | collective-permute-start | bytes 491528 | tf_op jit(solution)/shard_map/ppermute | solution.py:87
  259.1 7.8 collective-permute-done.62
  280.3 7.3 collective-permute-done.67
  292.7 5.9 collective-permute-done.22
  341.1 12.0 %collective-permute-done.74 = bf16[120,2048]{1,0:T(8,128)(2,1)} collective-permute-done((bf16[120,2048]{1,0:T(8,128)(2,1)}, bf16[120,2048]{1,0:T(8,128)(2,1)}, u32[]{:S(2)}, u32[]{:S(2)}) %collective-permute-start.74) | collective-permute-done | bytes 491552 | tf_op jit(solution)/shard_map/ppermute | solution.py:87
  386.7 7.2 collective-permute-done.41
  477.5 14.9 %collective-permute-done.43 = bf16[80,2048]{1,0:T(8,128)(2,1)S(1)} collective-permute-done((bf16[80,2048]{1,0:T(8,128)(2,1)S(1)}, bf16[80,2048]{1,0:T(8,128)(2,1)S(1)}, u32[]{:S(2)}, u32[]{:S(2)}) %collective-permute-start.43) | collective-permute-done | bytes 327712 | tf_op jit(solution)/shard_map/ppermute | solution.py:87
  492.8 7.1 collective-permute-done.44
  507.6 6.3 collective-permute-done.36
  517.5 6.5 collective-permute-done.50
  524.0 10.6 %collective-permute-done.51 = bf16[120,2048]{1,0:T(8,128)(2,1)S(1)} collective-permute-done((bf16[120,2048]{1,0:T(8,128)(2,1)S(1)}, bf16[120,2048]{1,0:T(8,128)(2,1)S(1)}, u32[]{:S(2)}, u32[]{:S(2)}) %collective-permute-start.51) | collective-permute-done | bytes 491552 | tf_op jit(solution)/shard_map/ppermute | solution.py:87
  553.9 10.3 %collective-permute-done.85 = bf16[120,2048]{1,0:T(8,128)(2,1)S(1)} collective-permute-done((bf16[120,2048]{1,0:T(8,128)(2,1)S(1)}, bf16[120,2048]{1,0:T(8,128)(2,1)S(1)}, u32[]{:S(2)}, u32[]{:S(2)}) %collective-permute-start.85) | collective-permute-done | bytes 491552 | tf_op jit(solution)/shard_map/ppermute | solution.py:87
  564.1 10.5 %collective-permute-done.86 = bf16[120,2048]{1,0:T(8,128)(2,1)S(1)} collective-permute-done((bf16[120,2048]{1,0:T(8,128)(2,1)S(1)}, bf16[120,2048]{1,0:T(8,128)(2,1)S(1)}, u32[]{:S(2)}, u32[]{:S(2)}) %collective-permute-start.86) | collective-permute-done | bytes 491552 | tf_op jit(solution)/shard_map/ppermute | solution.py:87
  577.5 6.2 collective-permute-done.87
  585.6 11.2 %collective-permute-done.88 = bf16[128,2176]{1,0:T(8,128)(2,1)S(1)} collective-permute-done((bf16[128,2176]{1,0:T(8,128)(2,1)S(1)}, bf16[128,2176]{1,0:T(8,128)(2,1)S(1)}, u32[]{:S(2)}, u32[]{:S(2)}) %collective-permute-start.88) | collective-permute-done | bytes 557088 | tf_op jit(solution)/shard_map/ppermute | solution.py:46
  598.6 10.3 %collective-permute-done.89 = bf16[128,2176]{1,0:T(8,128)(2,1)S(1)} collective-permute-done((bf16[128,2176]{1,0:T(8,128)(2,1)S(1)}, bf16[128,2176]{1,0:T(8,128)(2,1)S(1)}, u32[]{:S(2)}, u32[]{:S(2)}) %collective-permute-start.89) | collective-permute-done | bytes 557088 | tf_op jit(solution)/shard_map/ppermute | solution.py:46
  610.8 6.4 convolution_bitcast_fusion.1
  630.7 9.1 collective-permute-done.96
  639.8 11.1 %collective-permute-done.97 = bf16[120,2048]{1,0:T(8,128)(2,1)S(1)} collective-permute-done((bf16[120,2048]{1,0:T(8,128)(2,1)S(1)}, bf16[120,2048]{1,0:T(8,128)(2,1)S(1)}, u32[]{:S(2)}, u32[]{:S(2)}) %collective-permute-start.97) | collective-permute-done | bytes 491552 | tf_op jit(solution)/shard_map/ppermute | solution.py:87
  653.6 6.2 convolution_bitcast_fusion.2
  666.4 6.4 convolution_bitcast_fusion
  694.8 5.7 fusion
  730.1 8.0 multiply_reduce_fusion
  758.9 5.9 collective-permute-start.28
  787.0 7.3 collective-permute-done.111
  831.3 5.7 collective-permute-done.127
  844.3 26.9 %collective-permute-done.128 = bf16[128,2048]{1,0:T(8,128)(2,1)S(1)} collective-permute-done((bf16[128,2048]{1,0:T(8,128)(2,1)S(1)}, bf16[128,2048]{1,0:T(8,128)(2,1)S(1)}, u32[]{:S(2)}, u32[]{:S(2)}) %collective-permute-start.128) | collective-permute-done | bytes 524320 | tf_op jit(solution)/shard_map/ppermute | solution.py:479
  874.4 6.1 collective-permute-done.129
  880.6 9.8 %collective-permute-start.130 = (bf16[2,128,2048]{2,1,0:T(8,128)(2,1)S(1)}, bf16[2,128,2048]{2,1,0:T(8,128)(2,1)S(1)}, u32[]{:S(2)}, u32[]{:S(2)}) collective-permute-start(bf16[2,128,2048]{2,1,0:T(8,128)(2,1)S(1)} %pad_maximum_fusion.13), channel_id=1, source_target_pairs={{0,8},{8,0},{16,24},{24,16},{1,9},{9,1},{17,25},{25,17},{2,10},{10... | collective-permute-start | bytes 3145736 | tf_op jit(solution)/shard_map/ppermute | solution.py:87
  (1174 shorter events, 588.7 us)
Async XLA Ops:
  8.6 64.9 %collective-permute-start.2 = (bf16[264,1280]{1,0:T(8,128)(2,1)}, bf16[264,1280]{1,0:T(8,128)(2,1)}, u32[]{:S(2)}, u32[]{:S(2)}) collective-permute-start(bf16[264,1280]{1,0:T(8,128)(2,1)} %pad_maximum_fusion.14), channel_id=1, source_target_pairs={{2,0},{4,2},{6,4},{7,6},{5,7},{3,5},{1,3},{0,1},{10,8},{12,10},{14... | collective-permute-start | bytes 2027528 | tf_op jit(solution)/shard_map/ppermute | solution.py:49
  9.9 64.5 %collective-permute-start.6 = (bf16[264,1280]{1,0:T(8,128)(2,1)}, bf16[264,1280]{1,0:T(8,128)(2,1)}, u32[]{:S(2)}, u32[]{:S(2)}) collective-permute-start(bf16[264,1280]{1,0:T(8,128)(2,1)} %pad_maximum_fusion.14), channel_id=1, source_target_pairs={{0,2},{2,4},{4,6},{6,7},{7,5},{5,3},{3,1},{1,0},{8,10},{10,12},{12... | collective-permute-start | bytes 2027528 | tf_op jit(solution)/shard_map/ppermute | solution.py:46
  12.0 118.9 %collective-permute-start.12 = (bf16[128,2048]{1,0:T(8,128)(2,1)}, bf16[128,2048]{1,0:T(8,128)(2,1)}, u32[]{:S(2)}, u32[]{:S(2)}) collective-permute-start(bf16[128,2048]{1,0:T(8,128)(2,1)} %constant_dynamic-slice_fusion), channel_id=1, source_target_pairs={{0,0},{8,1},{16,2},{24,3},{1,4},{9,5},{17,6},{25,7},{2,8},{10,9},{... | collective-permute-start | bytes 1572872 | tf_op jit(solution)/shard_map/ppermute | solution.py:274
  17.3 53.9 %collective-permute-start = (bf16[1,128,2048]{2,1,0:T(8,128)(2,1)}, bf16[1,128,2048]{2,1,0:T(8,128)(2,1)}, u32[]{:S(2)}, u32[]{:S(2)}) collective-permute-start(bf16[1,128,2048]{2,1,0:T(8,128)(2,1)} %param.19), channel_id=1, source_target_pairs={{0,16},{8,24},{16,0},{24,8},{1,17},{9,25},{17,1},{25,9},{2,18},{10... | collective-permute-start | bytes 1572872 | tf_op jit(solution)/shard_map/ppermute | solution.py:87
  19.6 42.2 %collective-permute-start.10 = (s32[1,128]{1,0:T(1,128)S(1)}, s32[1,128]{1,0:T(1,128)S(1)}, u32[]{:S(2)}, u32[]{:S(2)}) collective-permute-start(s32[1,128]{1,0:T(1,128)S(1)} %copy-done.210), channel_id=1, source_target_pairs={{0,16},{8,24},{16,0},{24,8},{1,17},{9,25},{17,1},{25,9},{2,18},{10... | collective-permute-start | bytes 1544 | tf_op jit(solution)/shard_map/ppermute | solution.py:87
  73.5 27.6 %collective-permute-start.1 = (bf16[2,128,2048]{2,1,0:T(8,128)(2,1)}, bf16[2,128,2048]{2,1,0:T(8,128)(2,1)}, u32[]{:S(2)}, u32[]{:S(2)}) collective-permute-start(bf16[2,128,2048]{2,1,0:T(8,128)(2,1)} %pad_maximum_fusion.8), channel_id=1, source_target_pairs={{0,8},{8,0},{16,24},{24,16},{1,9},{9,1},{17,25},{25,17},{2,10},{10... | collective-permute-start | bytes 3145736 | tf_op jit(solution)/shard_map/ppermute | solution.py:87
  130.9 61.7 %collective-permute-start.16 = (bf16[128,2048]{1,0:T(8,128)(2,1)}, bf16[128,2048]{1,0:T(8,128)(2,1)}, u32[]{:S(2)}, u32[]{:S(2)}) collective-permute-start(bf16[128,2048]{1,0:T(8,128)(2,1)} %collective-permute-done.12), channel_id=1, source_target_pairs={{0,2},{2,4},{4,6},{6,7},{7,5},{5,3},{3,1},{1,0},{8,10},{10,12},{12... | collective-permute-start | bytes 1572872 | tf_op jit(solution)/shard_map/ppermute | solution.py:46
  131.0 62.7 %collective-permute-start.13 = (bf16[128,2048]{1,0:T(8,128)(2,1)}, bf16[128,2048]{1,0:T(8,128)(2,1)}, u32[]{:S(2)}, u32[]{:S(2)}) collective-permute-start(bf16[128,2048]{1,0:T(8,128)(2,1)} %collective-permute-done.12), channel_id=1, source_target_pairs={{2,0},{4,2},{6,4},{7,6},{5,7},{3,5},{1,3},{0,1},{10,8},{12,10},{14... | collective-permute-start | bytes 1572872 | tf_op jit(solution)/shard_map/ppermute | solution.py:49
  223.0 25.8 %collective-permute-start.58 = (bf16[128,2048]{1,0:T(8,128)(2,1)S(1)}, bf16[128,2048]{1,0:T(8,128)(2,1)S(1)}, u32[]{:S(2)}, u32[]{:S(2)}) collective-permute-start(bf16[128,2048]{1,0:T(8,128)(2,1)S(1)} %bitcast.648), channel_id=1, source_target_pairs={{2,0},{4,2},{6,4},{7,6},{5,7},{3,5},{1,3},{0,1},{10,8},{12,10},{14... | collective-permute-start | bytes 1572872 | tf_op jit(solution)/shard_map/ppermute | solution.py:49
  290.3 34.0 %collective-permute-start.70 = (bf16[64,2048]{1,0:T(8,128)(2,1)S(1)}, bf16[64,2048]{1,0:T(8,128)(2,1)}, u32[]{:S(2)}, u32[]{:S(2)}) collective-permute-start(bf16[64,2048]{1,0:T(8,128)(2,1)S(1)} %slice.1072), channel_id=1, source_target_pairs={{0,2},{2,4},{4,6},{6,7},{7,5},{5,3},{3,1},{1,0},{8,10},{10,12},{12... | collective-permute-start | bytes 786440 | tf_op jit(solution)/shard_map/ppermute | solution.py:46
  291.3 33.0 %collective-permute-start.71 = (bf16[64,2048]{1,0:T(8,128)(2,1)}, bf16[64,2048]{1,0:T(8,128)(2,1)}, u32[]{:S(2)}, u32[]{:S(2)}) collective-permute-start(bf16[64,2048]{1,0:T(8,128)(2,1)} %slice.1073), channel_id=1, source_target_pairs={{2,0},{4,2},{6,4},{7,6},{5,7},{3,5},{1,3},{0,1},{10,8},{12,10},{14... | collective-permute-start | bytes 786440 | tf_op jit(solution)/shard_map/ppermute | solution.py:49
  336.2 25.8 %collective-permute-start.31 = (bf16[80,2048]{1,0:T(8,128)(2,1)S(1)}, bf16[80,2048]{1,0:T(8,128)(2,1)S(1)}, u32[]{:S(2)}, u32[]{:S(2)}) collective-permute-start(bf16[80,2048]{1,0:T(8,128)(2,1)S(1)} %get-tuple-element.199), channel_id=1, source_target_pairs={{0,8},{8,0},{16,24},{24,16},{1,9},{9,1},{17,25},{25,17},{2,10},{10... | collective-permute-start | bytes 983048 | tf_op jit(solution)/shard_map/ppermute | solution.py:87
  336.4 26.4 %collective-permute-start.32 = (bf16[80,2048]{1,0:T(8,128)(2,1)S(1)}, bf16[80,2048]{1,0:T(8,128)(2,1)S(1)}, u32[]{:S(2)}, u32[]{:S(2)}) collective-permute-start(bf16[80,2048]{1,0:T(8,128)(2,1)S(1)} %get-tuple-element.198), channel_id=1, source_target_pairs={{0,16},{8,24},{16,0},{24,8},{1,17},{9,25},{17,1},{25,9},{2,18},{10... | collective-permute-start | bytes 983048 | tf_op jit(solution)/shard_map/ppermute | solution.py:87
  338.4 28.0 %collective-permute-start.33 = (bf16[80,2048]{1,0:T(8,128)(2,1)S(1)}, bf16[80,2048]{1,0:T(8,128)(2,1)S(1)}, u32[]{:S(2)}, u32[]{:S(2)}) collective-permute-start(bf16[80,2048]{1,0:T(8,128)(2,1)S(1)} %get-tuple-element.197), channel_id=1, source_target_pairs={{0,24},{8,16},{16,8},{24,0},{1,25},{9,17},{17,9},{25,1},{2,26},{10... | collective-permute-start | bytes 983048 | tf_op jit(solution)/shard_map/ppermute | solution.py:87
  341.0 30.2 %collective-permute-start.38 = (bf16[128,2048]{1,0:T(8,128)(2,1)S(1)}, bf16[128,2048]{1,0:T(8,128)(2,1)S(1)}, u32[]{:S(2)}, u32[]{:S(2)}) collective-permute-start(bf16[128,2048]{1,0:T(8,128)(2,1)S(1)} %copy-done.102), channel_id=1, source_target_pairs={{0,2},{2,4},{4,6},{6,7},{7,5},{5,3},{3,1},{1,0},{8,10},{10,12},{12... | collective-permute-start | bytes 1572872 | tf_op jit(solution)/shard_map/ppermute | solution.py:46
  465.6 36.6 %collective-permute-start.79 = (bf16[80,2048]{1,0:T(8,128)(2,1)}, bf16[80,2048]{1,0:T(8,128)(2,1)S(1)}, u32[]{:S(2)}, u32[]{:S(2)}) collective-permute-start(bf16[80,2048]{1,0:T(8,128)(2,1)} %get-tuple-element.213), channel_id=1, source_target_pairs={{0,16},{8,24},{16,0},{24,8},{1,17},{9,25},{17,1},{25,9},{2,18},{10... | collective-permute-start | bytes 983048 | tf_op jit(solution)/shard_map/ppermute | solution.py:87
  468.8 34.2 %collective-permute-start.80 = (bf16[80,2048]{1,0:T(8,128)(2,1)S(1)}, bf16[80,2048]{1,0:T(8,128)(2,1)S(1)}, u32[]{:S(2)}, u32[]{:S(2)}) collective-permute-start(bf16[80,2048]{1,0:T(8,128)(2,1)S(1)} %copy-done.122), channel_id=1, source_target_pairs={{0,24},{8,16},{16,8},{24,0},{1,25},{9,17},{17,9},{25,1},{2,26},{10... | collective-permute-start | bytes 983048 | tf_op jit(solution)/shard_map/ppermute | solution.py:87
  474.6 25.4 %collective-permute-start.44 = (bf16[80,2048]{1,0:T(8,128)(2,1)S(1)}, bf16[80,2048]{1,0:T(8,128)(2,1)S(1)}, u32[]{:S(2)}, u32[]{:S(2)}) collective-permute-start(bf16[80,2048]{1,0:T(8,128)(2,1)S(1)} %copy-done.129), channel_id=1, source_target_pairs={{0,24},{8,16},{16,8},{24,0},{1,25},{9,17},{17,9},{25,1},{2,26},{10... | collective-permute-start | bytes 983048 | tf_op jit(solution)/shard_map/ppermute | solution.py:87
  477.2 27.7 %collective-permute-start.34 = (bf16[80,2048]{1,0:T(8,128)(2,1)S(1)}, bf16[80,2048]{1,0:T(8,128)(2,1)S(1)}, u32[]{:S(2)}, u32[]{:S(2)}) collective-permute-start(bf16[80,2048]{1,0:T(8,128)(2,1)S(1)} %copy-done.126), channel_id=1, source_target_pairs={{0,8},{8,0},{16,24},{24,16},{1,9},{9,1},{17,25},{25,17},{2,10},{10... | collective-permute-start | bytes 983048 | tf_op jit(solution)/shard_map/ppermute | solution.py:87
  505.1 29.6 %collective-permute-start.51 = (bf16[120,2048]{1,0:T(8,128)(2,1)S(1)}, bf16[120,2048]{1,0:T(8,128)(2,1)S(1)}, u32[]{:S(2)}, u32[]{:S(2)}) collective-permute-start(bf16[120,2048]{1,0:T(8,128)(2,1)S(1)} %copy-done.106), channel_id=1, source_target_pairs={{0,24},{8,16},{16,8},{24,0},{1,25},{9,17},{17,9},{25,1},{2,26},{10... | collective-permute-start | bytes 1474568 | tf_op jit(solution)/shard_map/ppermute | solution.py:87
  506.5 251.7 %collective-permute-start.26 = (bf16[40,2048]{1,0:T(8,128)(2,1)}, bf16[40,2048]{1,0:T(8,128)(2,1)}, u32[]{:S(2)}, u32[]{:S(2)}) collective-permute-start(bf16[40,2048]{1,0:T(8,128)(2,1)} %get-tuple-element.243), channel_id=1, source_target_pairs={{0,8},{8,0},{16,24},{24,16},{1,9},{9,1},{17,25},{25,17},{2,10},{10... | collective-permute-start | bytes 491528 | tf_op jit(solution)/shard_map/ppermute | solution.py:87
  630.1 31.5 %collective-permute-start.106 = (bf16[1,128,2048]{2,1,0:T(8,128)(2,1)S(1)}, bf16[1,128,2048]{2,1,0:T(8,128)(2,1)S(1)}, u32[]{:S(2)}, u32[]{:S(2)}) collective-permute-start(bf16[1,128,2048]{2,1,0:T(8,128)(2,1)S(1)} %get-tuple-element.118), channel_id=1, source_target_pairs={{0,16},{8,24},{16,0},{24,8},{1,17},{9,25},{17,1},{25,9},{2,18},{10... | collective-permute-start | bytes 1572872 | tf_op jit(solution)/shard_map/ppermute | solution.py:87
  682.5 64.1 %collective-permute-start.100 = (bf16[128,2048]{1,0:T(8,128)(2,1)}, bf16[128,2048]{1,0:T(8,128)(2,1)}, u32[]{:S(2)}, u32[]{:S(2)}) collective-permute-start(bf16[128,2048]{1,0:T(8,128)(2,1)} %get-tuple-element.145), channel_id=1, source_target_pairs={{0,2},{2,4},{4,6},{6,7},{7,5},{5,3},{3,1},{1,0},{8,10},{10,12},{12... | collective-permute-start | bytes 1572872 | tf_op jit(solution)/shard_map/ppermute | solution.py:46
  683.1 64.1 %collective-permute-start.104 = (bf16[128,2048]{1,0:T(8,128)(2,1)}, bf16[128,2048]{1,0:T(8,128)(2,1)}, u32[]{:S(2)}, u32[]{:S(2)}) collective-permute-start(bf16[128,2048]{1,0:T(8,128)(2,1)} %get-tuple-element.146), channel_id=1, source_target_pairs={{2,0},{4,2},{6,4},{7,6},{5,7},{3,5},{1,3},{0,1},{10,8},{12,10},{14... | collective-permute-start | bytes 1572872 | tf_op jit(solution)/shard_map/ppermute | solution.py:49
  765.0 36.2 %collective-permute-start.108 = (bf16[2,128,2048]{2,1,0:T(8,128)(2,1)S(1)}, bf16[2,128,2048]{2,1,0:T(8,128)(2,1)S(1)}, u32[]{:S(2)}, u32[]{:S(2)}) collective-permute-start(bf16[2,128,2048]{2,1,0:T(8,128)(2,1)S(1)} %pad_maximum_fusion.12), channel_id=1, source_target_pairs={{0,8},{8,0},{16,24},{24,16},{1,9},{9,1},{17,25},{25,17},{2,10},{10... | collective-permute-start | bytes 3145736 | tf_op jit(solution)/shard_map/ppermute | solution.py:87
  773.1 26.9 %collective-permute-start.115 = (bf16[264,1280]{1,0:T(8,128)(2,1)S(1)}, bf16[264,1280]{1,0:T(8,128)(2,1)S(1)}, u32[]{:S(2)}, u32[]{:S(2)}) collective-permute-start(bf16[264,1280]{1,0:T(8,128)(2,1)S(1)} %fusion.175), channel_id=1, source_target_pairs={{2,0},{4,2},{6,4},{7,6},{5,7},{3,5},{1,3},{0,1},{10,8},{12,10},{14... | collective-permute-start | bytes 2027528 | tf_op jit(solution)/shard_map/ppermute | solution.py:49
  786.0 25.2 %collective-permute-start.126 = (bf16[128,2048]{1,0:T(8,128)(2,1)S(1)}, bf16[128,2048]{1,0:T(8,128)(2,1)S(1)}, u32[]{:S(2)}, u32[]{:S(2)}) collective-permute-start(bf16[128,2048]{1,0:T(8,128)(2,1)S(1)} %fusion.98), channel_id=1, source_target_pairs={{2,0},{4,2},{6,4},{7,6},{5,7},{3,5},{1,3},{0,1},{10,8},{12,10},{14... | collective-permute-start | bytes 1572872 | tf_op jit(solution)/shard_map/ppermute | solution.py:49
  794.5 25.6 %collective-permute-start.112 = (bf16[264,1280]{1,0:T(8,128)(2,1)S(1)}, bf16[264,1280]{1,0:T(8,128)(2,1)S(1)}, u32[]{:S(2)}, u32[]{:S(2)}) collective-permute-start(bf16[264,1280]{1,0:T(8,128)(2,1)S(1)} %fusion.171), channel_id=1, source_target_pairs={{0,2},{2,4},{4,6},{6,7},{7,5},{5,3},{3,1},{1,0},{8,10},{10,12},{12... | collective-permute-start | bytes 2027528 | tf_op jit(solution)/shard_map/ppermute | solution.py:46
  800.2 25.6 %collective-permute-start.116 = (bf16[264,1280]{1,0:T(8,128)(2,1)S(1)}, bf16[264,1280]{1,0:T(8,128)(2,1)S(1)}, u32[]{:S(2)}, u32[]{:S(2)}) collective-permute-start(bf16[264,1280]{1,0:T(8,128)(2,1)S(1)} %fusion.174), channel_id=1, source_target_pairs={{2,0},{4,2},{6,4},{7,6},{5,7},{3,5},{1,3},{0,1},{10,8},{12,10},{14... | collective-permute-start | bytes 2027528 | tf_op jit(solution)/shard_map/ppermute | solution.py:49
  820.2 51.6 %collective-permute-start.113 = (bf16[264,1280]{1,0:T(8,128)(2,1)S(1)}, bf16[264,1280]{1,0:T(8,128)(2,1)S(1)}, u32[]{:S(2)}, u32[]{:S(2)}) collective-permute-start(bf16[264,1280]{1,0:T(8,128)(2,1)S(1)} %fusion.170), channel_id=1, source_target_pairs={{0,2},{2,4},{4,6},{6,7},{7,5},{5,3},{3,1},{1,0},{8,10},{10,12},{12... | collective-permute-start | bytes 2027528 | tf_op jit(solution)/shard_map/ppermute | solution.py:46
  825.9 46.0 %collective-permute-start.117 = (bf16[264,1280]{1,0:T(8,128)(2,1)S(1)}, bf16[264,1280]{1,0:T(8,128)(2,1)S(1)}, u32[]{:S(2)}, u32[]{:S(2)}) collective-permute-start(bf16[264,1280]{1,0:T(8,128)(2,1)S(1)} %fusion.173), channel_id=1, source_target_pairs={{2,0},{4,2},{6,4},{7,6},{5,7},{3,5},{1,3},{0,1},{10,8},{12,10},{14... | collective-permute-start | bytes 2027528 | tf_op jit(solution)/shard_map/ppermute | solution.py:49
  837.5 33.7 %collective-permute-start.128 = (bf16[128,2048]{1,0:T(8,128)(2,1)S(1)}, bf16[128,2048]{1,0:T(8,128)(2,1)S(1)}, u32[]{:S(2)}, u32[]{:S(2)}) collective-permute-start(bf16[128,2048]{1,0:T(8,128)(2,1)S(1)} %fusion.93), channel_id=1, source_target_pairs={{0,0},{1,8},{2,16},{3,24},{4,1},{5,9},{6,17},{7,25},{8,2},{9,10},{... | collective-permute-start | bytes 1572872 | tf_op jit(solution)/shard_map/ppermute | solution.py:479
  (341 other events, 3961.1 us)

commit v2 on v1

v2 whole, which is shorter than its diff:
```python
import jax
import jax.numpy as jnp
import numpy as np
from jax import lax
from jax.experimental import pallas as pl
from jax.experimental.pallas import tpu as pltpu
from jax.sharding import PartitionSpec as P

HQ = 32
KEY_VALUE_HEADS = 4
HEAD_DIMENSION = 128
TOPK = 8

EPSILON = 1e-06
ROPE_BASE = 1000000.0
NEGATIVE = -1e30
EXACT = lax.Precision.HIGHEST
BF = jnp.bfloat16
F32 = jnp.float32
I32 = jnp.int32


def ring_order(count):
    width = 4 if count >= 16 else 2
    if count % width or count // width < 2:
        return list(range(count))
    depth = count // width
    order = [z * width for z in range(depth)]
    for turn, z in enumerate(reversed(range(depth))):
        columns = range(1, width) if turn % 2 == 0 else range(width - 1, 0, -1)
        order += [z * width + y for y in columns]
    return order


class Ring:
    def __init__(self, count):
        self.n = count
        self.order = ring_order(count)
        place = [0] * count
        for i, d in enumerate(self.order):
            place[d] = i
        self.up = [(self.order[i], self.order[(i + 1) % count]) for i in range(count)]
        self.down = [(b, a) for a, b in self.up]
        seats = jnp.arange(count, dtype=I32)
        mine = seats == lax.axis_index("shard")
        me = jnp.sum(jnp.where(mine, jnp.asarray(place, I32), 0))
        ahead = (me + seats) % count
        table = jnp.asarray(self.order, I32)
        self.index = jnp.sum(
            jnp.where(ahead[:, None] == seats[None, :], table[None, :], 0), axis=1
        )

    def forward(self, value):
        return lax.ppermute(value, "shard", self.up)

    def backward(self, value):
        return lax.ppermute(value, "shard", self.down)

    def gather(self, value):
        n, half = self.n, self.n // 2
        blocks = [None] * n
        blocks[0] = value
        for j in range(1, half):
            blocks[n - j] = self.forward(blocks[(n - j + 1) % n])
            blocks[j] = self.backward(blocks[j - 1])
        cut = value.shape[0] // 2 // 16 * 16
        top = self.forward(blocks[(half + 1) % n][:cut])
        bottom = self.backward(blocks[half - 1][cut:])
        blocks[half] = jnp.concatenate([top, bottom], axis=0)
        return blocks

    def reduce(self, parts):
        n, half = self.n, self.n // 2
        far = parts[half]
        rows = far.shape[0]
        cut = rows // 2 // 16 * 16
        top = self.forward(far[:cut].astype(BF))
        bottom = self.backward(far[cut:].astype(BF))
        ahead = jnp.pad(top.astype(F32), ((0, rows - cut), (0, 0)))
        behind = jnp.pad(bottom.astype(F32), ((cut, 0), (0, 0)))
        for j in range(half - 1, 0, -1):
            ahead = self.forward((parts[j] + ahead).astype(BF))
            behind = self.backward((parts[n - j] + behind).astype(BF))
        return parts[0], ahead, behind

    def chunks(self):
        n, half = self.n, self.n // 2
        if half < 3:
            return [[r] for r in range(n)]
        near = [[j, n - j] for j in range(1, half - 1)]
        return [[0]] + near + [[half - 1, n - half + 1, half]]


def swap(value, bit, count):
    return lax.ppermute(value, "seq", [(i, i ^ bit) for i in range(count)])


def seq_gather(value, count):
    have = {0: value}
    bit = count // 2
    while bit:
        for k in sorted(have):
            have[k ^ bit] = swap(have[k], bit, count)
        bit //= 2
    return [have[k] for k in range(count)]


def seq_reduce(parts, count):
    have = dict(enumerate(parts))
    bit = 1
    while bit < count:
        keys = [k for k in sorted(have) if k & bit]
        got = swap(jnp.concatenate([have[k].astype(BF) for k in keys]), bit, count)
        if bit * 2 == count:
            return have[0], got
        size = parts[0].shape[0]
        for i, k in enumerate(keys):
            have[k ^ bit] = have[k ^ bit] + got[i * size : (i + 1) * size].astype(F32)
            del have[k]
        bit *= 2
    return have[0], jnp.zeros_like(have[0], BF)


def tree_sum(values):
    values = list(values)
    while len(values) > 1:
        values = [values[i] + values[i + 1] for i in range(0, len(values), 2)]
    return values[0]


def after(value, *others):
    return lax.optimization_barrier((value,) + others)[0]


def shaped(shape, dtype):
    return jax.ShapeDtypeStruct(tuple(shape), dtype)


def run(body, outs, operands, scratch=()):
    spaces = {"s": pltpu.SMEM, "a": pl.ANY, "v": pltpu.VMEM}
    specs, arrays = [], []
    for item in operands:
        kind, array = item if isinstance(item, tuple) else ("v", item)
        specs.append(pl.BlockSpec(memory_space=spaces[kind]))
        arrays.append(array)
    results = pl.pallas_call(
        body,
        out_shape=list(outs),
        in_specs=specs,
        out_specs=[pl.BlockSpec(memory_space=pltpu.VMEM)] * len(outs),
        scratch_shapes=list(scratch),
        compiler_params=pltpu.CompilerParams(vmem_limit_bytes=60 << 20),
        cost_estimate=pl.CostEstimate(flops=1 << 20, bytes_accessed=1 << 16, transcendentals=0),
    )(*arrays)
    return list(results)


def dot(a, b, precision=None):
    return jnp.dot(a, b, preferred_element_type=F32, precision=precision)


def dot_nt(a, b, precision=None):
    return lax.dot_general(
        a, b, (((1,), (1,)), ((), ())), preferred_element_type=F32, precision=precision
    )


def dot_tn(a, b, precision=None):
    return lax.dot_general(
        a, b, (((0,), (0,)), ((), ())), preferred_element_type=F32, precision=precision
    )


def iota(shape, dim):
    return lax.broadcasted_iota(I32, shape, dim)


def at(start, size):
    return pl.ds(pl.multiple_of(start, size), size)


def row_scale(values):
    return lax.rsqrt(jnp.mean(values * values, axis=-1, keepdims=True) + EPSILON)


def as_column(row):
    size = row.shape[-1]
    same = iota((size, size), 0) == iota((size, size), 1)
    return jnp.sum(jnp.where(same, row, 0.0), axis=1, keepdims=True)


def turn(values, cosines, sines):
    return values * cosines + pltpu.roll(values, HEAD_DIMENSION // 2, 1) * sines


def weights_of(query, keys, bias):
    scores = dot_nt(query, keys) * HEAD_DIMENSION ** (-0.5) + bias
    terms = jnp.exp(scores - jnp.max(scores, axis=-1, keepdims=True))
    return terms * (1.0 / jnp.sum(terms, axis=-1, keepdims=True))


def per_device(
    inputs,
    seq_ids,
    routes,
    norm1_gain,
    w_query,
    key_weight,
    value_weight,
    q_gain,
    k_gain,
    w_out,
    norm2_gain,
    w_router,
    w_gate,
    w_up,
    w_down,
    cotangent,
):
    T = inputs.shape[1]
    D = inputs.shape[2]
    S = lax.axis_size("seq")
    N = lax.axis_size("shard")
    s = lax.axis_index("seq")
    d = lax.axis_index("shard")
    ring = Ring(N)
    heads = HQ // S
    replicas = S // KEY_VALUE_HEADS
    HD = HEAD_DIMENSION
    L = T * S
    E = S * N
    SP = -(-S // 8) * 8
    FF = w_gate.shape[2]
    cap = max(2, T * TOPK * 5 // (4 * E))
    slab = D // N
    QC = heads * HD
    C = QC + 2 * HD
    PR = w_out.shape[0] // S
    W = D + 128
    chunks = ring.chunks()

    sources = jnp.arange(S, dtype=I32) ^ s
    meta = jnp.concatenate([ring.index, sources, sources * N + d, jnp.stack([s])]).astype(I32)
    meta_s = ("s", meta)
    SRC, EXP = N, N + S

    XR = 16
    while E % XR or (E // XR) * slab + slab + 128 + T > C:
        XR *= 2
    groups = E // XR
    misc = groups * slab
    spare = C - (misc + slab + 128 + T)

    seat = jnp.arange(128, dtype=I32)[None, :] // (128 // N) == d

    def placed(gain):
        return jnp.where(seat, jnp.tile(gain, N)[None, :], jnp.zeros((), BF))

    def pack_body(m, wq, wk, wv, g1, g2, qg, kg, router, table, out, sems):
        me = m[N + 2 * S]
        copies = [
            pltpu.make_async_copy(
                wq.at[:, at(me * QC, QC)], out.at[pl.ds(0, slab), pl.ds(0, QC)], sems.at[0]
            ),
            pltpu.make_async_copy(
                wk.at[:, at(me // replicas * HD, HD)],
                out.at[pl.ds(0, slab), pl.ds(QC, HD)],
                sems.at[1],
            ),
            pltpu.make_async_copy(
                wv.at[:, at(me // replicas * HD, HD)],
                out.at[pl.ds(0, slab), pl.ds(QC + HD, HD)],
                sems.at[2],
            ),
        ]
        for c in copies:
            c.start()
        low = pl.ds(slab, XR)
        for g in range(groups):
            out[low, g * slab : (g + 1) * slab] = router[g * XR : (g + 1) * XR, :]

        def two(first, second, size):
            line = iota((XR, size), 0)
            first, second = first[...].astype(F32), second[...].astype(F32)
            return jnp.where(line == 0, first, jnp.where(line == 8, second, 0.0)).astype(BF)

        out[low, misc : misc + slab] = two(g1, g2, slab)
        out[low, misc + slab : misc + slab + 128] = two(qg, kg, 128)
        lines = table[...].astype(F32)
        lines = jnp.concatenate([lines, jnp.zeros((XR - TOPK, T), F32)], axis=0)
        out[low, misc + slab + 128 : misc + slab + 128 + T] = lines.astype(BF)
        if spare:
            out[low, C - spare :] = jnp.zeros((XR, spare), BF)
        for c in copies:
            c.wait()

    (block,) = run(
        pack_body,
        [shaped((slab + XR, C), BF)],
        [
            meta_s,
            ("a", w_query),
            ("a", key_weight),
            ("a", value_weight),
            norm1_gain.reshape(1, -1),
            norm2_gain.reshape(1, -1),
            placed(q_gain),
            placed(k_gain),
            w_router.T,
            routes[0].T,
        ],
        [pltpu.SemaphoreType.DMA((3,))],
    )
    x_rows = seq_gather(inputs[0], S)
    id_rows = seq_gather(seq_ids, S)
    blocks = ring.gather(block)

    piece = lax.dynamic_slice(w_out, (s * PR, 0), (PR, D))
    spread = [((g % S) * N + g // S, g) for g in range(S * N)]
    piece = lax.ppermute(piece, ("seq", "shard"), spread)
    piece = after(piece, blocks[N // 2])
    out_blocks = ring.gather(piece)

    grad_low = cotangent[0]
    dy_blocks = ring.gather(after(grad_low, out_blocks[N // 2]))

    positions = (sources[:, None] * T + jnp.arange(T, dtype=I32)).reshape(-1)
    inverse = ROPE_BASE ** (-2.0 * jnp.arange(HD // 2, dtype=F32) / HD)
    angles = positions.astype(F32)[:, None] * inverse[None, :]
    cosines, sines = jnp.cos(angles), jnp.sin(angles)
    cosines = jnp.concatenate([cosines, cosines], axis=1)
    sines = jnp.concatenate([-sines, sines], axis=1)

    def attend_body(*refs):
        m, xs, ids = refs[0], refs[1 : 1 + S], refs[1 + S : 1 + 2 * S]
        cos, sin = refs[1 + 2 * S : 3 + 2 * S]
        blk = refs[3 + 2 * S : 3 + 2 * S + N]
        rest = refs[3 + 2 * S + N :]
        h1, raw, rot, krot, vlow, out, bias, g1, g2, gq, router, table, keys = rest[:13]
        full, ext, sems = rest[13:]
        copies, small = [], []
        for r in range(N):
            c = pltpu.make_async_copy(
                blk[r].at[pl.ds(slab, XR)], ext.at[r], sems.at[0, r]
            )
            c.start()
            small.append(c)
        for r in range(N):
            c = pltpu.make_async_copy(
                blk[r].at[pl.ds(0, slab)], full.at[at(m[r] * slab, slab)], sems.at[1, r]
            )
            c.start()
            copies.append(c)

        id_f = [i[...].astype(F32) for i in ids]
        for a in range(S):
            column = as_column(id_f[a])
            q_pos = m[SRC + a] * T + iota((T, T), 0)
            for b in range(S):
                k_pos = m[SRC + b] * T + iota((T, T), 1)
                allowed = (k_pos <= q_pos) & (column == id_f[b])
                bias[a * T : (a + 1) * T, b * T : (b + 1) * T] = jnp.where(
                    allowed, 0.0, NEGATIVE
                )

        for c in small:
            c.wait()
        gq[...] = jnp.zeros((8, 128), F32)
        for r in range(N):
            place = at(m[r] * slab, slab)
            for g in range(groups):
                router[g * XR : (g + 1) * XR, place] = ext[r, :, g * slab : (g + 1) * slab]
            gains = ext[r, :, misc : misc + slab].astype(F32)
            g1[:, place] = gains[0:1]
            g2[:, place] = gains[8:9]
            pair = ext[r, :, misc + slab : misc + slab + 128].astype(F32)
            gq[0:1, :] += pair[0:1]
            gq[1:2, :] += pair[8:9]
            lines = ext[r, :, misc + slab + 128 : misc + slab + 128 + T].astype(F32)[:TOPK]
            table[r] = lines
            keys[r] = jnp.zeros((SP, T), F32)
            for k in range(S):
                expert = m[EXP + k].astype(F32)
                keys[r, k : k + 1, :] = jnp.max(
                    jnp.where(lines == expert, 1.0, 0.0), axis=0, keepdims=True
                )
        hits = keys[...].reshape(N * SP, T)
        earlier = jnp.where(iota((T, T), 0) < iota((T, T), 1), 1.0, 0.0).astype(BF)
        ranks = dot(hits.astype(BF), earlier)
        keys[...] = jnp.where(hits > 0.0, ranks, -1e6).reshape(N, SP, T)

        for k in range(S):
            x = xs[k][...].astype(F32)
            h1[k * T : (k + 1) * T, :] = (x * row_scale(x) * g1[...]).astype(BF)
        for c in copies:
            c.wait()

        wide = 256 if C % 256 == 0 else 128

        def project(i, carry):
            raw[:, at(i * wide, wide)] = dot(h1[...], full[:, at(i * wide, wide)])
            return carry

        lax.fori_loop(0, C // wide, project, 0)
        k_raw = raw[:, QC : QC + HD]
        krot[...] = turn(k_raw * row_scale(k_raw) * gq[1:2, :], cos[...], sin[...]).astype(BF)
        vlow[...] = raw[:, QC + HD :].astype(BF)

        def head(h, carry):
            lanes = at(h * HD, HD)
            q_raw = raw[:, lanes]
            q = turn(q_raw * row_scale(q_raw) * gq[0:1, :], cos[...], sin[...]).astype(BF)
            rot[:, lanes] = q
            p = weights_of(q, krot[...], bias[...]).astype(BF)
            out[:, lanes] = dot(p, vlow[...]).astype(BF)
            return carry

        lax.fori_loop(0, heads, head, 0)

    (
        h1,
        qkv,
        q_rot,
        k_rot,
        v_low,
        attended,
        bias,
        gain_one,
        gain_two,
        gain_qk,
        router_t,
        route_t,
        keys,
    ) = run(
        attend_body,
        [
            shaped((L, D), BF),
            shaped((L, C), F32),
            shaped((L, QC), BF),
            shaped((L, HD), BF),
            shaped((L, HD), BF),
            shaped((L, QC), BF),
            shaped((L, L), F32),
            shaped((1, D), F32),
            shaped((1, D), F32),
            shaped((8, 128), F32),
            shaped((E, D), BF),
            shaped((N, TOPK, T), F32),
            shaped((N, SP, T), F32),
        ],
        [meta_s] + x_rows + id_rows + [cosines, sines] + [("a", b) for b in blocks],
        [
            pltpu.VMEM((D, C), BF),
            pltpu.VMEM((N, XR, C), BF),
            pltpu.SemaphoreType.DMA((2, N)),
        ],
    )

    def fetch_out(m, pieces, full, sems):
        copies = []
        for r in range(N):
            c = pltpu.make_async_copy(pieces[r], full.at[at(m[r] * PR, PR)], sems.at[r])
            c.start()
            copies.append(c)
        return copies

    def project_body(*refs):
        m, o, pieces = refs[0], refs[1], refs[2 : 2 + N]
        out, full, sems = refs[2 + N :]
        for c in fetch_out(m, pieces, full, sems):
            c.wait()

        def tile(i, carry):
            out[:, at(i * 512, 512)] = dot(o[...], full[:, at(i * 512, 512)])
            return carry

        lax.fori_loop(0, D // 512, tile, 0)

    (out_part,) = run(
        project_body,
        [shaped((L, D), F32)],
        [meta_s, attended] + [("a", b) for b in out_blocks],
        [pltpu.VMEM((QC, D), BF), pltpu.SemaphoreType.DMA((N,))],
    )
    x2_own, x2_got = seq_reduce([out_part[k * T : (k + 1) * T] for k in range(S)], S)

    def second_body(x, own, got, g2, x2_out, h2_out):
        x2 = x[...].astype(F32) + own[...] + got[...].astype(F32)
        x2_out[...] = x2
        h2_out[...] = (x2 * row_scale(x2) * g2[...]).astype(BF)

    x_second, h2 = run(
        second_body,
        [shaped((T, D), F32), shaped((T, D), BF)],
        [inputs[0], x2_own, x2_got, gain_two],
    )

    def select(token_blocks, c):
        m = len(c)

        def body(*refs):
            key, tokens, outs = refs[0], refs[1 : 1 + m], refs[1 + m :]
            for k in range(S):
                acc = None
                for j, r in enumerate(c):
                    slot = key[r, k : k + 1, :] + float(j * cap)
                    pick = jnp.where(
                        iota((m * cap, T), 0).astype(F32) == slot, 1.0, 0.0
                    ).astype(BF)
                    term = dot(pick, tokens[j][...])
                    acc = term if acc is None else acc + term
                outs[k][...] = acc.astype(BF)

        return run(
            body, [shaped((m * cap, D), BF)] * S, [keys] + [token_blocks[r] for r in c]
        )

    def exchange(pieces):
        return [pieces[0]] + [swap(pieces[k], k, S) for k in range(1, S)]

    dy_rows = [exchange(select(dy_blocks, c)) for c in chunks]
    h2_blocks = ring.gather(h2)
    h2_rows = [exchange(select(h2_blocks, c)) for c in chunks]

    def gate_body(*refs):
        m, tokens = refs[0], refs[1 : 1 + N]
        router, table, key, gates_k, own, slots = refs[1 + N :]
        line = iota((E, T), 0).astype(F32)
        for r in range(N):
            logits = dot_nt(router[...], tokens[r][...])
            routed = jnp.zeros((E, T), F32)
            for j in range(TOPK):
                routed = jnp.where(line == table[r, j : j + 1, :], 1.0, routed)
            top = jnp.max(jnp.where(routed > 0.0, logits, NEGATIVE), axis=0, keepdims=True)
            terms = jnp.where(routed > 0.0, jnp.exp(logits - top), 0.0)
            gates = terms / jnp.sum(terms, axis=0, keepdims=True)
            if r == 0:
                eye = jnp.where(iota((E, 128), 0) == iota((E, 128), 1), 1.0, 0.0)
                own[...] = dot_tn(gates, eye, EXACT)
            gates_k[r] = jnp.zeros((SP, T), F32)
            for k in range(S):
                gate = jnp.sum(
                    jnp.where(line == m[EXP + k].astype(F32), gates, 0.0),
                    axis=0,
                    keepdims=True,
                )
                gates_k[r, k : k + 1, :] = gate
                pick = jnp.where(iota((cap, T), 0).astype(F32) == key[r, k : k + 1, :], 1.0, 0.0)
                slots[k, r : r + 1, :] = dot_nt(
                    jnp.broadcast_to(gate, (8, T)), pick, EXACT
                )[0:1]

    gate_k, gate_own, slot_gates = run(
        gate_body,
        [shaped((N, SP, T), F32), shaped((T, 128), F32), shaped((S, N, cap), F32)],
        [meta_s] + h2_blocks + [router_t, route_t, keys],
    )
    slot_gates = [slot_gates[0]] + [swap(slot_gates[k], k, S) for k in range(1, S)]

    gate_w, up_w, down_w = w_gate[0], w_up[0], w_down[0]

    def expert(c, x_pieces, y_pieces):
        m = len(c)
        size = m * cap
        pad = -(-size // 16) * 16
        rows = S * pad

        def body(*refs):
            mt, xs, ys = refs[0], refs[1 : 1 + S], refs[1 + S : 1 + 2 * S]
            wg, wu, wd = refs[1 + 2 * S : 4 + 2 * S]
            rest = refs[4 + 2 * S :]
            backs, fronts = rest[:S], rest[S : 2 * S]
            xp, yp, hid, dg_out, du_out, sums = rest[2 * S :]
            for k in range(S):
                for source, target in ((xs[k], xp), (ys[k], yp)):
                    value = source[...]
                    if pad > size:
                        value = jnp.concatenate(
                            [value, jnp.zeros((pad - size, D), BF)], axis=0
                        )
                    target[k * pad : (k + 1) * pad, :] = value
            sums[...] = jnp.zeros_like(sums)

            def first(i, carry):
                lanes = at(i * 256, 256)
                g = dot(xp[...], wg[:, lanes])
                u = dot(xp[...], wu[:, lanes])
                z = dot_nt(yp[...], wd[lanes, :])
                sig = 1.0 / (1.0 + jnp.exp(-g))
                silu = g * sig
                hidden = (silu * u).astype(BF)
                hid[:, lanes] = hidden
                du_out[:, lanes] = (z * silu).astype(BF)
                dg_out[:, lanes] = (z * u * sig * (1.0 + g * (1.0 - sig))).astype(BF)
                sums[...] += jnp.sum(z * hidden.astype(F32), axis=1, keepdims=True)
                return carry

            lax.fori_loop(0, FF // 256, first, 0)

            def second(i, carry):
                cols = at(i * 512, 512)
                back = dot_nt(dg_out[...], wg[cols, :]) + dot_nt(du_out[...], wu[cols, :])
                front = dot(hid[...], wd[:, cols])
                for k in range(S):
                    part = slice(k * pad, k * pad + size)
                    backs[k][:, cols] = back[part].astype(BF)
                    fronts[k][:, cols] = front[part].astype(BF)
                return carry

            lax.fori_loop(0, D // 512, second, 0)
            mine = iota((pad, 128), 1) == mt[EXP]
            for k in range(S):
                term = jnp.where(mine, sums[k * pad : (k + 1) * pad, 0:1], 0.0)
                backs[k][:, D:] = term[:size].astype(BF)

        outs = run(
            body,
            [shaped((size, W), BF)] * S
            + [shaped((size, D), BF)] * S
            + [shaped((rows, D), BF)] * 2
            + [shaped((rows, FF), BF)] * 3,
            [meta_s] + x_pieces + y_pieces + [gate_w, up_w, down_w],
            [pltpu.VMEM((rows, 128), F32)],
        )
        return outs[:S], outs[S : 2 * S], outs[2 * S :]

    backs, fronts, kept = [], [], []
    for i, c in enumerate(chunks):
        back, front, rest = expert(c, h2_rows[i], dy_rows[i])
        backs.append(back)
        fronts.append(front)
        kept.append(rest)

    def mix(i, pieces):
        c = chunks[i]
        m = len(c)
        wide = pieces[0].shape[1]

        def body(*refs):
            key, gate, rows, outs = refs[0], refs[1], refs[2 : 2 + S], refs[2 + S :]
            for j, r in enumerate(c):
                acc = None
                for k in range(S):
                    slot = key[r, k : k + 1, :] + float(j * cap)
                    hit = iota((m * cap, T), 0).astype(F32) == slot
                    weight = jnp.where(hit, gate[r, k : k + 1, :], 0.0).astype(BF)
                    term = dot_tn(weight, rows[k][...])
                    acc = term if acc is None else acc + term
                outs[j][...] = acc

        return run(body, [shaped((T, wide), F32)] * m, [keys, gate_k] + pieces)

    def combine(expert_pieces):
        sums = {}
        for i in reversed(range(len(chunks))):
            for r, value in zip(chunks[i], mix(i, exchange(expert_pieces[i]))):
                sums[r] = value
        return [sums[r] for r in range(N)]

    back_own, back_ahead, back_behind = ring.reduce(combine(backs))

    fronts[-1] = [after(fronts[-1][0], back_ahead)] + fronts[-1][1:]
    y_own, y_ahead, y_behind = ring.reduce(combine(fronts))
    result = (
        x_second + y_own + y_ahead.astype(F32) + y_behind.astype(F32)
    ).astype(BF)

    extra_rows = -(-(E // 8 * slab + slab) // D) * 8

    def tokens_body(own, ahead, behind, x2, g2, router, gates, hidden, dy, dx2, da, small):
        total = own[...] + ahead[...].astype(F32) + behind[...].astype(F32)
        gated = total[:, D:]
        dl = gated - gates[...] * jnp.sum(gated, axis=1, keepdims=True)
        grad = total[:, :D] + dot(dl[:, :E], router[...].astype(F32), EXACT)
        small[0:E, :] = dot_tn(dl, hidden[...].astype(F32), EXACT)[:E]
        scale = row_scale(x2[...])
        n2 = x2[...] * scale
        dn = grad * g2[...]
        small[E : E + 8, :] = jnp.broadcast_to(
            jnp.sum(grad * n2, axis=0, keepdims=True), (8, D)
        )
        out = dy[...].astype(F32) + scale * (
            dn - n2 * jnp.mean(dn * n2, axis=-1, keepdims=True)
        )
        dx2[...] = out
        da[...] = out.astype(BF)

    grad_second, grad_attn, small_two = run(
        tokens_body,
        [shaped((T, D), F32), shaped((T, D), BF), shaped((E + 8, D), F32)],
        [
            back_own,
            back_ahead,
            back_behind,
            x_second,
            gain_two,
            router_t,
            gate_own,
            h2,
            grad_low,
        ],
    )
    da_rows = seq_gather(grad_attn, S)

    def out_grad_body(*refs):
        m, o, das, small = refs[0], refs[1], refs[2 : 2 + S], refs[2 + S]
        outs, full = refs[3 + S : 3 + S + N], refs[3 + S + N]
        da = jnp.concatenate([a[...] for a in das], axis=0)
        if PR % 128:
            full[...] = dot_tn(o[...], da)
        for r in range(N):
            if PR % 128:
                outs[r][0:PR, :] = full[at(m[r] * PR, PR), :]
            else:
                outs[r][0:PR, :] = dot_tn(o[:, at(m[r] * PR, PR)], da)
            place = at(m[r] * slab, slab)
            tail = [small[8 * g : 8 * (g + 1), place] for g in range(E // 8 + 1)]
            used = len(tail) * slab
            room = extra_rows // 8 * D
            if room > used:
                tail.append(jnp.zeros((8, room - used), F32))
            tail = jnp.concatenate(tail, axis=1)
            for g in range(extra_rows // 8):
                outs[r][PR + 8 * g : PR + 8 * (g + 1), :] = tail[:, g * D : (g + 1) * D]

    out_parts = run(
        out_grad_body,
        [shaped((PR + extra_rows, D), F32)] * N,
        [meta_s, attended] + da_rows + [small_two],
        [pltpu.VMEM((QC, D) if PR % 128 else (8, 128), F32)],
    )
    out_own, out_ahead, out_behind = ring.reduce(out_parts)
    out_sum = (out_own + out_ahead.astype(F32) + out_behind.astype(F32)).astype(BF)
    out_piece = lax.ppermute(out_sum[:PR], ("seq", "shard"), [(b, a) for a, b in spread])
    out_pieces = seq_gather(out_piece, S)
    tail_pieces = seq_gather(out_sum[PR:], S)

    def out_join_body(*refs):
        m, pieces, tails = refs[0], refs[1 : 1 + S], refs[1 + S : 1 + 2 * S]
        out, small = refs[1 + 2 * S :]
        for k in range(S):
            out[at(m[SRC + k] * PR, PR), :] = pieces[k][...].astype(F32)
        small[...] = tree_sum([t[...].astype(F32) for t in tails])

    grad_out_w, tail_two = run(
        out_join_body,
        [shaped((S * PR, D), F32), shaped((extra_rows, D), F32)],
        [meta_s] + out_pieces + tail_pieces,
    )
    lines = [
        tail_two[8 * g : 8 * (g + 1), i * slab : (i + 1) * slab]
        for g in range(extra_rows // 8)
        for i in range(D // slab)
    ]
    grad_router = jnp.concatenate(lines[: E // 8], axis=0).T
    grad_gain_two = lines[E // 8][0]

    def back_body(*refs):
        m, das, pieces = refs[0], refs[1 : 1 + S], refs[1 + S : 1 + S + N]
        raw, rot, krot, vlow, bias_, gq, cos, sin = refs[1 + S + N : 9 + S + N]
        dq, dk_out, dv_out, gain, full, do, dk, dv, sems = refs[9 + S + N :]
        copies = fetch_out(m, pieces, full, sems)
        gain[...] = jnp.zeros_like(gain)
        dk[...] = jnp.zeros_like(dk)
        dv[...] = jnp.zeros_like(dv)
        for c in copies:
            c.wait()
        wide = 256 if QC % 256 == 0 else 128
        for k in range(S):

            def tile(i, carry, k=k):
                do[k * T : (k + 1) * T, at(i * wide, wide)] = dot_nt(
                    das[k][...], full[at(i * wide, wide), :]
                ).astype(BF)
                return carry

            lax.fori_loop(0, QC // wide, tile, 0)

        def head(h, carry):
            lanes = at(h * HD, HD)
            q = rot[:, lanes]
            grad = do[:, lanes]
            p = weights_of(q, krot[...], bias_[...])
            dp = dot_nt(grad, vlow[...])
            centre = jnp.sum(p * dp, axis=-1, keepdims=True)
            ds = (p * (dp - centre)).astype(BF)
            scale = HD ** (-0.5)
            dk[...] += dot_tn(ds, q) * scale
            dv[...] += dot_tn(p.astype(BF), grad)
            dqr = (dot(ds, krot[...]) * scale).astype(BF).astype(F32)
            dqn = turn(dqr, cos[...], -sin[...])
            q_raw = raw[:, lanes]
            factor = row_scale(q_raw)
            nq = q_raw * factor
            gain[0:1, :] += jnp.sum(dqn * nq, axis=0, keepdims=True)
            dn = dqn * gq[0:1, :]
            dq[:, lanes] = (
                factor * (dn - nq * jnp.mean(dn * nq, axis=-1, keepdims=True))
            ).astype(BF)
            return carry

        lax.fori_loop(0, heads, head, 0)
        dk_out[...] = dk[...].astype(BF)
        dv_out[...] = dv[...].astype(BF)

    grad_q, grad_k, grad_v, gain_sum = run(
        back_body,
        [
            shaped((L, QC), BF),
            shaped((L, HD), BF),
            shaped((L, HD), BF),
            shaped((8, 128), F32),
        ],
        [meta_s]
        + da_rows
        + [("a", b) for b in out_blocks]
        + [qkv, q_rot, k_rot, v_low, bias, gain_qk, cosines, sines],
        [
            pltpu.VMEM((QC, D), BF),
            pltpu.VMEM((L, QC), BF),
            pltpu.VMEM((L, HD), F32),
            pltpu.VMEM((L, HD), F32),
            pltpu.SemaphoreType.DMA((N,)),
        ],
    )
    if replicas > 1:
        both = jnp.concatenate([grad_k, grad_v], axis=1).astype(F32)
        bit = 1
        while bit < replicas:
            both = both + swap(both.astype(BF), bit, S).astype(F32)
            bit *= 2
        grad_k, grad_v = both[:, :HD], both[:, HD:]

    def weight_grad_body(m, h, dq, dk, dv, raw, gq, cos, sin, gain, *rest):
        outs, dkv = rest[:N], rest[N]
        k_raw = raw[:, QC : QC + HD]
        factor = row_scale(k_raw)
        nk = k_raw * factor
        dkn = turn(dk[...].astype(F32), cos[...], -sin[...])
        k_gain_part = jnp.sum(dkn * nk, axis=0, keepdims=True) * (1.0 / replicas)
        dn = dkn * gq[1:2, :]
        dk_raw = factor * (dn - nk * jnp.mean(dn * nk, axis=-1, keepdims=True))
        dkv[:, 0:HD] = dk_raw.astype(BF)
        dkv[:, HD:] = dv[...].astype(BF)
        for r in range(N):
            rows = h[:, at(m[r] * slab, slab)]
            outs[r][0:slab, 0:QC] = dot_tn(rows, dq[...])
            outs[r][0:slab, QC:] = dot_tn(rows, dkv[...])
            line = iota((8, 128), 0)
            outs[r][slab:, :] = jnp.zeros((8, C), F32)
            outs[r][slab:, 0:128] = jnp.where(
                line == 0, gain[0:1, :], jnp.where(line == 1, k_gain_part, 0.0)
            )

    results = run(
        weight_grad_body,
        [shaped((slab + 8, C), F32)] * N + [shaped((L, 2 * HD), BF)],
        [meta_s, h1, grad_q, grad_k, grad_v, qkv, gain_qk, cosines, sines, gain_sum],
    )
    block_parts, grad_kv = results[:N], results[N]
    block_own, block_ahead, block_behind = ring.reduce(block_parts)
    block_sum = (block_own + block_ahead.astype(F32) + block_behind.astype(F32)).astype(BF)
    block_pieces = seq_gather(block_sum, S)

    def first_back_body(*refs):
        m, dq, dkv, blk = refs[0], refs[1], refs[2], refs[3 : 3 + N]
        out, full, sems = refs[3 + N :]
        copies = []
        for r in range(N):
            c = pltpu.make_async_copy(
                blk[r].at[pl.ds(0, slab)], full.at[at(m[r] * slab, slab)], sems.at[r]
            )
            c.start()
            copies.append(c)
        share = (dkv[...].astype(F32) * (1.0 / replicas)).astype(BF)
        for c in copies:
            c.wait()

        def tile(i, carry):
            rows = at(i * 512, 512)
            out[:, rows] = dot_nt(dq[...], full[rows, 0:QC]) + dot_nt(share, full[rows, QC:])
            return carry

        lax.fori_loop(0, D // 512, tile, 0)

    (one_part,) = run(
        first_back_body,
        [shaped((L, D), F32)],
        [meta_s, grad_q, grad_kv] + [("a", b) for b in blocks],
        [pltpu.VMEM((D, C), BF), pltpu.SemaphoreType.DMA((N,))],
    )
    one_own, one_got = seq_reduce([one_part[k * T : (k + 1) * T] for k in range(S)], S)

    def inputs_body(x_ref, own, got, g1, dx2, out):
        x = x_ref[...].astype(F32)
        grad = own[...] + got[...].astype(F32)
        scale = row_scale(x)
        n1 = x * scale
        dn = grad * g1[...]
        out[...] = dx2[...] + scale * (
            dn - n1 * jnp.mean(dn * n1, axis=-1, keepdims=True)
        )

    (grad_inputs,) = run(
        inputs_body,
        [shaped((T, D), F32)],
        [inputs[0], one_own, one_got, gain_one, grad_second],
    )

    def join_body(*refs):
        m, pieces = refs[0], refs[1 : 1 + S]
        wq, wk, wv, oq, ok, ov, gains, rows = refs[1 + S :]
        for k in range(S):
            source = m[SRC + k]
            oq[:, at(source * QC, QC)] = pieces[k][0:slab, 0:QC].astype(F32)
            lanes = at(source // replicas * HD, HD)
            ok[:, lanes] = pieces[k][0:slab, QC : QC + HD].astype(F32)
            ov[:, lanes] = pieces[k][0:slab, QC + HD :].astype(F32)
        total = jnp.sum(oq[...] * wq[...].astype(F32), axis=1, keepdims=True)
        total += jnp.sum(ok[...] * wk[...].astype(F32), axis=1, keepdims=True)
        total += jnp.sum(ov[...] * wv[...].astype(F32), axis=1, keepdims=True)
        same = iota((slab, slab), 0) == iota((slab, slab), 1)
        rows[...] = jnp.broadcast_to(
            jnp.sum(jnp.where(same, total, 0.0), axis=0, keepdims=True), (8, slab)
        )
        gains[...] = tree_sum([p[slab:, 0:128].astype(F32) for p in pieces])

    grad_query, grad_key, grad_value, gain_rows, one_rows = run(
        join_body,
        [
            shaped((slab, S * QC), F32),
            shaped((slab, KEY_VALUE_HEADS * HD), F32),
            shaped((slab, KEY_VALUE_HEADS * HD), F32),
            shaped((8, 128), F32),
            shaped((8, slab), F32),
        ],
        [meta_s] + block_pieces + [w_query, key_weight, value_weight],
    )
    grad_gain_one = one_rows[0] / norm1_gain.astype(F32)
    share = HD // N
    grad_qgain = lax.dynamic_slice(gain_rows[0], (d * share,), (share,))
    grad_kgain = lax.dynamic_slice(gain_rows[1], (d * share,), (share,))

    stacked_gates = [
        jnp.stack([jnp.stack([g[r] for r in c]).reshape(-1) for g in slot_gates]) for c in chunks
    ]

    def expert_grad_body(*refs):
        count = len(chunks)
        gates, mats = refs[:count], refs[count : 6 * count]
        outs = refs[6 * count : 6 * count + 3]
        hid_s, dg_s, du_s = refs[6 * count + 3 :]
        offset = 0
        spans = []
        for i, c in enumerate(chunks):
            xp, yp, hid, dg, du = mats[5 * i : 5 * (i + 1)]
            size = len(c) * cap
            pad = -(-size // 16) * 16
            for k in range(S):
                column = as_column(gates[i][k : k + 1, :])
                if pad > size:
                    column = jnp.concatenate([column, jnp.zeros((pad - size, 1), F32)], axis=0)
                part = slice(k * pad, (k + 1) * pad)
                to = slice(offset + k * pad, offset + (k + 1) * pad)
                for source, target in ((hid, hid_s), (dg, dg_s), (du, du_s)):
                    target[to, :] = (source[part, :].astype(F32) * column).astype(BF)
            spans.append((xp, yp, slice(offset, offset + S * pad)))
            offset += S * pad

        def tile(i, carry):
            cols = at(i * 256, 256)
            x = jnp.concatenate([xp[:, cols] for xp, _, _ in spans], axis=0)
            y = jnp.concatenate([yp[:, cols] for _, yp, _ in spans], axis=0)
            outs[0][cols, :] = dot_tn(x, dg_s[...])
            outs[1][cols, :] = dot_tn(x, du_s[...])
            outs[2][:, cols] = dot_tn(hid_s[...], y)
            return carry

        lax.fori_loop(0, D // 256, tile, 0)

    total_rows = sum(S * (-(-len(c) * cap // 16) * 16) for c in chunks)
    grad_gate, grad_up, grad_down = run(
        expert_grad_body,
        [shaped((D, FF), F32), shaped((D, FF), F32), shaped((FF, D), F32)],
        stacked_gates + [a for rest in kept for a in rest],
        [pltpu.VMEM((total_rows, FF), BF)] * 3,
    )

    return (
        result[None],
        grad_inputs[None],
        grad_gain_one,
        grad_query,
        grad_key,
        grad_value,
        grad_qgain,
        grad_kgain,
        grad_out_w,
        grad_gain_two,
        grad_router,
        grad_gate[None],
        grad_up[None],
        grad_down[None],
    )


def solution(mesh):
    in_specs = (
        P("shard", "seq", None),
        P("shard", "seq"),
        P("shard", "seq", None),
        P("shard"),
        P("shard", None),
        P("shard", None),
        P("shard", None),
        P("shard"),
        P("shard"),
        P("shard", None),
        P("shard"),
        P("shard", None),
        P(("seq", "shard"), None, None),
        P(("seq", "shard"), None, None),
        P(("seq", "shard"), None, None),
        P("shard", "seq", None),
    )
    out_specs = (
        P("shard", "seq", None),
        P("shard", "seq", None),
        P("shard"),
        P("shard", None),
        P("shard", None),
        P("shard", None),
        P("shard"),
        P("shard"),
        P("shard", None),
        P("shard"),
        P("shard", None),
        P(("seq", "shard"), None, None),
        P(("seq", "shard"), None, None),
        P(("seq", "shard"), None, None),
    )
    return jax.shard_map(
        per_device, mesh=mesh, in_specs=in_specs, out_specs=out_specs, check_vma=False
    )
```

time: 925 us -> 844 us (0.912)
  Pallas kernels: 0 us -> 261 us
  matrix products: 174 us -> 0 us
  local copies, waits for them, and re-layouts: 172 us -> 39.8 us
  waiting for transfers between devices: 299 us -> 353 us
  other arithmetic: 83 us -> 41.2 us
  between operations: 42.2 us -> 2.73 us
    pallas_call x0 -> x34, Pallas kernels: none -> 261 us  [run(): pl.pallas_call(body, out_shape=list(outs), in_specs=specs, out_specs=[pl....]
    dot_general x82 -> x0, matrix products: 174 us -> none  [the longest x30 60.8 us: matmul(): return jnp.dot(a, b, preferred_element_type=F32)]
    ppermute x32, waiting for transfers between devices: 62.7 us -> 167 us  [forward(): return lax.ppermute(value, 'shard', self.up)]
    ppermute x68 -> x73, waiting for transfers between devices: 162 us -> 96.4 us  [swap(): return lax.ppermute(value, 'seq', [(i, i ^ bit) for i in range(count)])]
    dynamic_update_slice x32 -> x0, local copies, waits for them, and re-layouts: 46.2 us -> none  [the longest x8 14.9 us: per_device(): small = lax.dynamic_update_slice(small, flat, (ring.index[r], 0))]
    unnamed x546 -> x287, local copies, waits for them, and re-layouts: 58.6 us -> 20.4 us
    ppermute x1, waiting for transfers between devices: 0.01 us -> 31.8 us  [per_device(): piece = lax.ppermute(piece, ('seq', 'shard'), spread)]
    ppermute x32, starting transfers between devices: 15 us -> 45.5 us  [forward(): return lax.ppermute(value, 'shard', self.up)]
  transfers between devices with their start and end apart: 134 -> 139, of which waited for: 53 -> 47; matrix products, arithmetic and copies ran while one was open for 40% -> 5% of each run, Pallas kernels for 0% -> 29%
where the time goes in v2:
time: 844 us; the launch traced here: 834 us
  waiting for transfers between devices  353 us (42%)
  Pallas kernels  261 us (31%)
  starting transfers between devices  136 us (16%)
  other arithmetic  41.2 us (5%)
  local copies, waits for them, and re-layouts  39.8 us (5%)
    pallas_call x34, Pallas kernels, run(): pl.pallas_call(body, out_shape=list(outs), in_specs=specs, out_specs=[pl....  261 us
    ppermute x32, waiting for transfers between devices, forward(): return lax.ppermute(value, 'shard', self.up)  167 us
    ppermute x73, waiting for transfers between devices, swap(): return lax.ppermute(value, 'seq', [(i, i ^ bit) for i in range(count)])  96.4 us
    ppermute x73, starting transfers between devices, swap(): return lax.ppermute(value, 'seq', [(i, i ^ bit) for i in range(count)])  65.8 us
    ppermute x32, starting transfers between devices, forward(): return lax.ppermute(value, 'shard', self.up)  45.5 us
    ppermute x1, waiting for transfers between devices, per_device(): piece = lax.ppermute(piece, ('seq', 'shard'), spread)  31.8 us
    ppermute x32, waiting for transfers between devices, backward(): return lax.ppermute(value, 'shard', self.down)  30.1 us
    ppermute x1, waiting for transfers between devices, per_device(): lax.ppermute(out_sum[:PR], ('seq', 'shard'), [(b, a) for a, b in spread])  28.1 us
  transfers between devices with their start and end apart: 139, of which 47 were waited for; matrix products, arithmetic and copies ran while one was open for 5% of the time, Pallas kernels for 29%

profile of v2, /device:TPU:5, one launch (start us, length us, event | category | flops | bytes accessed | tf_op | source)
XLA Modules:
  0.0 834.3 jit_solution(11640435605642679999)
XLA Ops:
  13.0 15.3 %collective-permute-done.9.refs_18_.refs_10_ = bf16[272,1280]{1,0:T(8,128)(2,1)S(1)} collective-permute-done((bf16[272,1280]{1,0:T(8,128)(2,1)}, bf16[272,1280]{1,0:T(8,128)(2,1)S(1)}, u32[]{:S(2)}, u32[]{:S(2)}) %collective-permute-start.9) | collective-permute-done | bytes 696352 | tf_op jit(solution)/shard_map/ppermute | solution.py:54
  29.8 14.3 %collective-permute-done.10.refs_17_.refs_9_ = bf16[272,1280]{1,0:T(8,128)(2,1)S(1)} collective-permute-done((bf16[272,1280]{1,0:T(8,128)(2,1)S(1)}, bf16[272,1280]{1,0:T(8,128)(2,1)S(1)}, u32[]{:S(2)}, u32[]{:S(2)}) %collective-permute-start.10) | collective-permute-done | bytes 696352 | tf_op jit(solution)/shard_map/ppermute | solution.py:54
  45.5 13.3 %collective-permute-done.11.refs_16_.refs_8_ = bf16[272,1280]{1,0:T(8,128)(2,1)S(1)} collective-permute-done((bf16[272,1280]{1,0:T(8,128)(2,1)S(1)}, bf16[272,1280]{1,0:T(8,128)(2,1)S(1)}, u32[]{:S(2)}, u32[]{:S(2)}) %collective-permute-start.11) | collective-permute-done | bytes 696352 | tf_op jit(solution)/shard_map/ppermute | solution.py:54
  61.4 7.9 collective-permute-start.14
  69.4 31.8 %collective-permute-done.14.refs_2_.refs_5_ = bf16[128,2048]{1,0:T(8,128)(2,1)S(1)} collective-permute-done((bf16[128,2048]{1,0:T(8,128)(2,1)S(1)}, bf16[128,2048]{1,0:T(8,128)(2,1)S(1)}, u32[]{:S(2)}, u32[]{:S(2)}) %collective-permute-start.14) | collective-permute-done | bytes 524320 | tf_op jit(solution)/shard_map/ppermute | solution.py:320
  118.1 10.1 %collective-permute-done.19.refs_8_.refs_11_ = bf16[128,2048]{1,0:T(8,128)(2,1)S(1)} collective-permute-done((bf16[128,2048]{1,0:T(8,128)(2,1)S(1)}, bf16[128,2048]{1,0:T(8,128)(2,1)S(1)}, u32[]{:S(2)}, u32[]{:S(2)}) %collective-permute-start.19) | collective-permute-done | bytes 524320 | tf_op jit(solution)/shard_map/ppermute | solution.py:54
  132.3 7.9 collective-permute-done.20.refs_7_.refs_10_
  150.1 22.4 %shard_map.282 = (bf16[512,2048]{1,0:T(8,128)(2,1)}, f32[512,1280]{1,0:T(8,128)}, bf16[512,1024]{1,0:T(8,128)(2,1)}, bf16[512,128]{1,0:T(8,128)(2,1)}, bf16[512,...) custom-call(s32[17]{0:T(128)} %pad_add_fusion.m.refs_0_, ...), custom_call_target="tpu_custom_call" | custom-call | flops 1048576 | bytes 65536 | tf_op jit(solution)/shard_map/pallas_call | solution.py:146
  175.3 8.3 shard_map.283
  193.2 7.6 collective-permute-done.45.refs_1_
  258.7 12.5 %shard_map.288 = (bf16[40,2176]{1,0:T(8,128)(2,1)}, bf16[40,2176]{1,0:T(8,128)(2,1)}, bf16[40,2176]{1,0:T(8,128)(2,1)}, bf16[40,2176]{1,0:T(8,128)(2,1)}, bf16[4...) custom-call(s32[17]{0:T(128)} %pad_add_fusion.m.refs_0_, ...), custom_call_target="tpu_custom_call" | custom-call | flops 1048576 | bytes 65536 | tf_op jit(solution)/shard_map/pallas_call | solution.py:146
  302.1 7.9 collective-permute-done.44.refs_4_
  311.2 15.0 %shard_map.292 = (bf16[80,2176]{1,0:T(8,128)(2,1)}, bf16[80,2176]{1,0:T(8,128)(2,1)}, bf16[80,2176]{1,0:T(8,128)(2,1)}, bf16[80,2176]{1,0:T(8,128)(2,1)}, bf16[8...) custom-call(s32[17]{0:T(128)} %pad_add_fusion.m.refs_0_, ...), custom_call_target="tpu_custom_call" | custom-call | flops 1048576 | bytes 65536 | tf_op jit(solution)/shard_map/pallas_call | solution.py:146
  335.0 15.1 %shard_map.296 = (bf16[80,2176]{1,0:T(8,128)(2,1)}, bf16[80,2176]{1,0:T(8,128)(2,1)}, bf16[80,2176]{1,0:T(8,128)(2,1)}, bf16[80,2176]{1,0:T(8,128)(2,1)}, bf16[8...) custom-call(s32[17]{0:T(128)} %pad_add_fusion.m.refs_0_, ...), custom_call_target="tpu_custom_call" | custom-call | flops 1048576 | bytes 65536 | tf_op jit(solution)/shard_map/pallas_call | solution.py:146
  354.2 7.6 shard_map.285
  426.9 8.2 collective-permute-done.138
  437.7 20.5 %shard_map.300 = (bf16[120,2176]{1,0:T(8,128)(2,1)}, bf16[120,2176]{1,0:T(8,128)(2,1)}, bf16[120,2176]{1,0:T(8,128)(2,1)}, bf16[120,2176]{1,0:T(8,128)(2,1)}, bf...) custom-call(s32[17]{0:T(128)} %pad_add_fusion.m.refs_0_, ...), custom_call_target="tpu_custom_call" | custom-call | flops 1048576 | bytes 65536 | tf_op jit(solution)/shard_map/pallas_call | solution.py:146
  462.1 9.6 %collective-permute-done.81.refs_4_ = bf16[120,2176]{1,0:T(8,128)(2,1)S(1)} collective-permute-done((bf16[120,2176]{1,0:T(8,128)(2,1)}, bf16[120,2176]{1,0:T(8,128)(2,1)S(1)}, u32[]{:S(2)}, u32[]{:S(2)}) %collective-permute-start.81) | collective-permute-done | bytes 522272 | tf_op jit(solution)/shard_map/ppermute | solution.py:95
  471.7 11.7 %collective-permute-done.82.refs_5_ = bf16[120,2176]{1,0:T(8,128)(2,1)S(1)} collective-permute-done((bf16[120,2176]{1,0:T(8,128)(2,1)}, bf16[120,2176]{1,0:T(8,128)(2,1)S(1)}, u32[]{:S(2)}, u32[]{:S(2)}) %collective-permute-start.82) | collective-permute-done | bytes 522272 | tf_op jit(solution)/shard_map/ppermute | solution.py:95
  504.2 8.2 collective-permute-done.84
  573.8 28.9 %shard_map.307 = (bf16[512,1024]{1,0:T(8,128)(2,1)}, bf16[512,128]{1,0:T(8,128)(2,1)}, bf16[512,128]{1,0:T(8,128)(2,1)}, f32[8,128]{1,0:T(8,128)}) custom-call(s32[17]{0:T(128)} %pad_add_fusion.m.refs_0_, bf16[128,2048]{1,0:T(8,128)(2,1)} %get-tuple-element.257.refs_1_.refs_2_, bf16[128,2048]{1,0:T(8,128)(2,1)} %copy-done.31, bf16[128,2048]{1,0:T(8,128)(2,1)} %copy-done.30, ...), custom_call_target="tpu_custom_call" | custom-call | flops 1048576 | bytes 65536 | tf_op jit(solution)/shard_map/pallas_call | solution.py:146
  602.7 8.3 %shard_map.308 = (f32[264,1280]{1,0:T(8,128)}, f32[264,1280]{1,0:T(8,128)}, f32[264,1280]{1,0:T(8,128)}, f32[264,1280]{1,0:T(8,128)}, f32[264,1280]{1,0:T(8,128)...) custom-call(s32[17]{0:T(128)} %pad_add_fusion.m.refs_0_, ...), custom_call_target="tpu_custom_call" | custom-call | flops 1048576 | bytes 65536 | tf_op jit(solution)/shard_map/pallas_call | solution.py:146
  612.5 7.8 shard_map.312
  621.7 9.3 %shard_map.309 = f32[512,2048]{1,0:T(8,128)} custom-call(s32[17]{0:T(128)} %pad_add_fusion.m.refs_0_, bf16[512,1024]{1,0:T(8,128)(2,1)} %get-tuple-element.264.dq.refs_1_, bf16[512,256]{1,0:T(8,128)(2,1)} %get-tuple-element.269.refs_2_, bf16[272,1280]{1,0:T(8,128)(2,1)} %shard_map.281.refs_11_.refs_3_, bf16[272,1280]{1,0:T(8,128)(2,1)} %copy-done.16, ...), custom_call_target="tpu_custom_call" | custom-call | flops 1048576 | bytes 65536 | tf_op jit(solution)/shard_map/pallas_call | solution.py:146
  640.5 10.6 %collective-permute-done.121 = bf16[64,2048]{1,0:T(8,128)(2,1)S(1)} collective-permute-done((bf16[64,2048]{1,0:T(8,128)(2,1)S(1)}, bf16[64,2048]{1,0:T(8,128)(2,1)S(1)}, u32[]{:S(2)}, u32[]{:S(2)}) %collective-permute-start.121) | collective-permute-done | bytes 262176 | tf_op jit(solution)/shard_map/ppermute | solution.py:54
  660.9 9.5 %collective-permute-done.122 = bf16[136,2048]{1,0:T(8,128)(2,1)S(1)} collective-permute-done((bf16[136,2048]{1,0:T(8,128)(2,1)S(1)}, bf16[136,2048]{1,0:T(8,128)(2,1)S(1)}, u32[]{:S(2)}, u32[]{:S(2)}) %collective-permute-start.122) | collective-permute-done | bytes 557088 | tf_op jit(solution)/shard_map/ppermute | solution.py:54
  672.4 12.4 %collective-permute-done.111 = bf16[264,1280]{1,0:T(8,128)(2,1)S(1)} collective-permute-done((bf16[264,1280]{1,0:T(8,128)(2,1)S(1)}, bf16[264,1280]{1,0:T(8,128)(2,1)S(1)}, u32[]{:S(2)}, u32[]{:S(2)}) %collective-permute-start.111) | collective-permute-done | bytes 675872 | tf_op jit(solution)/shard_map/ppermute | solution.py:54
  686.9 9.9 %collective-permute-done.123 = bf16[136,2048]{1,0:T(8,128)(2,1)S(1)} collective-permute-done((bf16[136,2048]{1,0:T(8,128)(2,1)S(1)}, bf16[136,2048]{1,0:T(8,128)(2,1)S(1)}, u32[]{:S(2)}, u32[]{:S(2)}) %collective-permute-start.123) | collective-permute-done | bytes 557088 | tf_op jit(solution)/shard_map/ppermute | solution.py:54
  698.6 12.7 %collective-permute-done.112 = bf16[264,1280]{1,0:T(8,128)(2,1)S(1)} collective-permute-done((bf16[264,1280]{1,0:T(8,128)(2,1)S(1)}, bf16[264,1280]{1,0:T(8,128)(2,1)S(1)}, u32[]{:S(2)}, u32[]{:S(2)}) %collective-permute-start.112) | collective-permute-done | bytes 675872 | tf_op jit(solution)/shard_map/ppermute | solution.py:54
  725.0 12.7 %collective-permute-done.113 = bf16[264,1280]{1,0:T(8,128)(2,1)S(1)} collective-permute-done((bf16[264,1280]{1,0:T(8,128)(2,1)S(1)}, bf16[264,1280]{1,0:T(8,128)(2,1)S(1)}, u32[]{:S(2)}, u32[]{:S(2)}) %collective-permute-start.113) | collective-permute-done | bytes 675872 | tf_op jit(solution)/shard_map/ppermute | solution.py:54
  746.3 28.1 %collective-permute-done.129.refs_1_ = bf16[128,2048]{1,0:T(8,128)(2,1)} collective-permute-done((bf16[128,2048]{1,0:T(8,128)(2,1)S(1)}, bf16[128,2048]{1,0:T(8,128)(2,1)}, u32[]{:S(2)}, u32[]{:S(2)}) %collective-permute-start.129) | collective-permute-done | bytes 524320 | tf_op jit(solution)/shard_map/ppermute | solution.py:734
  781.9 29.2 %shard_map.314 = (f32[2048,768]{1,0:T(8,128)}, f32[2048,768]{1,0:T(8,128)}, f32[768,2048]{1,0:T(8,128)}) custom-call(f32[4,40]{1,0:T(4,128)} %pad_maximum_fusion.5.refs_0_, f32[4,80]{1,0:T(4,128)} %pad_maximum_fusion.6.refs_1_, f32[4,80]{1,0:T(4,128)} %pad_maximum_fusion.7.refs_2_, f32[4,120]{1,0:T(4,128)} %pad_maximum_fusion.12.refs_3_, ...), custom_call_target="tpu_custom_call" | custom-call | flops 1048576 | bytes 65536 | tf_op jit(solution)/shard_map/pallas_call | solution.py:146
  (685 shorter events, 396.9 us)
Async XLA Ops:
  61.4 39.7 %collective-permute-start.14 = (bf16[128,2048]{1,0:T(8,128)(2,1)S(1)}, bf16[128,2048]{1,0:T(8,128)(2,1)S(1)}, u32[]{:S(2)}, u32[]{:S(2)}) collective-permute-start(bf16[128,2048]{1,0:T(8,128)(2,1)S(1)} %constant_dynamic-slice_fusion.2), channel_id=1, source_target_pairs={{0,0},{8,1},{16,2},{24,3},{1,4},{9,5},{17,6},{25,7},{2,8},{10,9},{... | collective-permute-start | bytes 1572872 | tf_op jit(solution)/shard_map/ppermute | solution.py:320
  142.5 30.0 %collective-permute-start.21 = (bf16[64,2048]{1,0:T(8,128)(2,1)S(1)}, bf16[64,2048]{1,0:T(8,128)(2,1)}, u32[]{:S(2)}, u32[]{:S(2)}) collective-permute-start(bf16[64,2048]{1,0:T(8,128)(2,1)S(1)} %slice.349), channel_id=1, source_target_pairs={{0,2},{2,4},{4,6},{6,7},{7,5},{5,3},{3,1},{1,0},{8,10},{10,12},{12... | collective-permute-start | bytes 786440 | tf_op jit(solution)/shard_map/ppermute | solution.py:54
  217.3 26.9 %collective-permute-start.67 = (bf16[128,2048]{1,0:T(8,128)(2,1)S(1)}, bf16[128,2048]{1,0:T(8,128)(2,1)S(1)}, u32[]{:S(2)}, u32[]{:S(2)}) collective-permute-start(bf16[128,2048]{1,0:T(8,128)(2,1)S(1)} %collective-permute-done.56.refs_1_), channel_id=1, source_target_pairs={{2,0},{4,2},{6,4},{7,6},{5,7},{3,5},{1,3},{0,1},{10,8},{12,10},{14... | collective-permute-start | bytes 1572872 | tf_op jit(solution)/shard_map/ppermute | solution.py:57
  217.3 27.3 %collective-permute-start.68 = (bf16[128,2048]{1,0:T(8,128)(2,1)S(1)}, bf16[128,2048]{1,0:T(8,128)(2,1)S(1)}, u32[]{:S(2)}, u32[]{:S(2)}) collective-permute-start(bf16[128,2048]{1,0:T(8,128)(2,1)S(1)} %collective-permute-done.57.refs_2_), channel_id=1, source_target_pairs={{0,2},{2,4},{4,6},{6,7},{7,5},{5,3},{3,1},{1,0},{8,10},{10,12},{12... | collective-permute-start | bytes 1572872 | tf_op jit(solution)/shard_map/ppermute | solution.py:54
  236.6 37.2 %collective-permute-start.28 = (bf16[128,2048]{1,0:T(8,128)(2,1)}, bf16[128,2048]{1,0:T(8,128)(2,1)S(1)}, u32[]{:S(2)}, u32[]{:S(2)}) collective-permute-start(bf16[128,2048]{1,0:T(8,128)(2,1)} %get-tuple-element.172.refs_1_.hidden), channel_id=1, source_target_pairs={{0,2},{2,4},{4,6},{6,7},{7,5},{5,3},{3,1},{1,0},{8,10},{10,12},{12... | collective-permute-start | bytes 1572872 | tf_op jit(solution)/shard_map/ppermute | solution.py:54
  237.8 33.5 %collective-permute-start.60 = (bf16[80,2048]{1,0:T(8,128)(2,1)}, bf16[80,2048]{1,0:T(8,128)(2,1)}, u32[]{:S(2)}, u32[]{:S(2)}) collective-permute-start(bf16[80,2048]{1,0:T(8,128)(2,1)} %get-tuple-element.209), channel_id=1, source_target_pairs={{0,24},{8,16},{16,8},{24,0},{1,25},{9,17},{17,9},{25,1},{2,26},{10... | collective-permute-start | bytes 983048 | tf_op jit(solution)/shard_map/ppermute | solution.py:95
  245.9 35.4 %collective-permute-start.25 = (bf16[128,2048]{1,0:T(8,128)(2,1)}, bf16[128,2048]{1,0:T(8,128)(2,1)S(1)}, u32[]{:S(2)}, u32[]{:S(2)}) collective-permute-start(bf16[128,2048]{1,0:T(8,128)(2,1)} %get-tuple-element.172.refs_1_.hidden), channel_id=1, source_target_pairs={{2,0},{4,2},{6,4},{7,6},{5,7},{3,5},{1,3},{0,1},{10,8},{12,10},{14... | collective-permute-start | bytes 1572872 | tf_op jit(solution)/shard_map/ppermute | solution.py:57
  292.6 34.4 %collective-permute-start.30 = (bf16[128,2048]{1,0:T(8,128)(2,1)S(1)}, bf16[128,2048]{1,0:T(8,128)(2,1)S(1)}, u32[]{:S(2)}, u32[]{:S(2)}) collective-permute-start(bf16[128,2048]{1,0:T(8,128)(2,1)S(1)} %collective-permute-done.29.refs_7_.refs_2_), channel_id=1, source_target_pairs={{0,2},{2,4},{4,6},{6,7},{7,5},{5,3},{3,1},{1,0},{8,10},{10,12},{12... | collective-permute-start | bytes 1572872 | tf_op jit(solution)/shard_map/ppermute | solution.py:54
  296.0 31.9 %collective-permute-start.27 = (bf16[128,2048]{1,0:T(8,128)(2,1)S(1)}, bf16[128,2048]{1,0:T(8,128)(2,1)S(1)}, u32[]{:S(2)}, u32[]{:S(2)}) collective-permute-start(bf16[128,2048]{1,0:T(8,128)(2,1)S(1)} %collective-permute-done.26.refs_3_.refs_1_), channel_id=1, source_target_pairs={{2,0},{4,2},{6,4},{7,6},{5,7},{3,5},{1,3},{0,1},{10,8},{12,10},{14... | collective-permute-start | bytes 1572872 | tf_op jit(solution)/shard_map/ppermute | solution.py:57
  310.0 40.2 %collective-permute-start.72 = (bf16[120,2048]{1,0:T(8,128)(2,1)}, bf16[120,2048]{1,0:T(8,128)(2,1)S(1)}, u32[]{:S(2)}, u32[]{:S(2)}) collective-permute-start(bf16[120,2048]{1,0:T(8,128)(2,1)} %get-tuple-element.221), channel_id=1, source_target_pairs={{0,16},{8,24},{16,0},{24,8},{1,17},{9,25},{17,1},{25,9},{2,18},{10... | collective-permute-start | bytes 1474568 | tf_op jit(solution)/shard_map/ppermute | solution.py:95
  353.3 26.8 %collective-permute-start.61 = (bf16[80,2048]{1,0:T(8,128)(2,1)}, bf16[80,2048]{1,0:T(8,128)(2,1)}, u32[]{:S(2)}, u32[]{:S(2)}) collective-permute-start(bf16[80,2048]{1,0:T(8,128)(2,1)} %get-tuple-element.211), channel_id=1, source_target_pairs={{0,8},{8,0},{16,24},{24,16},{1,9},{9,1},{17,25},{25,17},{2,10},{10... | collective-permute-start | bytes 983048 | tf_op jit(solution)/shard_map/ppermute | solution.py:95
  363.4 26.1 %collective-permute-start.63 = (bf16[80,2048]{1,0:T(8,128)(2,1)}, bf16[80,2048]{1,0:T(8,128)(2,1)S(1)}, u32[]{:S(2)}, u32[]{:S(2)}) collective-permute-start(bf16[80,2048]{1,0:T(8,128)(2,1)} %get-tuple-element.213), channel_id=1, source_target_pairs={{0,24},{8,16},{16,8},{24,0},{1,25},{9,17},{17,9},{25,1},{2,26},{10... | collective-permute-start | bytes 983048 | tf_op jit(solution)/shard_map/ppermute | solution.py:95
  382.7 53.3 %collective-permute-start.73 = (bf16[120,2048]{1,0:T(8,128)(2,1)}, bf16[120,2048]{1,0:T(8,128)(2,1)S(1)}, u32[]{:S(2)}, u32[]{:S(2)}) collective-permute-start(bf16[120,2048]{1,0:T(8,128)(2,1)} %get-tuple-element.222), channel_id=1, source_target_pairs={{0,24},{8,16},{16,8},{24,0},{1,25},{9,17},{17,9},{25,1},{2,26},{10... | collective-permute-start | bytes 1474568 | tf_op jit(solution)/shard_map/ppermute | solution.py:95
  390.2 46.4 %collective-permute-start.64 = (bf16[120,2048]{1,0:T(8,128)(2,1)}, bf16[120,2048]{1,0:T(8,128)(2,1)S(1)}, u32[]{:S(2)}, u32[]{:S(2)}) collective-permute-start(bf16[120,2048]{1,0:T(8,128)(2,1)} %get-tuple-element.216), channel_id=1, source_target_pairs={{0,8},{8,0},{16,24},{24,16},{1,9},{9,1},{17,25},{25,17},{2,10},{10... | collective-permute-start | bytes 1474568 | tf_op jit(solution)/shard_map/ppermute | solution.py:95
  390.2 46.4 %collective-permute-start.65 = (bf16[120,2048]{1,0:T(8,128)(2,1)}, bf16[120,2048]{1,0:T(8,128)(2,1)S(1)}, u32[]{:S(2)}, u32[]{:S(2)}) collective-permute-start(bf16[120,2048]{1,0:T(8,128)(2,1)} %get-tuple-element.217), channel_id=1, source_target_pairs={{0,16},{8,24},{16,0},{24,8},{1,17},{9,25},{17,1},{25,9},{2,18},{10... | collective-permute-start | bytes 1474568 | tf_op jit(solution)/shard_map/ppermute | solution.py:95
  396.0 40.6 %collective-permute-start.66 = (bf16[120,2048]{1,0:T(8,128)(2,1)}, bf16[120,2048]{1,0:T(8,128)(2,1)S(1)}, u32[]{:S(2)}, u32[]{:S(2)}) collective-permute-start(bf16[120,2048]{1,0:T(8,128)(2,1)} %get-tuple-element.218), channel_id=1, source_target_pairs={{0,24},{8,16},{16,8},{24,0},{1,25},{9,17},{17,9},{25,1},{2,26},{10... | collective-permute-start | bytes 1474568 | tf_op jit(solution)/shard_map/ppermute | solution.py:95
  404.6 30.4 %collective-permute-start.138 = (f32[8,40]{1,0:T(8,128)S(1)}, f32[8,40]{1,0:T(8,128)S(1)}, u32[]{:S(2)}, u32[]{:S(2)}) collective-permute-start(f32[8,40]{1,0:T(8,128)S(1)} %get-tuple-element.345), channel_id=1, source_target_pairs={{0,24},{8,16},{16,8},{24,0},{1,25},{9,17},{17,9},{25,1},{2,26},{10... | collective-permute-start | bytes 3848 | tf_op jit(solution)/shard_map/ppermute | solution.py:95
  493.4 43.5 %collective-permute-start.87 = (bf16[120,2048]{1,0:T(8,128)(2,1)S(1)}, bf16[120,2048]{1,0:T(8,128)(2,1)S(1)}, u32[]{:S(2)}, u32[]{:S(2)}) collective-permute-start(bf16[120,2048]{1,0:T(8,128)(2,1)S(1)} %copy-done.139), channel_id=1, source_target_pairs={{0,8},{8,0},{16,24},{24,16},{1,9},{9,1},{17,25},{25,17},{2,10},{10... | collective-permute-start | bytes 1474568 | tf_op jit(solution)/shard_map/ppermute | solution.py:95
  493.6 43.3 %collective-permute-start.88 = (bf16[120,2048]{1,0:T(8,128)(2,1)S(1)}, bf16[120,2048]{1,0:T(8,128)(2,1)S(1)}, u32[]{:S(2)}, u32[]{:S(2)}) collective-permute-start(bf16[120,2048]{1,0:T(8,128)(2,1)S(1)} %copy-done.138), channel_id=1, source_target_pairs={{0,16},{8,24},{16,0},{24,8},{1,17},{9,25},{17,1},{25,9},{2,18},{10... | collective-permute-start | bytes 1474568 | tf_op jit(solution)/shard_map/ppermute | solution.py:95
  494.8 42.1 %collective-permute-start.89 = (bf16[120,2048]{1,0:T(8,128)(2,1)S(1)}, bf16[120,2048]{1,0:T(8,128)(2,1)S(1)}, u32[]{:S(2)}, u32[]{:S(2)}) collective-permute-start(bf16[120,2048]{1,0:T(8,128)(2,1)S(1)} %copy-done.137), channel_id=1, source_target_pairs={{0,24},{8,16},{16,8},{24,0},{1,25},{9,17},{17,9},{25,1},{2,26},{10... | collective-permute-start | bytes 1474568 | tf_op jit(solution)/shard_map/ppermute | solution.py:95
  569.4 67.6 %collective-permute-start.96 = (bf16[128,2048]{1,0:T(8,128)(2,1)}, bf16[128,2048]{1,0:T(8,128)(2,1)}, u32[]{:S(2)}, u32[]{:S(2)}) collective-permute-start(bf16[128,2048]{1,0:T(8,128)(2,1)} %add_convert_fusion.22), channel_id=1, source_target_pairs={{2,0},{4,2},{6,4},{7,6},{5,7},{3,5},{1,3},{0,1},{10,8},{12,10},{14... | collective-permute-start | bytes 1572872 | tf_op jit(solution)/shard_map/ppermute | solution.py:57
  571.4 142.3 %collective-permute-start.92 = (bf16[128,2048]{1,0:T(8,128)(2,1)}, bf16[128,2048]{1,0:T(8,128)(2,1)S(1)}, u32[]{:S(2)}, u32[]{:S(2)}) collective-permute-start(bf16[128,2048]{1,0:T(8,128)(2,1)} %add_convert_fusion.25), channel_id=1, source_target_pairs={{0,2},{2,4},{4,6},{6,7},{7,5},{5,3},{3,1},{1,0},{8,10},{10,12},{12... | collective-permute-start | bytes 1572872 | tf_op jit(solution)/shard_map/ppermute | solution.py:54
  633.7 111.1 %collective-permute-start.108 = (bf16[256,2048]{1,0:T(8,128)(2,1)S(1)}, bf16[256,2048]{1,0:T(8,128)(2,1)S(1)}, u32[]{:S(2)}, u32[]{:S(2)}) collective-permute-start(bf16[256,2048]{1,0:T(8,128)(2,1)S(1)} %pad_maximum_fusion.1), channel_id=1, source_target_pairs={{0,8},{8,0},{16,24},{24,16},{1,9},{9,1},{17,25},{25,17},{2,10},{10... | collective-permute-start | bytes 3145736 | tf_op jit(solution)/shard_map/ppermute | solution.py:95
  713.6 27.7 %collective-permute-start.117 = (bf16[264,1280]{1,0:T(8,128)(2,1)S(1)}, bf16[264,1280]{1,0:T(8,128)(2,1)S(1)}, u32[]{:S(2)}, u32[]{:S(2)}) collective-permute-start(bf16[264,1280]{1,0:T(8,128)(2,1)S(1)} %add_convert_fusion.1), channel_id=1, source_target_pairs={{2,0},{4,2},{6,4},{7,6},{5,7},{3,5},{1,3},{0,1},{10,8},{12,10},{14... | collective-permute-start | bytes 2027528 | tf_op jit(solution)/shard_map/ppermute | solution.py:57
  723.2 53.1 %collective-permute-start.97 = (bf16[128,2048]{1,0:T(8,128)(2,1)}, bf16[128,2048]{1,0:T(8,128)(2,1)}, u32[]{:S(2)}, u32[]{:S(2)}) collective-permute-start(bf16[128,2048]{1,0:T(8,128)(2,1)} %add_convert_fusion.21), channel_id=1, source_target_pairs={{2,0},{4,2},{6,4},{7,6},{5,7},{3,5},{1,3},{0,1},{10,8},{12,10},{14... | collective-permute-start | bytes 1572872 | tf_op jit(solution)/shard_map/ppermute | solution.py:57
  723.8 55.8 %collective-permute-start.93 = (bf16[128,2048]{1,0:T(8,128)(2,1)}, bf16[128,2048]{1,0:T(8,128)(2,1)}, u32[]{:S(2)}, u32[]{:S(2)}) collective-permute-start(bf16[128,2048]{1,0:T(8,128)(2,1)} %add_convert_fusion.24), channel_id=1, source_target_pairs={{0,2},{2,4},{4,6},{6,7},{7,5},{5,3},{3,1},{1,0},{8,10},{10,12},{12... | collective-permute-start | bytes 1572872 | tf_op jit(solution)/shard_map/ppermute | solution.py:54
  737.7 36.7 %collective-permute-start.129 = (bf16[128,2048]{1,0:T(8,128)(2,1)S(1)}, bf16[128,2048]{1,0:T(8,128)(2,1)}, u32[]{:S(2)}, u32[]{:S(2)}) collective-permute-start(bf16[128,2048]{1,0:T(8,128)(2,1)S(1)} %slice.375), channel_id=1, source_target_pairs={{0,0},{1,8},{2,16},{3,24},{4,1},{5,9},{6,17},{7,25},{8,2},{9,10},{... | collective-permute-start | bytes 1572872 | tf_op jit(solution)/shard_map/ppermute | solution.py:734
  741.8 70.6 %collective-permute-start.119 = (bf16[264,1280]{1,0:T(8,128)(2,1)S(1)}, bf16[264,1280]{1,0:T(8,128)(2,1)S(1)}, u32[]{:S(2)}, u32[]{:S(2)}) collective-permute-start(bf16[264,1280]{1,0:T(8,128)(2,1)S(1)} %add_convert_fusion.refs_1_), channel_id=1, source_target_pairs={{0,16},{8,24},{16,0},{24,8},{1,17},{9,25},{17,1},{25,9},{2,18},{10... | collective-permute-start | bytes 2027528 | tf_op jit(solution)/shard_map/ppermute | solution.py:95
  746.3 65.4 %collective-permute-start.109 = (bf16[128,2048]{1,0:T(8,128)(2,1)}, bf16[128,2048]{1,0:T(8,128)(2,1)}, u32[]{:S(2)}, u32[]{:S(2)}) collective-permute-start(bf16[128,2048]{1,0:T(8,128)(2,1)} %get-tuple-element.320), channel_id=1, source_target_pairs={{0,16},{8,24},{16,0},{24,8},{1,17},{9,25},{17,1},{25,9},{2,18},{10... | collective-permute-start | bytes 1572872 | tf_op jit(solution)/shard_map/ppermute | solution.py:95
  774.4 37.7 %collective-permute-start.131 = (bf16[128,2048]{1,0:T(8,128)(2,1)}, bf16[128,2048]{1,0:T(8,128)(2,1)}, u32[]{:S(2)}, u32[]{:S(2)}) collective-permute-start(bf16[128,2048]{1,0:T(8,128)(2,1)} %collective-permute-done.129.refs_1_), channel_id=1, source_target_pairs={{0,16},{8,24},{16,0},{24,8},{1,17},{9,25},{17,1},{25,9},{2,18},{10... | collective-permute-start | bytes 1572872 | tf_op jit(solution)/shard_map/ppermute | solution.py:95
  776.4 35.5 %collective-permute-start.133 = (bf16[8,2048]{1,0:T(8,128)(2,1)S(1)}, bf16[8,2048]{1,0:T(8,128)(2,1)S(1)}, u32[]{:S(2)}, u32[]{:S(2)}) collective-permute-start(bf16[8,2048]{1,0:T(8,128)(2,1)S(1)} %slice.376.refs_5_), channel_id=1, source_target_pairs={{0,8},{8,0},{16,24},{24,16},{1,9},{9,1},{17,25},{25,17},{2,10},{10... | collective-permute-start | bytes 98312 | tf_op jit(solution)/shard_map/ppermute | solution.py:95
  779.6 31.6 %collective-permute-start.134 = (bf16[8,2048]{1,0:T(8,128)(2,1)S(1)}, bf16[8,2048]{1,0:T(8,128)(2,1)S(1)}, u32[]{:S(2)}, u32[]{:S(2)}) collective-permute-start(bf16[8,2048]{1,0:T(8,128)(2,1)S(1)} %slice.376.refs_5_), channel_id=1, source_target_pairs={{0,16},{8,24},{16,0},{24,8},{1,17},{9,25},{17,1},{25,9},{2,18},{10... | collective-permute-start | bytes 98312 | tf_op jit(solution)/shard_map/ppermute | solution.py:95
  (249 other events, 3524.3 us)

commit v3 on v2

v3 whole, which is shorter than its diff:
```python
import jax
import jax.numpy as jnp
import numpy as np
from jax import lax
from jax.experimental import pallas as pl
from jax.experimental.pallas import tpu as pltpu
from jax.sharding import PartitionSpec as P

HQ = 32
KEY_VALUE_HEADS = 4
HEAD_DIMENSION = 128
TOPK = 8

EPSILON = 1e-06
ROPE_BASE = 1000000.0
NEGATIVE = -1e30
EXACT = lax.Precision.HIGHEST
BF = jnp.bfloat16
F32 = jnp.float32
I32 = jnp.int32


def ring_order(count):
    width = 4 if count >= 16 else 2
    if count % width or count // width < 2:
        return list(range(count))
    depth = count // width
    order = [z * width for z in range(depth)]
    for turn, z in enumerate(reversed(range(depth))):
        columns = range(1, width) if turn % 2 == 0 else range(width - 1, 0, -1)
        order += [z * width + y for y in columns]
    return order


class Ring:
    def __init__(self, count):
        self.n = count
        self.half = count // 2
        self.order = ring_order(count)
        place = [0] * count
        for i, d in enumerate(self.order):
            place[d] = i
        self.up = [(self.order[i], self.order[(i + 1) % count]) for i in range(count)]
        self.down = [(b, a) for a, b in self.up]
        seats = jnp.arange(count, dtype=I32)
        mine = seats == lax.axis_index("shard")
        me = jnp.sum(jnp.where(mine, jnp.asarray(place, I32), 0))
        ahead = (me + seats) % count
        table = jnp.asarray(self.order, I32)
        self.index = jnp.sum(
            jnp.where(ahead[:, None] == seats[None, :], table[None, :], 0), axis=1
        )

    def forward(self, value):
        return lax.ppermute(value, "shard", self.up)

    def backward(self, value):
        return lax.ppermute(value, "shard", self.down)


def halfway(rows):
    return rows // 2 // 16 * 16


class Gather:
    def __init__(self, ring, chain, value):
        self.ring, self.chain = ring, chain
        n = ring.n
        self.cut = halfway(value.shape[0])
        self.blocks = [None] * n
        self.blocks[0] = [value]
        self.done = 1
        self.blocks[n - 1] = [ring.forward(value)]
        self.blocks[1] = [ring.backward(value)]

    def step(self):
        ring, n, j = self.ring, self.ring.n, self.done
        a, b = self.chain.gate(self.blocks[n - j][0], self.blocks[j][0])
        self.blocks[n - j], self.blocks[j] = [a], [b]
        self.done = j + 1
        if j + 1 < ring.half:
            self.blocks[n - j - 1] = [ring.forward(a)]
            self.blocks[j + 1] = [ring.backward(b)]
        else:
            self.blocks[ring.half] = [
                ring.forward(a[: self.cut]),
                ring.backward(b[self.cut :]),
            ]

    def arrive(self):
        n, j = self.ring.n, self.done
        a, b = self.chain.gate(self.blocks[n - j][0], self.blocks[j][0])
        self.blocks[n - j], self.blocks[j] = [a], [b]

    def finish(self):
        self.blocks[self.ring.half] = list(self.chain.gate(*self.blocks[self.ring.half]))


class Reduce:
    def __init__(self, ring, chain, top, bottom):
        self.ring, self.chain = ring, chain
        self.cut = top.shape[0]
        self.left = ring.half - 1
        self.ahead, self.behind = ring.forward(top), ring.backward(bottom)

    def step(self, part_ahead, part_behind):
        first = self.left == self.ring.half - 1
        cut = self.cut

        def body(a_ref, a_in, b_ref, b_in, a_out, b_out):
            if first:
                a_out[:cut, :] = (a_ref[:cut, :] + a_in[...].astype(F32)).astype(BF)
                a_out[cut:, :] = a_ref[cut:, :].astype(BF)
                b_out[:cut, :] = b_ref[:cut, :].astype(BF)
                b_out[cut:, :] = (b_ref[cut:, :] + b_in[...].astype(F32)).astype(BF)
            else:
                a_out[...] = (a_ref[...] + a_in[...].astype(F32)).astype(BF)
                b_out[...] = (b_ref[...] + b_in[...].astype(F32)).astype(BF)

        shape = shaped(part_ahead.shape, BF)
        a, b = self.chain.run(
            body, [shape, shape], [part_ahead, self.ahead, part_behind, self.behind]
        )
        self.left -= 1
        self.ahead, self.behind = self.ring.forward(a), self.ring.backward(b)


def swap(value, bit, count):
    return lax.ppermute(value, "seq", [(i, i ^ bit) for i in range(count)])


def seq_gather(chain, value, count):
    have = {0: value}
    bit = count // 2
    while bit:
        for k in sorted(have):
            if k:
                (have[k],) = chain.gate(have[k])
            have[k ^ bit] = swap(have[k], bit, count)
        bit //= 2
    return [have[k] for k in range(count)]


def tree_sum(values):
    values = list(values)
    while len(values) > 1:
        values = [values[i] + values[i + 1] for i in range(0, len(values), 2)]
    return values[0]


def shaped(shape, dtype):
    return jax.ShapeDtypeStruct(tuple(shape), dtype)


class Chain:
    def __init__(self):
        self.token = jnp.zeros((8, 128), F32)

    def gate(self, *arrays):
        *arrays, self.token = lax.optimization_barrier(tuple(arrays) + (self.token,))
        return arrays

    def run(self, body, outs, operands, scratch=()):
        spaces = {"s": pltpu.SMEM, "a": pl.ANY, "v": pltpu.VMEM}
        specs, arrays = [], []
        for item in list(operands) + [("a", self.token)]:
            kind, array = item if isinstance(item, tuple) else ("v", item)
            specs.append(pl.BlockSpec(memory_space=spaces[kind]))
            arrays.append(array)
        given, made = len(operands), len(outs)

        def call(*refs):
            rest = refs[given + 1 :]
            body(*refs[:given], *rest[:made], *rest[made + 1 :])

        *results, self.token = pl.pallas_call(
            call,
            out_shape=list(outs) + [shaped((8, 128), F32)],
            in_specs=specs,
            out_specs=[pl.BlockSpec(memory_space=pltpu.VMEM)] * made
            + [pl.BlockSpec(memory_space=pl.ANY)],
            scratch_shapes=list(scratch),
            input_output_aliases={given: made},
            compiler_params=pltpu.CompilerParams(vmem_limit_bytes=60 << 20),
            cost_estimate=pl.CostEstimate(
                flops=1 << 20, bytes_accessed=1 << 16, transcendentals=0
            ),
        )(*arrays)
        return results


def dot(a, b, precision=None):
    return jnp.dot(a, b, preferred_element_type=F32, precision=precision)


def dot_nt(a, b, precision=None):
    return lax.dot_general(
        a, b, (((1,), (1,)), ((), ())), preferred_element_type=F32, precision=precision
    )


def dot_tn(a, b, precision=None):
    return lax.dot_general(
        a, b, (((0,), (0,)), ((), ())), preferred_element_type=F32, precision=precision
    )


def iota(shape, dim):
    return lax.broadcasted_iota(I32, shape, dim)


def at(start, size):
    return pl.ds(pl.multiple_of(start, size), size)


def row_scale(values):
    return lax.rsqrt(jnp.mean(values * values, axis=-1, keepdims=True) + EPSILON)


def as_column(row):
    size = row.shape[-1]
    same = iota((size, size), 0) == iota((size, size), 1)
    return jnp.sum(jnp.where(same, row, 0.0), axis=1, keepdims=True)


def turn(values, cosines, sines):
    return values * cosines + pltpu.roll(values, HEAD_DIMENSION // 2, 1) * sines


def weights_of(query, keys, bias):
    scores = dot_nt(query, keys) * HEAD_DIMENSION ** (-0.5) + bias
    terms = jnp.exp(scores - jnp.max(scores, axis=-1, keepdims=True))
    return terms * (1.0 / jnp.sum(terms, axis=-1, keepdims=True))


def flat(lists):
    return [a for part in lists for a in part]


def regroup(refs, lists):
    out, i = [], 0
    for part in lists:
        out.append(refs[i : i + len(part)])
        i += len(part)
    return out


def per_device(
    inputs,
    seq_ids,
    routes,
    norm1_gain,
    w_query,
    key_weight,
    value_weight,
    q_gain,
    k_gain,
    w_out,
    norm2_gain,
    w_router,
    w_gate,
    w_up,
    w_down,
    cotangent,
):
    T = inputs.shape[1]
    D = inputs.shape[2]
    S = lax.axis_size("seq")
    N = lax.axis_size("shard")
    s = lax.axis_index("seq")
    d = lax.axis_index("shard")
    ring = Ring(N)
    half = ring.half
    chain = Chain()
    run, gate = chain.run, chain.gate
    heads = HQ // S
    replicas = S // KEY_VALUE_HEADS
    HD = HEAD_DIMENSION
    L = T * S
    E = S * N
    SP = -(-S // 8) * 8
    FF = w_gate.shape[2]
    cap = max(2, T * TOPK * 5 // (4 * E))
    slab = D // N
    QC = heads * HD
    C = QC + 2 * HD
    PR = w_out.shape[0] // S
    W = D + 128

    if (S, N) == (4, 8):
        quarter = [2, 0, 3, 1]
        spot = ring.index % 2 * 4 + ring.index // 2
        spread = []
        for s_to in range(S):
            for d_to in range(N):
                s_from = quarter.index(d_to // 2)
                spread.append((s_from * N + 2 * s_to + d_to % 2, s_to * N + d_to))
    else:
        quarter = list(range(S))
        spot = ring.index
        spread = [((g % S) * N + g // S, g) for g in range(S * N)]
    seat_s = jnp.arange(S, dtype=I32)
    sources = seat_s ^ s
    quarters = jnp.asarray(quarter, I32)
    quarter_of = jnp.sum(
        jnp.where(sources[:, None] == seat_s[None, :], quarters[None, :], 0), axis=1
    )
    meta = jnp.concatenate(
        [ring.index, spot, sources, sources * N + d, quarter_of]
    ).astype(I32)
    meta_s = ("s", meta)
    SPOT, SRC, EXP, QUA = N, 2 * N, 2 * N + S, 2 * N + 2 * S

    XR = 16
    while E % XR or (E // XR) * slab + slab + 128 + T > C:
        XR *= 2
    groups = E // XR
    misc = groups * slab
    spare = C - (misc + slab + 128 + T)

    seat = jnp.arange(128, dtype=I32)[None, :] // (128 // N) == d
    both_gains = jnp.stack([norm1_gain, norm2_gain])
    head_gains = jnp.where(
        seat, jnp.tile(jnp.stack([q_gain, k_gain]), (1, N)), jnp.zeros((), BF)
    )

    def pack_body(m, wq, wk, wv, gains, head_gain, router, table, out, sems):
        me = m[0]
        copies = [
            pltpu.make_async_copy(
                wq.at[:, at(me * QC, QC)], out.at[pl.ds(0, slab), pl.ds(0, QC)], sems.at[0]
            ),
            pltpu.make_async_copy(
                wk.at[:, at(me // replicas * HD, HD)],
                out.at[pl.ds(0, slab), pl.ds(QC, HD)],
                sems.at[1],
            ),
            pltpu.make_async_copy(
                wv.at[:, at(me // replicas * HD, HD)],
                out.at[pl.ds(0, slab), pl.ds(QC + HD, HD)],
                sems.at[2],
            ),
        ]
        for c in copies:
            c.start()
        low = pl.ds(slab, XR)
        for g in range(groups):
            out[low, g * slab : (g + 1) * slab] = router[g * XR : (g + 1) * XR, :]

        def two(pair, size):
            line = iota((XR, size), 0)
            pair = pair[...].astype(F32)
            return jnp.where(
                line == 0, pair[0:1], jnp.where(line == 8, pair[1:2], 0.0)
            ).astype(BF)

        out[low, misc : misc + slab] = two(gains, slab)
        out[low, misc + slab : misc + slab + 128] = two(head_gain, 128)
        lines = table[...].astype(F32)
        lines = jnp.concatenate([lines, jnp.zeros((XR - TOPK, T), F32)], axis=0)
        out[low, misc + slab + 128 : misc + slab + 128 + T] = lines.astype(BF)
        if spare:
            out[low, C - spare :] = jnp.zeros((XR, spare), BF)
        for c in copies:
            c.wait()

    (block,) = run(
        pack_body,
        [shaped((slab + XR, C), BF)],
        [
            ("s", s.reshape(1).astype(I32)),
            ("a", w_query),
            ("a", key_weight),
            ("a", value_weight),
            both_gains,
            head_gains,
            w_router.T,
            routes[0].T,
        ],
        [pltpu.SemaphoreType.DMA((3,))],
    )
    first = Gather(ring, chain, block)
    IR = 16

    def rows_body(x, ids, out):
        out[0:T, :] = x[...]
        line = jnp.broadcast_to(ids[...].astype(F32), (IR, T))
        out[T:, 0:T] = line.astype(BF)
        out[T:, T:] = jnp.zeros((IR, D - T), BF)

    (x_own,) = run(rows_body, [shaped((T + IR, D), BF)], [inputs[0], seq_ids])
    x_have = {0: x_own}
    bit = S // 2
    for step in range(half - 1):
        if bit:
            for k in sorted(x_have):
                if k:
                    (x_have[k],) = gate(x_have[k])
                x_have[k ^ bit] = swap(x_have[k], bit, S)
            bit //= 2
        first.step()
        if step == 0:
            piece = lax.dynamic_slice(w_out, (quarter_of[0] * PR, 0), (PR, D))
            (piece,) = gate(piece)
            piece = lax.ppermute(piece, ("seq", "shard"), spread)
    x_rows = [x_have[k] for k in range(S)]
    x_rows[1:] = gate(*x_rows[1:])

    positions = (sources[:, None] * T + jnp.arange(T, dtype=I32)).reshape(-1)
    inverse = ROPE_BASE ** (-2.0 * jnp.arange(HD // 2, dtype=F32) / HD)
    angles = positions.astype(F32)[:, None] * inverse[None, :]
    cosines, sines = jnp.cos(angles), jnp.sin(angles)
    cosines = jnp.concatenate([cosines, cosines], axis=1)
    sines = jnp.concatenate([-sines, sines], axis=1)
    cosines, sines, piece = gate(cosines, sines, piece)

    first.finish()
    blocks = first.blocks
    grad_low = cotangent[0]
    (dy_low,) = gate(grad_low)
    dy = Gather(ring, chain, dy_low)

    def fetch_block(m, parts, r, full, sem):
        copies, start = [], 0
        for i, part in enumerate(parts):
            rows = min(slab - start, part.shape[0])
            if rows > 0:
                base = pl.multiple_of(m[r] * slab + start, 16)
                copies.append(
                    pltpu.make_async_copy(
                        part.at[pl.ds(0, rows)], full.at[pl.ds(base, rows)], sem.at[r, i]
                    )
                )
            start += part.shape[0]
        for c in copies:
            c.start()
        return copies

    def project_body(*refs):
        m, xs = refs[0], refs[1 : 1 + S]
        cos, sin = refs[1 + S : 3 + S]
        rest = refs[3 + S :]
        blk = regroup(rest, blocks)
        rest = rest[sum(len(b) for b in blocks) :]
        h1, raw, krot, vlow, bias, g1, g2, gq, router, table, keys = rest[:11]
        full, ext, sems, ext_sems = rest[11:]
        small, copies = [], []
        for r in range(N):
            last = blk[r][-1]
            c = pltpu.make_async_copy(
                last.at[pl.ds(last.shape[0] - XR, XR)], ext.at[r], ext_sems.at[r]
            )
            c.start()
            small.append(c)
        for r in range(N):
            copies += fetch_block(m, blk[r], r, full, sems)

        id_f = [x[T : T + IR, 0:T].astype(F32)[0:1] for x in xs]
        for a in range(S):
            column = as_column(id_f[a])
            q_pos = m[SRC + a] * T + iota((T, T), 0)
            for b in range(S):
                k_pos = m[SRC + b] * T + iota((T, T), 1)
                allowed = (k_pos <= q_pos) & (column == id_f[b])
                bias[a * T : (a + 1) * T, b * T : (b + 1) * T] = jnp.where(
                    allowed, 0.0, NEGATIVE
                )

        for c in small:
            c.wait()
        gq[...] = jnp.zeros((8, 128), F32)
        for r in range(N):
            place = at(m[r] * slab, slab)
            for g in range(groups):
                router[g * XR : (g + 1) * XR, place] = ext[r, :, g * slab : (g + 1) * slab]
            gains = ext[r, :, misc : misc + slab].astype(F32)
            g1[:, place] = gains[0:1]
            g2[:, place] = gains[8:9]
            pair = ext[r, :, misc + slab : misc + slab + 128].astype(F32)
            gq[0:1, :] += pair[0:1]
            gq[1:2, :] += pair[8:9]
            lines = ext[r, :, misc + slab + 128 : misc + slab + 128 + T].astype(F32)[:TOPK]
            table[r] = lines
            keys[r] = jnp.zeros((SP, T), F32)
            for k in range(S):
                expert = m[EXP + k].astype(F32)
                keys[r, k : k + 1, :] = jnp.max(
                    jnp.where(lines == expert, 1.0, 0.0), axis=0, keepdims=True
                )
        hits = keys[...].reshape(N * SP, T)
        earlier = jnp.where(iota((T, T), 0) < iota((T, T), 1), 1.0, 0.0).astype(BF)
        ranks = dot(hits.astype(BF), earlier)
        keys[...] = jnp.where(hits > 0.0, ranks, -1e6).reshape(N, SP, T)

        for k in range(S):
            x = xs[k][0:T, :].astype(F32)
            h1[k * T : (k + 1) * T, :] = (x * row_scale(x) * g1[...]).astype(BF)
        for c in copies:
            c.wait()

        wide = 256 if C % 256 == 0 else 128

        def project(i, carry):
            raw[:, at(i * wide, wide)] = dot(h1[...], full[:, at(i * wide, wide)])
            return carry

        lax.fori_loop(0, C // wide, project, 0)
        k_raw = raw[:, QC : QC + HD]
        krot[...] = turn(k_raw * row_scale(k_raw) * gq[1:2, :], cos[...], sin[...]).astype(BF)
        vlow[...] = raw[:, QC + HD :].astype(BF)

    (
        h1,
        qkv,
        k_rot,
        v_low,
        bias,
        gain_one,
        gain_two,
        gain_qk,
        router_t,
        route_t,
        keys,
    ) = run(
        project_body,
        [
            shaped((L, D), BF),
            shaped((L, C), F32),
            shaped((L, HD), BF),
            shaped((L, HD), BF),
            shaped((L, L), F32),
            shaped((1, D), F32),
            shaped((1, D), F32),
            shaped((8, 128), F32),
            shaped((E, D), BF),
            shaped((N, TOPK, T), F32),
            shaped((N, SP, T), F32),
        ],
        [meta_s] + x_rows + [cosines, sines] + [("a", b) for b in flat(blocks)],
        [
            pltpu.VMEM((D, C), BF),
            pltpu.VMEM((N, XR, C), BF),
            pltpu.SemaphoreType.DMA((N, 2)),
            pltpu.SemaphoreType.DMA((N,)),
        ],
    )

    def attend_body(raw, krot, vlow, bias_, gq, cos, sin, rot, out):
        def head(h, carry):
            lanes = at(h * HD, HD)
            q_raw = raw[:, lanes]
            q = turn(q_raw * row_scale(q_raw) * gq[0:1, :], cos[...], sin[...]).astype(BF)
            rot[:, lanes] = q
            p = weights_of(q, krot[...], bias_[...]).astype(BF)
            out[:, lanes] = dot(p, vlow[...]).astype(BF)
            return carry

        lax.fori_loop(0, heads, head, 0)

    near_pairs = [[j, N - j] for j in range(half - 2, 0, -1)]
    near = flat(near_pairs) + [0]
    far = [half - 1, N - half + 1, half]

    def select(token_blocks, groups, rows=0, joint=False):
        order = flat(groups)
        chosen = [token_blocks[r] for r in order]
        size = len(order) * cap
        rows = max(rows, size)

        def body(*refs):
            mt, key, rest = refs[0], refs[1], refs[2:]
            tokens = regroup(rest, chosen)
            outs = rest[sum(len(b) for b in chosen) :]
            start = i = 0
            for group in groups:
                m = len(group)
                values = []
                for j in range(m):
                    parts = [t[...] for t in tokens[i + j]]
                    values.append(parts[0] if len(parts) == 1 else jnp.concatenate(parts, axis=0))
                for k in range(S):
                    acc = None
                    for j, r in enumerate(group):
                        slot = key[r, k : k + 1, :] + float(j * cap)
                        pick = jnp.where(
                            iota((m * cap, T), 0).astype(F32) == slot, 1.0, 0.0
                        ).astype(BF)
                        term = dot(pick, values[j])
                        acc = term if acc is None else acc + term
                    if joint:
                        outs[0][mt[SRC + k], start : start + m * cap, :] = acc.astype(BF)
                    else:
                        outs[k][start : start + m * cap, :] = acc.astype(BF)
                start += m * cap
                i += m
            if rows > size:
                for k in range(S):
                    outs[k][size:, :] = jnp.zeros((rows - size, D), BF)

        shapes = [shaped((S, rows, D), BF)] if joint else [shaped((rows, D), BF)] * S
        return run(body, shapes, [meta_s, keys] + flat(chosen))

    def exchange(pieces):
        return [pieces[0]] + [swap(pieces[k], k, S) for k in range(1, S)]

    def arrive(pieces):
        pieces[1:] = gate(*pieces[1:])

    def all_to_all(rows):
        return lax.all_to_all(rows, "seq", 0, 0, tiled=True)

    last_pair = near_pairs[-1] + [0]
    longer = T + 8
    dy.step()
    q_rot, attended = run(
        attend_body,
        [shaped((L, QC), BF), shaped((L, QC), BF)],
        [qkv, k_rot, v_low, bias, gain_qk, cosines, sines],
    )
    for j in range(2, half - 1):
        dy.arrive()
        if j + 1 < half - 1:
            dy.step()
    (piece,) = gate(piece)
    out_ring = Gather(ring, chain, piece)
    (dy_near,) = select(dy.blocks, near_pairs + [[0]], joint=True)
    dy_near = all_to_all(dy_near)
    while out_ring.done < half:
        out_ring.step()
    out_ring.finish()
    out_blocks = out_ring.blocks
    dy.step()

    def fetch_out(m, parts, full, sems):
        copies = []
        for r in range(N):
            start = 0
            for i, part in enumerate(parts[r]):
                rows = part.shape[0]
                base = pl.multiple_of(m[SPOT + r] * PR + start, 16)
                copies.append(
                    pltpu.make_async_copy(part, full.at[pl.ds(base, rows)], sems.at[r, i])
                )
                start += rows
        for c in copies:
            c.start()
        return copies

    def seq_reduce(make, ring_step=None):
        sent, kept = make()
        have = dict(zip(range(0, S, 2), kept))
        if ring_step is not None:
            ring_step()
        got = [swap(v, 1, S) for v in sent]
        bit = 2
        while bit < S:
            keys_sent = [k for k in sorted(have) if k & bit]
            keys_kept = [k for k in sorted(have) if not k & bit]
            order = sorted(have)

            def body(*refs):
                n = len(order)
                values, arrived, outs = refs[:n], refs[n : 2 * n], refs[2 * n :]
                total = {
                    k: values[i][...] + arrived[i][...].astype(F32)
                    for i, k in enumerate(order)
                }
                for i, k in enumerate(keys_sent):
                    outs[i][...] = total[k].astype(BF)
                for i, k in enumerate(keys_kept):
                    outs[len(keys_sent) + i][...] = total[k]

            result = run(
                body,
                [shaped((T, D), BF)] * len(keys_sent)
                + [shaped((T, D), F32)] * len(keys_kept),
                [have[k] for k in order] + got,
            )
            sent, kept = result[: len(keys_sent)], result[len(keys_sent) :]
            have = dict(zip(keys_kept, kept))
            if ring_step is not None:
                ring_step()
            got = [swap(v, bit, S) for v in sent]
            bit *= 2
        return have[0], got[0]

    reduce_shapes = [shaped((T, D), BF)] * (S // 2) + [shaped((T, D), F32)] * (S // 2)

    def make_output():
        def body(*refs):
            m, o, rest = refs[0], refs[1], refs[2:]
            parts = regroup(rest, out_blocks)
            rest = rest[sum(len(b) for b in out_blocks) :]
            outs, (full, sems) = rest[:S], rest[S:]
            for c in fetch_out(m, parts, full, sems):
                c.wait()

            def tile(i, carry):
                lanes = at(i * 512, 512)
                value = dot(o[...], full[:, lanes])
                for j, k in enumerate(range(1, S, 2)):
                    outs[j][:, lanes] = value[k * T : (k + 1) * T].astype(BF)
                for j, k in enumerate(range(0, S, 2)):
                    outs[S // 2 + j][:, lanes] = value[k * T : (k + 1) * T]
                return carry

            lax.fori_loop(0, D // 512, tile, 0)

        result = run(
            body,
            reduce_shapes,
            [meta_s, attended] + [("a", b) for b in flat(out_blocks)],
            [pltpu.VMEM((QC, D), BF), pltpu.SemaphoreType.DMA((N, 2))],
        )
        return result[: S // 2], result[S // 2 :]

    x2_own, x2_got = seq_reduce(make_output)
    (dy_near,) = gate(dy_near)
    dy.step()
    dy.finish()
    picked = select(dy.blocks, [far], longer)
    (x2_got,) = gate(x2_got)

    def second_body(x, own, got, g2, x2_out, h2_out):
        x2 = x[...].astype(F32) + own[...] + got[...].astype(F32)
        x2_out[...] = x2
        h2_out[...] = (x2 * row_scale(x2) * g2[...]).astype(BF)

    x_second, h2 = run(
        second_body,
        [shaped((T, D), F32), shaped((T, D), BF)],
        [inputs[0], x2_own, x2_got, gain_two],
    )

    walk = Gather(ring, chain, h2)
    dy_far = exchange(picked)
    h2_near = [None] * (len(near_pairs))
    for j in range(1, half):
        walk.step()
        if j == 1:
            picked = select(walk.blocks, [near_pairs[-1], [0]], longer)
            arrive(dy_far)
            moving = h2_near[-1] = exchange(picked)
        elif j < half - 1:
            picked = select(walk.blocks, [[j, N - j]])
            arrive(moving)
            moving = h2_near[half - 2 - j] = exchange(picked)
    walk.finish()
    picked = select(walk.blocks, [far])

    def gate_body(*refs):
        m, rest = refs[0], refs[1:]
        tokens = regroup(rest, walk.blocks)
        rest = rest[sum(len(b) for b in walk.blocks) :]
        router, table, key, gates_k, own, slots = rest
        line = iota((E, T), 0).astype(F32)
        for r in range(N):
            logits = [dot_nt(router[...], t[...]) for t in tokens[r]]
            logits = logits[0] if len(logits) == 1 else jnp.concatenate(logits, axis=1)
            routed = jnp.zeros((E, T), F32)
            for j in range(TOPK):
                routed = jnp.where(line == table[r, j : j + 1, :], 1.0, routed)
            top = jnp.max(jnp.where(routed > 0.0, logits, NEGATIVE), axis=0, keepdims=True)
            terms = jnp.where(routed > 0.0, jnp.exp(logits - top), 0.0)
            gates = terms / jnp.sum(terms, axis=0, keepdims=True)
            if r == 0:
                eye = jnp.where(iota((E, 128), 0) == iota((E, 128), 1), 1.0, 0.0)
                own[...] = dot_tn(gates, eye, EXACT)
            gates_k[r] = jnp.zeros((SP, T), F32)
            for k in range(S):
                value = jnp.sum(
                    jnp.where(line == m[EXP + k].astype(F32), gates, 0.0),
                    axis=0,
                    keepdims=True,
                )
                gates_k[r, k : k + 1, :] = value
                pick = jnp.where(iota((cap, T), 0).astype(F32) == key[r, k : k + 1, :], 1.0, 0.0)
                slots[k, r : r + 1, :] = dot_nt(
                    jnp.broadcast_to(value, (8, T)), pick, EXACT
                )[0:1]

    gate_k, gate_own, slot_gates = run(
        gate_body,
        [shaped((N, SP, T), F32), shaped((T, 128), F32), shaped((S, N, cap), F32)],
        [meta_s] + flat(walk.blocks) + [router_t, route_t, keys],
    )

    slot_pieces = [slot_gates[0]] + [swap(slot_gates[k], k, S) for k in range(1, 3)]
    arrive(moving)
    arrive(slot_pieces)
    h2_far = exchange(picked)
    slot_pieces += [swap(slot_gates[k], k, S) for k in range(3, S)]

    gate_w, up_w, down_w = w_gate[0], w_up[0], w_down[0]

    def expert(x_parts, y_parts, back_sizes, front_rows=0, joint=False):
        x_used = [used for _, used in x_parts]
        y_used = [used for _, used in y_parts]
        x_parts = [part for part, _ in x_parts]
        y_parts = [part for part, _ in y_parts]
        size = sum(x_used)
        pad = -(-size // 16) * 16
        rows = S * pad
        starts = np.cumsum([0] + list(back_sizes))
        front_count = 1 if joint else S

        def body(*refs):
            mt, rest = refs[0], refs[1:]
            xs = regroup(rest, x_parts)
            rest = rest[S * len(x_parts) :]
            ys = regroup(rest, y_parts)
            rest = rest[sum(len(p) for p in y_parts) :]
            wg_in, wu_in, wd_in = rest[:3]
            rest = rest[3:]
            outs = [rest[i * S : (i + 1) * S] for i in range(len(back_sizes))]
            rest = rest[S * len(back_sizes) :]
            fronts, rest = rest[:front_count], rest[front_count:]
            xp, yp, hid, dg_out, du_out, sums, wg, wu, wd, sems = rest

            def copies(i):
                lanes = at(i * 256, 256)
                return [
                    pltpu.make_async_copy(wg_in.at[:, lanes], wg.at[:, lanes], sems.at[0, i]),
                    pltpu.make_async_copy(wu_in.at[:, lanes], wu.at[:, lanes], sems.at[1, i]),
                    pltpu.make_async_copy(wd_in.at[lanes, :], wd.at[lanes, :], sems.at[2, i]),
                ]

            for i in range(FF // 256):
                for c in copies(i):
                    c.start()
            for k in range(S):
                for sources_, used, target in ((xs, x_used, xp), (ys, y_used, yp)):
                    values = [
                        part[0][mt[SRC + k], 0:n, :] if len(part) == 1 else part[k][0:n, :]
                        for part, n in zip(sources_, used)
                    ]
                    if pad > size:
                        values.append(jnp.zeros((pad - size, D), BF))
                    value = values[0] if len(values) == 1 else jnp.concatenate(values, axis=0)
                    target[k * pad : (k + 1) * pad, :] = value
            sums[...] = jnp.zeros_like(sums)

            def first(i, carry):
                lanes = at(i * 256, 256)
                for c in copies(i):
                    c.wait()
                g = dot(xp[...], wg[:, lanes])
                u = dot(xp[...], wu[:, lanes])
                z = dot_nt(yp[...], wd[lanes, :])
                sig = 1.0 / (1.0 + jnp.exp(-g))
                silu = g * sig
                hidden = (silu * u).astype(BF)
                hid[:, lanes] = hidden
                du_out[:, lanes] = (z * silu).astype(BF)
                dg_out[:, lanes] = (z * u * sig * (1.0 + g * (1.0 - sig))).astype(BF)
                sums[...] += jnp.sum(z * hidden.astype(F32), axis=1, keepdims=True)
                return carry

            lax.fori_loop(0, FF // 256, first, 0)

            def second(i, carry):
                cols = at(i * 512, 512)
                back = dot_nt(dg_out[...], wg[cols, :]) + dot_nt(du_out[...], wu[cols, :])
                front = dot(hid[...], wd[:, cols])
                for k in range(S):
                    for n, part in enumerate(outs):
                        low = k * pad + int(starts[n])
                        high = k * pad + int(starts[n + 1])
                        part[k][:, cols] = back[low:high].astype(BF)
                    part = front[k * pad : k * pad + size].astype(BF)
                    if joint:
                        fronts[0][mt[SRC + k], :, cols] = part
                    else:
                        fronts[k][0:size, cols] = part
                    if front_rows > size:
                        fronts[k][size:, cols] = jnp.zeros((front_rows - size, 512), BF)
                return carry

            lax.fori_loop(0, D // 512, second, 0)
            mine = iota((pad, 128), 1) == mt[EXP]
            for k in range(S):
                term = jnp.where(mine, sums[k * pad : (k + 1) * pad, 0:1], 0.0)
                for n, part in enumerate(outs):
                    part[k][:, D:] = term[int(starts[n]) : int(starts[n + 1])].astype(BF)

        result = run(
            body,
            [shaped((b, W), BF) for b in back_sizes for _ in range(S)]
            + (
                [shaped((S, size, D), BF)]
                if joint
                else [shaped((max(size, front_rows), D), BF)] * S
            )
            + [shaped((rows, D), BF)] * 2
            + [shaped((rows, FF), BF)] * 3,
            [meta_s]
            + flat(x_parts)
            + flat(y_parts)
            + [("a", gate_w), ("a", up_w), ("a", down_w)],
            [
                pltpu.VMEM((rows, 128), F32),
                pltpu.VMEM((D, FF), BF),
                pltpu.VMEM((D, FF), BF),
                pltpu.VMEM((FF, D), BF),
                pltpu.SemaphoreType.DMA((3, FF // 256)),
            ],
        )
        count = len(back_sizes)
        returned = [result[i * S : (i + 1) * S] for i in range(count)]
        rest = result[S * count :]
        return returned, rest[:front_count], rest[front_count:]

    pair = 2 * cap
    near_sizes = [pair] * (len(near_pairs) - 1) + [pair + cap]
    near_used = [pair] * (len(near_pairs) - 1) + [pair + cap]
    near_back, near_front, near_kept = expert(
        list(zip(h2_near, near_used)), [([dy_near], sum(near_used))], near_sizes, 0, True
    )
    arrive(h2_far)
    slot_pieces[3:] = gate(*slot_pieces[3:])
    near_back[-1] = exchange(near_back[-1])
    (far_back,), far_front, far_kept = expert(
        [(h2_far, 3 * cap)], [(dy_far, 3 * cap)], [3 * cap], T + 16
    )
    arrive(near_back[-1])
    far_back = exchange(far_back)

    def mix(group, pieces, split=False, first=0):
        m = len(group)
        wide = pieces[0].shape[-1]
        joint = pieces[0].ndim == 3
        cut = halfway(T)

        def body(*refs):
            mt, key, gate_ = refs[:3]
            rows, outs = refs[3 : 3 + len(pieces)], refs[3 + len(pieces) :]
            used = slice(first * cap, (first + m) * cap)
            for j, r in enumerate(group):
                acc = None
                for k in range(S):
                    slot = key[r, k : k + 1, :] + float(j * cap)
                    hit = iota((m * cap, T), 0).astype(F32) == slot
                    weight = jnp.where(hit, gate_[r, k : k + 1, :], 0.0).astype(BF)
                    source = rows[0][mt[SRC + k], used, :] if joint else rows[k][used, :]
                    term = dot_tn(weight, source)
                    acc = term if acc is None else acc + term
                if split and j == m - 1:
                    outs[j][...] = acc[:cut].astype(BF)
                    outs[j + 1][...] = acc[cut:].astype(BF)
                else:
                    outs[j][...] = acc

        shapes = [shaped((T, wide), F32)] * m
        if split:
            shapes[-1:] = [shaped((cut, wide), BF), shaped((T - cut, wide), BF)]
        return run(body, shapes, [meta_s, keys, gate_k] + pieces)

    def mix_and_step(walk_, group, pieces):
        m = len(group)

        def body(key, gate_, a_in, b_in, *refs):
            rows, outs = refs[:S], refs[S:]
            for j, (r, arrived) in enumerate(zip(group, (a_in, b_in))):
                acc = arrived[...].astype(F32)
                for k in range(S):
                    slot = key[r, k : k + 1, :] + float(j * cap)
                    hit = iota((m * cap, T), 0).astype(F32) == slot
                    weight = jnp.where(hit, gate_[r, k : k + 1, :], 0.0).astype(BF)
                    acc += dot_tn(weight, rows[k][0 : m * cap, :])
                outs[j][...] = acc.astype(BF)

        shape = shaped(walk_.ahead.shape, BF)
        a, b = run(
            body, [shape, shape], [keys, gate_k, walk_.ahead, walk_.behind] + pieces
        )
        walk_.left -= 1
        walk_.ahead, walk_.behind = ring.forward(a), ring.backward(b)

    def as_rows(values, group):
        return jnp.stack([jnp.stack([v[r] for r in group]).reshape(-1) for v in values])

    row_gates = [as_rows(slot_pieces, near), as_rows(slot_pieces, far)]

    def row_grad(left, right, scale_left, shape, by_column):
        def body(*refs):
            gates, lefts, rights = refs[:2], refs[2:4], refs[4:6]
            out, scaled = refs[6:]
            offset = 0
            source = lefts if scale_left else rights
            for i, g in enumerate(gates):
                size, rows = g.shape[1], source[i].shape[0] // S
                for k in range(S):
                    column = as_column(g[k : k + 1, :])
                    if rows > size:
                        column = jnp.concatenate(
                            [column, jnp.zeros((rows - size, 1), F32)], axis=0
                        )
                    scaled[offset : offset + rows, :] = (
                        source[i][k * rows : (k + 1) * rows, :].astype(F32) * column
                    ).astype(BF)
                    offset += rows
            plain = rights if scale_left else lefts

            def tile(i, carry):
                cols = at(i * 512, 512)
                other = jnp.concatenate([p[:, cols] for p in plain], axis=0)
                if by_column:
                    out[:, cols] = dot_tn(scaled[...], other)
                else:
                    out[cols, :] = dot_tn(other, scaled[...])
                return carry

            lax.fori_loop(0, D // 512, tile, 0)

        total = sum(a.shape[0] for a in left)
        (result,) = run(
            body,
            [shaped(shape, F32)],
            row_gates + list(left) + list(right),
            [pltpu.VMEM((total, FF), BF)],
        )
        return result

    kept = list(zip(near_kept, far_kept))
    x_kept, y_kept, hid_kept, dg_kept, du_kept = kept

    back_parts = {}
    a, b, c = last_pair
    back_parts[a], back_parts[b], back_parts[c] = mix(last_pair, near_back[-1])
    grad_gate = row_grad(x_kept, dg_kept, False, (D, FF), False)
    arrive(far_back)
    far_top, far_bottom = mix(far[2:], far_back, split=True, first=2)
    back = Reduce(ring, chain, far_top, far_bottom)
    back_parts[far[0]], back_parts[far[1]] = mix(far[:2], far_back)

    def back_step():
        back.step(back_parts[back.left], back_parts[N - back.left])

    back_step()
    grads = [
        lambda: row_grad(x_kept, du_kept, False, (D, FF), False),
        lambda: row_grad(hid_kept, y_kept, True, (FF, D), True),
    ]
    done_grads = []
    for i in range(len(near_pairs) - 1):
        near_back[i] = exchange(near_back[i])
        if grads:
            done_grads.append(grads.pop(0)())
        arrive(near_back[i])
        if i + 2 == len(near_pairs):
            far_front = exchange(far_front)
        mix_and_step(back, near_pairs[i], near_back[i])
    if grads:
        done_grads.append(grads.pop(0)())
    while back.left > 0:
        back_step()
    grad_up, grad_down = done_grads
    arrive(far_front)
    y_parts = {}
    y_parts[far[0]], y_parts[far[1]], y_top, y_bottom = mix(far, far_front, split=True)
    back.ahead, back.behind, y_top, y_bottom = gate(back.ahead, back.behind, y_top, y_bottom)
    front = Reduce(ring, chain, y_top, y_bottom)

    extra_rows = -(-(E // 8 * slab + slab) // D) * 8

    def tokens_body(own, ahead, behind, x2, g2, router, gates, hidden, dy_, dx2, da, small):
        total = own[...] + ahead[...].astype(F32) + behind[...].astype(F32)
        gated = total[:, D:]
        dl = gated - gates[...] * jnp.sum(gated, axis=1, keepdims=True)
        grad = total[:, :D] + dot(dl[:, :E], router[...].astype(F32), EXACT)
        small[0:E, :] = dot_tn(dl, hidden[...].astype(F32), EXACT)[:E]
        scale = row_scale(x2[...])
        n2 = x2[...] * scale
        dn = grad * g2[...]
        small[E : E + 8, :] = jnp.broadcast_to(
            jnp.sum(grad * n2, axis=0, keepdims=True), (8, D)
        )
        out = dy_[...].astype(F32) + scale * (
            dn - n2 * jnp.mean(dn * n2, axis=-1, keepdims=True)
        )
        dx2[...] = out
        da[...] = out.astype(BF)

    grad_second, grad_attn, small_two = run(
        tokens_body,
        [shaped((T, D), F32), shaped((T, D), BF), shaped((E + 8, D), F32)],
        [
            back_parts[0],
            back.ahead,
            back.behind,
            x_second,
            gain_two,
            router_t,
            gate_own,
            h2,
            grad_low,
        ],
    )
    da_have = {0: grad_attn}
    bit = S // 2
    front_sent = False
    while bit:
        for k in sorted(da_have):
            if k:
                (da_have[k],) = gate(da_have[k])
            da_have[k ^ bit] = swap(da_have[k], bit, S)
        if bit == S // 2:
            front.step(y_parts[half - 1], y_parts[N - half + 1])
        elif not front_sent:
            near_front = [all_to_all(gate(near_front[0])[0])]
            front_sent = True
        bit //= 2
    da_rows = [da_have[k] for k in range(S)]
    da_rows[1:] = gate(*da_rows[1:])

    def out_grad_body(*refs):
        m, o, das, small = refs[0], refs[1], refs[2 : 2 + S], refs[2 + S]
        outs, full = refs[3 + S : 4 + S + N], refs[4 + S + N]
        da = jnp.concatenate([a[...] for a in das], axis=0)
        if PR % 128:
            full[...] = dot_tn(o[...], da)
        cut = halfway(PR + extra_rows)
        for r in range(N):
            if PR % 128:
                value = full[at(m[SPOT + r] * PR, PR), :]
            else:
                value = dot_tn(o[:, at(m[SPOT + r] * PR, PR)], da)
            place = at(m[r] * slab, slab)
            tail = [small[8 * g : 8 * (g + 1), place] for g in range(E // 8 + 1)]
            used = len(tail) * slab
            room = extra_rows // 8 * D
            if room > used:
                tail.append(jnp.zeros((8, room - used), F32))
            tail = jnp.concatenate(tail, axis=1)
            tail = [tail[:, g * D : (g + 1) * D] for g in range(extra_rows // 8)]
            if r == half:
                whole = jnp.concatenate([value] + tail, axis=0).astype(BF)
                outs[N - 1][...] = whole[:cut]
                outs[N][...] = whole[cut:]
            else:
                target = outs[r - (r > half)]
                target[0:PR, :] = value
                for g in range(extra_rows // 8):
                    target[PR + 8 * g : PR + 8 * (g + 1), :] = tail[g]

    out_cut = halfway(PR + extra_rows)
    *out_list, out_top, out_bottom = run(
        out_grad_body,
        [shaped((PR + extra_rows, D), F32)] * (N - 1)
        + [shaped((out_cut, D), BF), shaped((PR + extra_rows - out_cut, D), BF)],
        [meta_s, attended] + da_rows + [small_two],
        [pltpu.VMEM((QC, D) if PR % 128 else (8, 128), F32)],
    )
    out_parts = {r: out_list[r - (r > half)] for r in range(N) if r != half}
    out_walk = Reduce(ring, chain, out_top, out_bottom)

    def both_steps():
        if out_walk.left > 0:
            out_walk.step(out_parts[out_walk.left], out_parts[N - out_walk.left])

    def do_body(*refs):
        m, das, rest = refs[0], refs[1 : 1 + S], refs[1 + S :]
        parts = regroup(rest, out_blocks)
        do, full, sems = rest[sum(len(b) for b in out_blocks) :]
        for c in fetch_out(m, parts, full, sems):
            c.wait()
        da = jnp.concatenate([a[...] for a in das], axis=0)
        wide = 256 if QC % 256 == 0 else 128

        def tile(i, carry):
            do[:, at(i * wide, wide)] = dot_nt(da, full[at(i * wide, wide), :]).astype(BF)
            return carry

        lax.fori_loop(0, QC // wide, tile, 0)

    (grad_heads,) = run(
        do_body,
        [shaped((L, QC), BF)],
        [meta_s] + da_rows + [("a", b) for b in flat(out_blocks)],
        [pltpu.VMEM((QC, D), BF), pltpu.SemaphoreType.DMA((N, 2))],
    )
    front.ahead, front.behind = gate(front.ahead, front.behind)
    out_walk.step(out_parts[out_walk.left], out_parts[N - out_walk.left])

    def back_body(first_head, count):
        def body(raw_in, rot_in, do_in, krot, vlow, bias_, gq, cos, sin, dk0, dv0, gain0, *rest):
            dq, dk, dv, gain, raw, rot, do, sems = rest
            lanes_here = pl.ds(first_head * HD, count * HD)
            copies = [
                pltpu.make_async_copy(raw_in.at[:, lanes_here], raw, sems.at[0]),
                pltpu.make_async_copy(rot_in.at[:, lanes_here], rot, sems.at[1]),
                pltpu.make_async_copy(do_in.at[:, lanes_here], do, sems.at[2]),
            ]
            for c in copies:
                c.start()
            dk[...] = dk0[...]
            dv[...] = dv0[...]
            gain[...] = gain0[...]
            for c in copies:
                c.wait()

            def head(h, carry):
                lanes = at(h * HD, HD)
                q = rot[:, lanes]
                grad = do[:, lanes]
                p = weights_of(q, krot[...], bias_[...])
                dp = dot_nt(grad, vlow[...])
                centre = jnp.sum(p * dp, axis=-1, keepdims=True)
                ds = (p * (dp - centre)).astype(BF)
                scale = HD ** (-0.5)
                dk[...] += dot_tn(ds, q) * scale
                dv[...] += dot_tn(p.astype(BF), grad)
                dqr = (dot(ds, krot[...]) * scale).astype(BF).astype(F32)
                dqn = turn(dqr, cos[...], -sin[...])
                q_raw = raw[:, lanes]
                factor = row_scale(q_raw)
                nq = q_raw * factor
                gain[0:1, :] += jnp.sum(dqn * nq, axis=0, keepdims=True)
                dn = dqn * gq[0:1, :]
                dq[:, lanes] = (
                    factor * (dn - nq * jnp.mean(dn * nq, axis=-1, keepdims=True))
                ).astype(BF)
                return carry

            lax.fori_loop(0, count, head, 0)

        return body

    calls = 2
    per_call = heads // calls
    grad_k, grad_v = jnp.zeros((L, HD), F32), jnp.zeros((L, HD), F32)
    gain_sum = jnp.zeros((8, 128), F32)
    grad_q = []
    for i in range(calls):
        dq, grad_k, grad_v, gain_sum = run(
            back_body(i * per_call, per_call),
            [
                shaped((L, per_call * HD), BF),
                shaped((L, HD), F32),
                shaped((L, HD), F32),
                shaped((8, 128), F32),
            ],
            [("a", qkv), ("a", q_rot), ("a", grad_heads)]
            + [k_rot, v_low, bias, gain_qk, cosines, sines, grad_k, grad_v, gain_sum],
            [
                pltpu.VMEM((L, per_call * HD), F32),
                pltpu.VMEM((L, per_call * HD), BF),
                pltpu.VMEM((L, per_call * HD), BF),
                pltpu.SemaphoreType.DMA((3,)),
            ],
        )
        grad_q.append(dq)
        both_steps()
    while out_walk.left > 0:
        both_steps()

    def final_y_body(x2, own, ahead, behind, out):
        out[...] = (
            x2[...] + own[...] + ahead[...].astype(F32) + behind[...].astype(F32)
        ).astype(BF)

    grad_k, grad_v = grad_k.astype(BF), grad_v.astype(BF)
    if replicas > 1:
        both = jnp.concatenate([grad_k, grad_v], axis=1).astype(F32)
        bit = 1
        while bit < replicas:
            both = both + swap(both.astype(BF), bit, S).astype(F32)
            bit *= 2
        grad_k, grad_v = both[:, :HD], both[:, HD:]

    def key_body(dk, dv, raw_in, gq, cos, sin, gain, dkv, gains, raw, sem):
        c = pltpu.make_async_copy(raw_in.at[:, pl.ds(QC, HD)], raw, sem)
        c.start()
        c.wait()
        k_raw = raw[...]
        factor = row_scale(k_raw)
        nk = k_raw * factor
        dkn = turn(dk[...].astype(F32), cos[...], -sin[...])
        k_part = jnp.sum(dkn * nk, axis=0, keepdims=True) * (1.0 / replicas)
        dn = dkn * gq[1:2, :]
        dk_raw = factor * (dn - nk * jnp.mean(dn * nk, axis=-1, keepdims=True))
        dkv[:, 0:HD] = dk_raw.astype(BF)
        dkv[:, HD:] = dv[...].astype(BF)
        line = iota((8, 128), 0)
        gains[...] = jnp.where(line == 0, gain[0:1, :], jnp.where(line == 1, k_part, 0.0))

    grad_kv, gain_lines = run(
        key_body,
        [shaped((L, 2 * HD), BF), shaped((8, 128), F32)],
        [grad_k, grad_v, ("a", qkv), gain_qk, cosines, sines, gain_sum],
        [pltpu.VMEM((L, HD), F32), pltpu.SemaphoreType.DMA],
    )

    block_rows = slab + 8
    block_cut = halfway(block_rows)

    def weight_grad(offsets, split=False):
        def body(m, h, *rest):
            dqs, rest = rest[:calls], rest[calls:]
            dkv, gains, outs = rest[0], rest[1], rest[2:]
            span = per_call * HD
            for j, r in enumerate(offsets):
                rows = h[:, at(m[r] * slab, slab)]
                pieces = [dot_tn(rows, dq[...]) for dq in dqs] + [dot_tn(rows, dkv[...])]
                spots = [slice(i * span, (i + 1) * span) for i in range(calls)]
                spots.append(slice(QC, C))
                tail = jnp.concatenate([gains[...], jnp.zeros((8, C - 128), F32)], axis=1)
                for spot_, piece_ in zip(spots, pieces):
                    if split:
                        outs[0][:, spot_] = piece_[:block_cut].astype(BF)
                        low = jnp.concatenate([piece_[block_cut:], tail[:, spot_]], axis=0)
                        outs[1][:, spot_] = low.astype(BF)
                    else:
                        outs[j][0:slab, spot_] = piece_
                if not split:
                    outs[j][slab:, :] = tail

        if split:
            shapes = [shaped((block_cut, C), BF), shaped((block_rows - block_cut, C), BF)]
        else:
            shapes = [shaped((block_rows, C), F32)] * len(offsets)
        return run(body, shapes, [meta_s, h1] + grad_q + [grad_kv, gain_lines])

    def total_body(own, ahead, behind, *outs):
        total = own[...] + ahead[...].astype(F32) + behind[...].astype(F32)
        start = 0
        for out in outs:
            out[...] = total[start : start + out.shape[0]].astype(BF)
            start += out.shape[0]

    out_piece, out_tail = run(
        total_body,
        [shaped((PR, D), BF), shaped((extra_rows, D), BF)],
        [out_parts[0], out_walk.ahead, out_walk.behind],
    )
    block_top, block_bottom = weight_grad([half], split=True)
    block_walk = Reduce(ring, chain, block_top, block_bottom)
    out_piece = lax.ppermute(out_piece, ("seq", "shard"), [(b, a) for a, b in spread])
    block_parts = {}

    def more_blocks(offsets):
        block_parts.update(zip(offsets, weight_grad(offsets)))

    def block_step():
        block_walk.step(block_parts[block_walk.left], block_parts[N - block_walk.left])

    more_blocks([half - 1, N - half + 1])
    block_step()
    more_blocks([r for r in range(N) if r not in block_parts and r != half])
    def make_first():
        def body(*refs):
            m, dqs, rest = refs[0], refs[1 : 1 + calls], refs[1 + calls :]
            dkv, rest = rest[0], rest[1:]
            blk = regroup(rest, blocks)
            rest = rest[sum(len(b) for b in blocks) :]
            outs, (full, sems) = rest[:S], rest[S:]
            copies = []
            for r in range(N):
                copies += fetch_block(m, blk[r], r, full, sems)
            share = (dkv[...].astype(F32) * (1.0 / replicas)).astype(BF)
            for c in copies:
                c.wait()
            span = per_call * HD

            def tile(i, carry):
                lanes = at(i * 512, 512)
                value = dot_nt(share, full[lanes, QC:])
                for j in range(calls):
                    value += dot_nt(dqs[j][...], full[lanes, j * span : (j + 1) * span])
                for j, k in enumerate(range(1, S, 2)):
                    outs[j][:, lanes] = value[k * T : (k + 1) * T].astype(BF)
                for j, k in enumerate(range(0, S, 2)):
                    outs[S // 2 + j][:, lanes] = value[k * T : (k + 1) * T]
                return carry

            lax.fori_loop(0, D // 512, tile, 0)

        result = run(
            body,
            reduce_shapes,
            [meta_s] + grad_q + [grad_kv] + [("a", b) for b in flat(blocks)],
            [pltpu.VMEM((D, C), BF), pltpu.SemaphoreType.DMA((N, 2))],
        )
        return result[: S // 2], result[S // 2 :]

    out_have = {0: out_piece}
    tail_have = {0: out_tail}
    bits = []
    while not bits or bits[-1] > 1:
        bits.append(bits[-1] // 2 if bits else S // 2)

    def tail_step():
        bit_ = bits.pop(0) if bits else 0
        pairs = [(have, k) for have in (out_have, tail_have) for k in sorted(have)]
        for have, k in pairs:
            if bit_ and k:
                (have[k],) = gate(have[k])
        if block_walk.left > 0:
            block_step()
        for have, k in pairs:
            if bit_:
                if not k:
                    (have[k],) = gate(have[k])
                have[k ^ bit_] = swap(have[k], bit_, S)

    one_own, one_got = seq_reduce(make_first, tail_step)
    near_front[:] = gate(*near_front)
    for r, part in zip(near, mix(near, near_front)):
        y_parts[r] = part
    while block_walk.left > 0 or bits:
        tail_step()
    out_pieces = [out_have[k] for k in range(S)]
    tail_pieces = [tail_have[k] for k in range(S)]
    out_pieces[1:] = gate(*out_pieces[1:])

    def out_join_body(*refs):
        m, pieces, tails = refs[0], refs[1 : 1 + S], refs[1 + S : 1 + 2 * S]
        out, small = refs[1 + 2 * S :]
        for k in range(S):
            out[at(m[QUA + k] * PR, PR), :] = pieces[k][...].astype(F32)
        small[...] = tree_sum([t_[...].astype(F32) for t_ in tails])

    grad_out_w, tail_two = run(
        out_join_body,
        [shaped((S * PR, D), F32), shaped((extra_rows, D), F32)],
        [meta_s] + out_pieces + tail_pieces,
    )

    def inputs_body(x_ref, own, got, g1, dx2, out):
        x = x_ref[...].astype(F32)
        grad = own[...] + got[...].astype(F32)
        scale = row_scale(x)
        n1 = x * scale
        dn = grad * g1[...]
        out[...] = dx2[...] + scale * (
            dn - n1 * jnp.mean(dn * n1, axis=-1, keepdims=True)
        )

    (grad_inputs,) = run(
        inputs_body,
        [shaped((T, D), F32)],
        [inputs[0], one_own, one_got, gain_one, grad_second],
    )

    (block_sum,) = run(
        total_body,
        [shaped((block_rows, C), BF)],
        [block_parts[0], block_walk.ahead, block_walk.behind],
    )
    block_have = {0: block_sum}
    bit = S // 2
    for k in sorted(block_have):
        block_have[k ^ bit] = swap(block_have[k], bit, S)

    front.step(y_parts[front.left], y_parts[N - front.left])
    while bit > 1:
        bit //= 2
        for k in sorted(block_have):
            if k:
                (block_have[k],) = gate(block_have[k])
            block_have[k ^ bit] = swap(block_have[k], bit, S)
    block_pieces = [block_have[k] for k in range(S)]
    while front.left > 0:
        front.step(y_parts[front.left], y_parts[N - front.left])
    block_pieces[1:] = gate(*block_pieces[1:])

    def join_body(*refs):
        m, pieces = refs[0], refs[1 : 1 + S]
        wq, wk, wv, oq, ok, ov, gains, rows = refs[1 + S :]
        for k in range(S):
            source = m[SRC + k]
            oq[:, at(source * QC, QC)] = pieces[k][0:slab, 0:QC].astype(F32)
            lanes = at(source // replicas * HD, HD)
            ok[:, lanes] = pieces[k][0:slab, QC : QC + HD].astype(F32)
            ov[:, lanes] = pieces[k][0:slab, QC + HD :].astype(F32)
        total = jnp.sum(oq[...] * wq[...].astype(F32), axis=1, keepdims=True)
        total += jnp.sum(ok[...] * wk[...].astype(F32), axis=1, keepdims=True)
        total += jnp.sum(ov[...] * wv[...].astype(F32), axis=1, keepdims=True)
        same = iota((slab, slab), 0) == iota((slab, slab), 1)
        rows[...] = jnp.broadcast_to(
            jnp.sum(jnp.where(same, total, 0.0), axis=0, keepdims=True), (8, slab)
        )
        gains[...] = tree_sum([p[slab:, 0:128].astype(F32) for p in pieces])

    grad_query, grad_key, grad_value, gain_rows, one_rows = run(
        join_body,
        [
            shaped((slab, S * QC), F32),
            shaped((slab, KEY_VALUE_HEADS * HD), F32),
            shaped((slab, KEY_VALUE_HEADS * HD), F32),
            shaped((8, 128), F32),
            shaped((8, slab), F32),
        ],
        [meta_s] + block_pieces + [w_query, key_weight, value_weight],
    )
    (result,) = run(
        final_y_body,
        [shaped((T, D), BF)],
        [x_second, y_parts[0], front.ahead, front.behind],
    )

    grad_gain_one = one_rows[0] / norm1_gain.astype(F32)
    share = HD // N
    grad_qgain = lax.dynamic_slice(gain_rows[0], (d * share,), (share,))
    grad_kgain = lax.dynamic_slice(gain_rows[1], (d * share,), (share,))

    lines = [
        tail_two[8 * g : 8 * (g + 1), i * slab : (i + 1) * slab]
        for g in range(extra_rows // 8)
        for i in range(D // slab)
    ]
    grad_router = jnp.concatenate(lines[: E // 8], axis=0).T
    grad_gain_two = lines[E // 8][0]

    return (
        result[None],
        grad_inputs[None],
        grad_gain_one,
        grad_query,
        grad_key,
        grad_value,
        grad_qgain,
        grad_kgain,
        grad_out_w,
        grad_gain_two,
        grad_router,
        grad_gate[None],
        grad_up[None],
        grad_down[None],
    )


def solution(mesh):
    in_specs = (
        P("shard", "seq", None),
        P("shard", "seq"),
        P("shard", "seq", None),
        P("shard"),
        P("shard", None),
        P("shard", None),
        P("shard", None),
        P("shard"),
        P("shard"),
        P("shard", None),
        P("shard"),
        P("shard", None),
        P(("seq", "shard"), None, None),
        P(("seq", "shard"), None, None),
        P(("seq", "shard"), None, None),
        P("shard", "seq", None),
    )
    out_specs = (
        P("shard", "seq", None),
        P("shard", "seq", None),
        P("shard"),
        P("shard", None),
        P("shard", None),
        P("shard", None),
        P("shard"),
        P("shard"),
        P("shard", None),
        P("shard"),
        P("shard", None),
        P(("seq", "shard"), None, None),
        P(("seq", "shard"), None, None),
        P(("seq", "shard"), None, None),
    )
    return jax.shard_map(
        per_device, mesh=mesh, in_specs=in_specs, out_specs=out_specs, check_vma=False
    )
```

time: 844 us -> 706 us (0.84)
  waiting for transfers between devices: 353 us -> 203 us
  Pallas kernels: 261 us -> 308 us
  other arithmetic: 41.2 us -> 10.3 us
    ppermute x32, waiting for transfers between devices: 167 us -> 96.8 us  [forward(): return lax.ppermute(value, 'shard', self.up)]
    pallas_call x34 -> x52, Pallas kernels: 261 us -> 308 us  [run(): pl.pallas_call(call, out_shape=list(outs) + [shaped((8, 128), F32)], in_s...]
    ppermute x1, waiting for transfers between devices: 28.1 us -> 0.01 us  [per_device(): lax.ppermute(out_piece, ('seq', 'shard'), [(b, a) for a, b in spread])]
    ppermute x73 -> x48, waiting for transfers between devices: 96.4 us -> 77.9 us  [swap(): return lax.ppermute(value, 'seq', [(i, i ^ bit) for i in range(count)])]
    ppermute x32, waiting for transfers between devices: 30.1 us -> 12.6 us  [backward(): return lax.ppermute(value, 'shard', self.down)]
    ppermute x32, starting transfers between devices: 45.5 us -> 28.2 us  [forward(): return lax.ppermute(value, 'shard', self.up)]
    ppermute x1, waiting for transfers between devices: 31.8 us -> 15.5 us  [per_device(): piece = lax.ppermute(piece, ('seq', 'shard'), spread)]
    ppermute x32, starting transfers between devices: 13.4 us -> 29.1 us  [backward(): return lax.ppermute(value, 'shard', self.down)]
  transfers between devices with their start and end apart: 139 -> 116, of which waited for: 47 -> 49; matrix products, arithmetic and copies ran while one was open for 5% -> 3% of each run, Pallas kernels for 29% -> 39%
where the time goes in v3:
time: 706 us; the launch traced here: 693 us
  Pallas kernels  308 us (44%)
  waiting for transfers between devices  203 us (29%)
  starting transfers between devices  136 us (19%)
  local copies, waits for them, and re-layouts  33 us (5%)
  other arithmetic  10.3 us (1%)
    pallas_call x52, Pallas kernels, run(): pl.pallas_call(call, out_shape=list(outs) + [shaped((8, 128), F32)], in_s...  308 us
    ppermute x32, waiting for transfers between devices, forward(): return lax.ppermute(value, 'shard', self.up)  96.8 us
    ppermute x48, waiting for transfers between devices, swap(): return lax.ppermute(value, 'seq', [(i, i ^ bit) for i in range(count)])  77.9 us
    ppermute x48, starting transfers between devices, swap(): return lax.ppermute(value, 'seq', [(i, i ^ bit) for i in range(count)])  62.9 us
    ppermute x32, starting transfers between devices, backward(): return lax.ppermute(value, 'shard', self.down)  29.1 us
    ppermute x32, starting transfers between devices, forward(): return lax.ppermute(value, 'shard', self.up)  28.2 us
    unnamed x200, local copies, waits for them, and re-layouts  21.2 us
    ppermute x1, waiting for transfers between devices, per_device(): piece = lax.ppermute(piece, ('seq', 'shard'), spread)  15.5 us
  transfers between devices with their start and end apart: 116, of which 49 were waited for; matrix products, arithmetic and copies ran while one was open for 3% of the time, Pallas kernels for 39%

profile of v3, /device:TPU:5, one launch (start us, length us, event | category | flops | bytes accessed | tf_op | source)
XLA Modules:
  0.0 692.6 jit_solution(8873702224561084183)
XLA Ops:
  10.8 13.3 %collective-permute-done.2.refs_15_.refs_12_ = bf16[272,1280]{1,0:T(8,128)(2,1)S(1)} collective-permute-done((bf16[272,1280]{1,0:T(8,128)(2,1)}, bf16[272,1280]{1,0:T(8,128)(2,1)S(1)}, u32[]{:S(2)}, u32[]{:S(2)}) %collective-permute-start.2) | collective-permute-done | bytes 696352 | tf_op jit(solution)/shard_map/ppermute | solution.py:55
  27.1 11.6 %collective-permute-done.1.refs_3_ = bf16[144,2048]{1,0:T(8,128)(2,1)} collective-permute-done((bf16[144,2048]{1,0:T(8,128)(2,1)}, bf16[144,2048]{1,0:T(8,128)(2,1)}, u32[]{:S(2)}, u32[]{:S(2)}) %collective-permute-start.1) | collective-permute-done | bytes 589856 | tf_op jit(solution)/shard_map/ppermute | solution.py:129
  46.7 7.9 %collective-permute-done.7.refs_13_.refs_10_ = bf16[272,1280]{1,0:T(8,128)(2,1)S(1)} collective-permute-done((bf16[272,1280]{1,0:T(8,128)(2,1)}, bf16[272,1280]{1,0:T(8,128)(2,1)S(1)}, u32[]{:S(2)}, u32[]{:S(2)}) %collective-permute-start.7) | collective-permute-done | bytes 696352 | tf_op jit(solution)/shard_map/ppermute | solution.py:55
  59.4 15.5 %collective-permute-done.9.refs_2_.refs_5_ = bf16[128,2048]{1,0:T(8,128)(2,1)} collective-permute-done((bf16[128,2048]{1,0:T(8,128)(2,1)S(1)}, bf16[128,2048]{1,0:T(8,128)(2,1)}, u32[]{:S(2)}, u32[]{:S(2)}) %collective-permute-start.9) | collective-permute-done | bytes 524320 | tf_op jit(solution)/shard_map/ppermute | solution.py:405
  85.0 11.1 %shard_map.292 = (bf16[512,2048]{1,0:T(8,128)(2,1)}, f32[512,1280]{1,0:T(8,128)}, bf16[512,128]{1,0:T(8,128)(2,1)}, bf16[512,128]{1,0:T(8,128)(2,1)}, f32[512,51...) custom-call(s32[28]{0:T(128)} %concatenate.12.refs_0_, ...), custom_call_target="tpu_custom_call", output_to_operand_aliasing={{11}: (16, {})} | custom-call | flops 1048576 | bytes 65536 | tf_op jit(solution)/shard_map/pallas_call | solution.py:176
  97.7 15.5 %shard_map.293 = (bf16[512,1024]{1,0:T(8,128)(2,1)}, bf16[512,1024]{1,0:T(8,128)(2,1)}, f32[8,128]{1,0:T(8,128)}) custom-call(f32[512,1280]{1,0:T(8,128)} %get-tuple-element.404.refs_0_.refs_2_, bf16[512,128]{1,0:T(8,128)(2,1)} %get-tuple-element.405.refs_1_.refs_3_, ...), custom_call_target="tpu_custom_call", output_to_operand_aliasing={{2}: (7, {})} | custom-call | flops 1048576 | bytes 65536 | tf_op jit(solution)/shard_map/pallas_call | solution.py:176
  119.9 7.6 %all-to-all-start = ((bf16[4,200,2048]{2,1,0:T(8,128)(2,1)}), bf16[4,200,2048]{2,1,0:T(8,128)(2,1)S(1)}, u32[]{:S(2)}, u32[]{:S(2)}) async-start(bf16[4,200,2048]{2,1,0:T(8,128)(2,1)} %get-tuple-element.446), calls=%async_computation | async-start | bytes 6553600 | tf_op jit(solution)/shard_map/all_to_all | solution.py:610
  129.2 11.4 %collective-permute-done.18.refs_9_.refs_12_ = bf16[128,2048]{1,0:T(8,128)(2,1)S(1)} collective-permute-done((bf16[128,2048]{1,0:T(8,128)(2,1)}, bf16[128,2048]{1,0:T(8,128)(2,1)S(1)}, u32[]{:S(2)}, u32[]{:S(2)}) %collective-permute-start.18) | collective-permute-done | bytes 524320 | tf_op jit(solution)/shard_map/ppermute | solution.py:55
  143.9 10.6 %collective-permute-done.20.refs_8_.refs_11_ = bf16[128,2048]{1,0:T(8,128)(2,1)S(1)} collective-permute-done((bf16[128,2048]{1,0:T(8,128)(2,1)S(1)}, bf16[128,2048]{1,0:T(8,128)(2,1)S(1)}, u32[]{:S(2)}, u32[]{:S(2)}) %collective-permute-start.20) | collective-permute-done | bytes 524320 | tf_op jit(solution)/shard_map/ppermute | solution.py:55
  162.6 8.0 %shard_map.295 = (bf16[128,2048]{1,0:T(8,128)(2,1)}, bf16[128,2048]{1,0:T(8,128)(2,1)}, f32[128,2048]{1,0:T(8,128)}, f32[128,2048]{1,0:T(8,128)}, f32[8,128]{1,0:T(8,128)}) custom-call(s32[28]{0:T(128)} %concatenate.12.refs_0_, bf16[512,1024]{1,0:T(8,128)(2,1)} %get-tuple-element.412.refs_1_, ...), custom_call_target="tpu_custom_call", output_to_operand_aliasing={{4}: (11, {})} | custom-call | flops 1048576 | bytes 65536 | tf_op jit(solution)/shard_map/pallas_call | solution.py:176
  179.8 7.6 %collective-permute-done.27.refs_3_ = bf16[128,2048]{1,0:T(8,128)(2,1)} collective-permute-done((bf16[128,2048]{1,0:T(8,128)(2,1)}, bf16[128,2048]{1,0:T(8,128)(2,1)}, u32[]{:S(2)}, u32[]{:S(2)}) %collective-permute-start.27) | collective-permute-done | bytes 524320 | tf_op jit(solution)/shard_map/ppermute | solution.py:55
  226.9 10.1 %collective-permute-done.37.refs_8_ = bf16[136,2048]{1,0:T(8,128)(2,1)} collective-permute-done((bf16[136,2048]{1,0:T(8,128)(2,1)}, bf16[136,2048]{1,0:T(8,128)(2,1)}, u32[]{:S(2)}, u32[]{:S(2)}) %collective-permute-start.37) | collective-permute-done | bytes 557088 | tf_op jit(solution)/shard_map/ppermute | solution.py:129
  241.6 6.8 collective-permute-done.41.refs_7_
  248.4 12.0 %collective-permute-done.42.refs_8_ = bf16[136,2048]{1,0:T(8,128)(2,1)} collective-permute-done((bf16[136,2048]{1,0:T(8,128)(2,1)}, bf16[136,2048]{1,0:T(8,128)(2,1)}, u32[]{:S(2)}, u32[]{:S(2)}) %collective-permute-start.42) | collective-permute-done | bytes 557088 | tf_op jit(solution)/shard_map/ppermute | solution.py:129
  273.5 7.4 %shard_map.302 = (f32[8,8,128]{2,1,0:T(8,128)}, f32[128,128]{1,0:T(8,128)}, f32[4,8,40]{2,1,0:T(8,128)}, f32[8,128]{1,0:T(8,128)}) custom-call(s32[28]{0:T(128)} %concatenate.12.refs_0_, bf16[128,2048]{1,0:T(8,128)(2,1)} %get-tuple-element.460.refs_4_.refs_1_.refs_7_, bf16[128,2048]{1,0:T(8,128)(2,1)} %copy-done.19, ...), custom_call_target="tpu_custom_call", output_to_operand_aliasing={{3}: (13, {})} | custom-call | flops 1048576 | bytes 65536 | tf_op jit(solution)/shard_map/pallas_call | solution.py:176
  287.5 28.3 %shard_map.303 = (bf16[80,2176]{1,0:T(8,128)(2,1)}, bf16[80,2176]{1,0:T(8,128)(2,1)}, bf16[80,2176]{1,0:T(8,128)(2,1)}, bf16[80,2176]{1,0:T(8,128)(2,1)}, bf16[1...) custom-call(s32[28]{0:T(128)} %concatenate.12.refs_0_, ...), custom_call_target="tpu_custom_call", output_to_operand_aliasing={{14}: (13, {})} | custom-call | flops 1048576 | bytes 65536 | tf_op jit(solution)/shard_map/pallas_call | solution.py:176
  319.3 19.4 %shard_map.304 = (bf16[120,2176]{1,0:T(8,128)(2,1)}, bf16[120,2176]{1,0:T(8,128)(2,1)}, bf16[120,2176]{1,0:T(8,128)(2,1)}, bf16[120,2176]{1,0:T(8,128)(2,1)}, bf...) custom-call(s32[28]{0:T(128)} %concatenate.12.refs_0_, ...), custom_call_target="tpu_custom_call", output_to_operand_aliasing={{13}: (12, {})} | custom-call | flops 1048576 | bytes 65536 | tf_op jit(solution)/shard_map/pallas_call | solution.py:176
  347.9 12.4 %shard_map.306 = (f32[2048,768]{1,0:T(8,128)}, f32[8,128]{1,0:T(8,128)}) custom-call(f32[4,200]{1,0:T(4,128)} %pad_maximum_fusion.2.refs_0_, f32[4,120]{1,0:T(4,128)} %pad_maximum_fusion.7.refs_1_, bf16[832,2048]{1,0:T(8,128)(2,1)} %get-tuple-element.537.refs_2_, bf16[512,2048]{1,0:T(8,128)(2,1)} %get-tuple-element.538.refs_3_, ...), custom_call_target="tpu_custom_call", output_to_operand_aliasing={{1}: (6, {})} | custom-call | flops 1048576 | bytes 65536 | tf_op jit(solution)/shard_map/pallas_call | solution.py:176
  385.3 12.4 %shard_map.310 = (f32[2048,768]{1,0:T(8,128)}, f32[8,128]{1,0:T(8,128)}) custom-call(f32[4,200]{1,0:T(4,128)} %pad_maximum_fusion.2.refs_0_, f32[4,120]{1,0:T(4,128)} %pad_maximum_fusion.7.refs_1_, bf16[832,2048]{1,0:T(8,128)(2,1)} %get-tuple-element.537.refs_2_, bf16[512,2048]{1,0:T(8,128)(2,1)} %get-tuple-element.538.refs_3_, ...), custom_call_target="tpu_custom_call", output_to_operand_aliasing={{1}: (6, {})} | custom-call | flops 1048576 | bytes 65536 | tf_op jit(solution)/shard_map/pallas_call | solution.py:176
  409.9 12.3 %shard_map.312 = (f32[768,2048]{1,0:T(8,128)}, f32[8,128]{1,0:T(8,128)}) custom-call(f32[4,200]{1,0:T(4,128)} %pad_maximum_fusion.2.refs_0_, f32[4,120]{1,0:T(4,128)} %pad_maximum_fusion.7.refs_1_, bf16[832,768]{1,0:T(8,128)(2,1)} %get-tuple-element.570.refs_2_, bf16[512,768]{1,0:T(8,128)(2,1)} %get-tuple-element.571.refs_3_, ...), custom_call_target="tpu_custom_call", output_to_operand_aliasing={{1}: (6, {})} | custom-call | flops 1048576 | bytes 65536 | tf_op jit(solution)/shard_map/pallas_call | solution.py:176
  427.6 8.6 %collective-permute-done.73.refs_6_ = bf16[144,2048]{1,0:T(8,128)(2,1)S(1)} collective-permute-done((bf16[144,2048]{1,0:T(8,128)(2,1)S(1)}, bf16[144,2048]{1,0:T(8,128)(2,1)S(1)}, u32[]{:S(2)}, u32[]{:S(2)}) %collective-permute-start.73) | collective-permute-done | bytes 589856 | tf_op jit(solution)/shard_map/ppermute | solution.py:129
  464.6 7.6 %shard_map.317 = (f32[136,2048]{1,0:T(8,128)}, f32[136,2048]{1,0:T(8,128)}, f32[136,2048]{1,0:T(8,128)}, f32[136,2048]{1,0:T(8,128)}, f32[136,2048]{1,0:T(8,128)...) custom-call(s32[28]{0:T(128)} %concatenate.12.refs_0_, ...), custom_call_target="tpu_custom_call", output_to_operand_aliasing={{9}: (7, {})} | custom-call | flops 1048576 | bytes 65536 | tf_op jit(solution)/shard_map/pallas_call | solution.py:176
  473.7 7.9 %shard_map.318 = (bf16[512,1024]{1,0:T(8,128)(2,1)}, f32[8,128]{1,0:T(8,128)}) custom-call(s32[28]{0:T(128)} %concatenate.12.refs_0_, bf16[128,2048]{1,0:T(8,128)(2,1)} %get-tuple-element.594.refs_2_.refs_1_, bf16[128,2048]{1,0:T(8,128)(2,1)} %copy-done.16, bf16[128,2048]{1,0:T(8,128)(2,1)} %copy-done.15, ...), custom_call_target="tpu_custom_call", output_to_operand_aliasing={{1}: (14, {})} | custom-call | flops 1048576 | bytes 65536 | tf_op jit(solution)/shard_map/pallas_call | solution.py:176
  488.9 11.1 %shard_map.320 = (bf16[512,512]{1,0:T(8,128)(2,1)}, f32[512,128]{1,0:T(8,128)}, f32[512,128]{1,0:T(8,128)}, f32[8,128]{1,0:T(8,128)}, f32[8,128]{1,0:T(8,128)}) custom-call(f32[512,1280]{1,0:T(8,128)} %get-tuple-element.404.refs_0_.refs_2_, bf16[512,1024]{1,0:T(8,128)(2,1)} %get-tuple-element.625.refs_1_, ...), custom_call_target="tpu_custom_call", output_to_operand_aliasing={{4}: (12, {})} | custom-call | flops 1048576 | bytes 65536 | tf_op jit(solution)/shard_map/pallas_call | solution.py:176
  505.6 11.1 %shard_map.322 = (bf16[512,512]{1,0:T(8,128)(2,1)}, f32[512,128]{1,0:T(8,128)}, f32[512,128]{1,0:T(8,128)}, f32[8,128]{1,0:T(8,128)}, f32[8,128]{1,0:T(8,128)}) custom-call(f32[512,1280]{1,0:T(8,128)} %get-tuple-element.404.refs_0_.refs_2_, bf16[512,1024]{1,0:T(8,128)(2,1)} %get-tuple-element.625.refs_1_, ...), custom_call_target="tpu_custom_call", output_to_operand_aliasing={{4}: (12, {})} | custom-call | flops 1048576 | bytes 65536 | tf_op jit(solution)/shard_map/pallas_call | solution.py:176
  522.3 7.0 %all-to-all-start.1 = ((bf16[4,200,2048]{2,1,0:T(8,128)(2,1)}), bf16[4,200,2048]{2,1,0:T(8,128)(2,1)S(1)}, u32[]{:S(2)}, u32[]{:S(2)}) async-start(bf16[4,200,2048]{2,1,0:T(8,128)(2,1)} %get-tuple-element.602), calls=%async_computation.1 | async-start | bytes 6553600 | tf_op jit(solution)/shard_map/all_to_all | solution.py:610
  555.4 6.6 shard_map.329
  562.0 9.0 %shard_map.330 = (bf16[128,2048]{1,0:T(8,128)(2,1)}, bf16[128,2048]{1,0:T(8,128)(2,1)}, f32[128,2048]{1,0:T(8,128)}, f32[128,2048]{1,0:T(8,128)}, f32[8,128]{1,0:T(8,128)}) custom-call(s32[28]{0:T(128)} %concatenate.12.refs_0_, bf16[512,512]{1,0:T(8,128)(2,1)} %get-tuple-element.647.refs_2_.refs_1_, ...), custom_call_target="tpu_custom_call", output_to_operand_aliasing={{4}: (13, {})} | custom-call | flops 1048576 | bytes 65536 | tf_op jit(solution)/shard_map/pallas_call | solution.py:176
  576.9 13.2 %collective-permute-start.98 = (bf16[128,2048]{1,0:T(8,128)(2,1)}, bf16[128,2048]{1,0:T(8,128)(2,1)}, u32[]{:S(2)}, u32[]{:S(2)}) collective-permute-start(bf16[128,2048]{1,0:T(8,128)(2,1)} %get-tuple-element.675), channel_id=1, source_target_pairs={{0,8},{8,0},{16,24},{24,16},{1,9},{9,1},{17,25},{25,17},{2,10},{10... | collective-permute-start | bytes 1572872 | tf_op jit(solution)/shard_map/ppermute | solution.py:129
  618.3 6.1 shard_map.334
  640.8 12.3 %collective-permute-done.109.refs_3_ = bf16[264,1280]{1,0:T(8,128)(2,1)S(1)} collective-permute-done((bf16[264,1280]{1,0:T(8,128)(2,1)}, bf16[264,1280]{1,0:T(8,128)(2,1)S(1)}, u32[]{:S(2)}, u32[]{:S(2)}) %collective-permute-start.109) | collective-permute-done | bytes 675872 | tf_op jit(solution)/shard_map/ppermute | solution.py:129
  657.8 11.3 %collective-permute-done.107.refs_1_ = bf16[128,2048]{1,0:T(8,128)(2,1)S(1)} collective-permute-done((bf16[128,2048]{1,0:T(8,128)(2,1)}, bf16[128,2048]{1,0:T(8,128)(2,1)S(1)}, u32[]{:S(2)}, u32[]{:S(2)}) %collective-permute-start.107) | collective-permute-done | bytes 524320 | tf_op jit(solution)/shard_map/ppermute | solution.py:55
  (518 shorter events, 337.6 us)
Async XLA Ops:
  45.5 29.3 %collective-permute-start.9 = (bf16[128,2048]{1,0:T(8,128)(2,1)S(1)}, bf16[128,2048]{1,0:T(8,128)(2,1)}, u32[]{:S(2)}, u32[]{:S(2)}) collective-permute-start(bf16[128,2048]{1,0:T(8,128)(2,1)S(1)} %constant_dynamic-slice_fusion), channel_id=1, source_target_pairs={{8,0},{9,1},{24,2},{25,3},{0,4},{1,5},{16,6},{17,7},{10,8},{11,9},... | collective-permute-start | bytes 1572872 | tf_op jit(solution)/shard_map/ppermute | solution.py:405
  55.7 24.7 %collective-permute-start.10 = (bf16[128,1280]{1,0:T(8,128)(2,1)S(1)}, bf16[128,1280]{1,0:T(8,128)(2,1)S(1)}, u32[]{:S(2)}, u32[]{:S(2)}) collective-permute-start(bf16[128,1280]{1,0:T(8,128)(2,1)S(1)} %slice.192), channel_id=1, source_target_pairs={{0,2},{2,4},{4,6},{6,7},{7,5},{5,3},{3,1},{1,0},{8,10},{10,12},{12... | collective-permute-start | bytes 983048 | tf_op jit(solution)/shard_map/ppermute | solution.py:55
  57.1 23.3 %collective-permute-start.11 = (bf16[144,1280]{1,0:T(8,128)(2,1)S(1)}, bf16[144,1280]{1,0:T(8,128)(2,1)S(1)}, u32[]{:S(2)}, u32[]{:S(2)}) collective-permute-start(bf16[144,1280]{1,0:T(8,128)(2,1)S(1)} %slice.193), channel_id=1, source_target_pairs={{2,0},{4,2},{6,4},{7,6},{5,7},{3,5},{1,3},{0,1},{10,8},{12,10},{14... | collective-permute-start | bytes 1105928 | tf_op jit(solution)/shard_map/ppermute | solution.py:58
  119.9 59.9 %all-to-all-start = ((bf16[4,200,2048]{2,1,0:T(8,128)(2,1)}), bf16[4,200,2048]{2,1,0:T(8,128)(2,1)S(1)}, u32[]{:S(2)}, u32[]{:S(2)}) async-start(bf16[4,200,2048]{2,1,0:T(8,128)(2,1)} %get-tuple-element.446), calls=%async_computation | async-start | bytes 6553600 | tf_op jit(solution)/shard_map/all_to_all | solution.py:610
  179.6 22.6 %collective-permute-start.26 = (bf16[128,2048]{1,0:T(8,128)(2,1)}, bf16[128,2048]{1,0:T(8,128)(2,1)}, u32[]{:S(2)}, u32[]{:S(2)}) collective-permute-start(bf16[128,2048]{1,0:T(8,128)(2,1)} %get-tuple-element.443), channel_id=1, source_target_pairs={{0,16},{8,24},{16,0},{24,8},{1,17},{9,25},{17,1},{25,9},{2,18},{10... | collective-permute-start | bytes 1572872 | tf_op jit(solution)/shard_map/ppermute | solution.py:129
  210.5 26.5 %collective-permute-start.37 = (bf16[136,2048]{1,0:T(8,128)(2,1)}, bf16[136,2048]{1,0:T(8,128)(2,1)}, u32[]{:S(2)}, u32[]{:S(2)}) collective-permute-start(bf16[136,2048]{1,0:T(8,128)(2,1)} %get-tuple-element.466), channel_id=1, source_target_pairs={{0,24},{8,16},{16,8},{24,0},{1,25},{9,17},{17,9},{25,1},{2,26},{10... | collective-permute-start | bytes 1671176 | tf_op jit(solution)/shard_map/ppermute | solution.py:129
  226.1 22.4 %collective-permute-start.41 = (bf16[136,2048]{1,0:T(8,128)(2,1)}, bf16[136,2048]{1,0:T(8,128)(2,1)}, u32[]{:S(2)}, u32[]{:S(2)}) collective-permute-start(bf16[136,2048]{1,0:T(8,128)(2,1)} %get-tuple-element.473), channel_id=1, source_target_pairs={{0,16},{8,24},{16,0},{24,8},{1,17},{9,25},{17,1},{25,9},{2,18},{10... | collective-permute-start | bytes 1671176 | tf_op jit(solution)/shard_map/ppermute | solution.py:129
  237.0 23.5 %collective-permute-start.42 = (bf16[136,2048]{1,0:T(8,128)(2,1)}, bf16[136,2048]{1,0:T(8,128)(2,1)}, u32[]{:S(2)}, u32[]{:S(2)}) collective-permute-start(bf16[136,2048]{1,0:T(8,128)(2,1)} %get-tuple-element.474), channel_id=1, source_target_pairs={{0,24},{8,16},{16,8},{24,0},{1,25},{9,17},{17,9},{25,1},{2,26},{10... | collective-permute-start | bytes 1671176 | tf_op jit(solution)/shard_map/ppermute | solution.py:129
  237.3 23.2 %collective-permute-start.38 = (bf16[128,2048]{1,0:T(8,128)(2,1)S(1)}, bf16[128,2048]{1,0:T(8,128)(2,1)S(1)}, u32[]{:S(2)}, u32[]{:S(2)}) collective-permute-start(bf16[128,2048]{1,0:T(8,128)(2,1)S(1)} %collective-permute-done.33.refs_3_.refs_8_), channel_id=1, source_target_pairs={{0,2},{2,4},{4,6},{6,7},{7,5},{5,3},{3,1},{1,0},{8,10},{10,12},{12... | collective-permute-start | bytes 1572872 | tf_op jit(solution)/shard_map/ppermute | solution.py:55
  237.8 22.7 %collective-permute-start.39 = (bf16[128,2048]{1,0:T(8,128)(2,1)S(1)}, bf16[128,2048]{1,0:T(8,128)(2,1)S(1)}, u32[]{:S(2)}, u32[]{:S(2)}) collective-permute-start(bf16[128,2048]{1,0:T(8,128)(2,1)S(1)} %collective-permute-done.34.refs_2_.refs_3_), channel_id=1, source_target_pairs={{2,0},{4,2},{6,4},{7,6},{5,7},{3,5},{1,3},{0,1},{10,8},{12,10},{14... | collective-permute-start | bytes 1572872 | tf_op jit(solution)/shard_map/ppermute | solution.py:58
  262.1 22.1 %collective-permute-start.45 = (bf16[80,2048]{1,0:T(8,128)(2,1)}, bf16[80,2048]{1,0:T(8,128)(2,1)S(1)}, u32[]{:S(2)}, u32[]{:S(2)}) collective-permute-start(bf16[80,2048]{1,0:T(8,128)(2,1)} %get-tuple-element.489), channel_id=1, source_target_pairs={{0,8},{8,0},{16,24},{24,16},{1,9},{9,1},{17,25},{25,17},{2,10},{10... | collective-permute-start | bytes 983048 | tf_op jit(solution)/shard_map/ppermute | solution.py:129
  263.0 21.6 %collective-permute-start.46 = (bf16[80,2048]{1,0:T(8,128)(2,1)}, bf16[80,2048]{1,0:T(8,128)(2,1)S(1)}, u32[]{:S(2)}, u32[]{:S(2)}) collective-permute-start(bf16[80,2048]{1,0:T(8,128)(2,1)} %get-tuple-element.490), channel_id=1, source_target_pairs={{0,16},{8,24},{16,0},{24,8},{1,17},{9,25},{17,1},{25,9},{2,18},{10... | collective-permute-start | bytes 983048 | tf_op jit(solution)/shard_map/ppermute | solution.py:129
  263.5 22.1 %collective-permute-start.47 = (bf16[80,2048]{1,0:T(8,128)(2,1)}, bf16[80,2048]{1,0:T(8,128)(2,1)S(1)}, u32[]{:S(2)}, u32[]{:S(2)}) collective-permute-start(bf16[80,2048]{1,0:T(8,128)(2,1)} %get-tuple-element.491), channel_id=1, source_target_pairs={{0,24},{8,16},{16,8},{24,0},{1,25},{9,17},{17,9},{25,1},{2,26},{10... | collective-permute-start | bytes 983048 | tf_op jit(solution)/shard_map/ppermute | solution.py:129
  284.2 32.6 %collective-permute-start.53 = (bf16[120,2048]{1,0:T(8,128)(2,1)}, bf16[120,2048]{1,0:T(8,128)(2,1)S(1)}, u32[]{:S(2)}, u32[]{:S(2)}) collective-permute-start(bf16[120,2048]{1,0:T(8,128)(2,1)} %get-tuple-element.510), channel_id=1, source_target_pairs={{0,8},{8,0},{16,24},{24,16},{1,9},{9,1},{17,25},{25,17},{2,10},{10... | collective-permute-start | bytes 1474568 | tf_op jit(solution)/shard_map/ppermute | solution.py:129
  284.6 32.7 %collective-permute-start.54 = (bf16[120,2048]{1,0:T(8,128)(2,1)}, bf16[120,2048]{1,0:T(8,128)(2,1)S(1)}, u32[]{:S(2)}, u32[]{:S(2)}) collective-permute-start(bf16[120,2048]{1,0:T(8,128)(2,1)} %get-tuple-element.511), channel_id=1, source_target_pairs={{0,16},{8,24},{16,0},{24,8},{1,17},{9,25},{17,1},{25,9},{2,18},{10... | collective-permute-start | bytes 1474568 | tf_op jit(solution)/shard_map/ppermute | solution.py:129
  285.6 32.9 %collective-permute-start.55 = (bf16[120,2048]{1,0:T(8,128)(2,1)}, bf16[120,2048]{1,0:T(8,128)(2,1)S(1)}, u32[]{:S(2)}, u32[]{:S(2)}) collective-permute-start(bf16[120,2048]{1,0:T(8,128)(2,1)} %get-tuple-element.512), channel_id=1, source_target_pairs={{0,24},{8,16},{16,8},{24,0},{1,25},{9,17},{17,9},{25,1},{2,26},{10... | collective-permute-start | bytes 1474568 | tf_op jit(solution)/shard_map/ppermute | solution.py:129
  286.7 31.9 %collective-permute-start.56 = (f32[8,40]{1,0:T(8,128)S(1)}, f32[8,40]{1,0:T(8,128)S(1)}, u32[]{:S(2)}, u32[]{:S(2)}) collective-permute-start(f32[8,40]{1,0:T(8,128)S(1)} %get-tuple-element.750), channel_id=1, source_target_pairs={{0,24},{8,16},{16,8},{24,0},{1,25},{9,17},{17,9},{25,1},{2,26},{10... | collective-permute-start | bytes 3848 | tf_op jit(solution)/shard_map/ppermute | solution.py:129
  315.8 23.7 %collective-permute-start.50 = (bf16[120,2176]{1,0:T(8,128)(2,1)}, bf16[120,2176]{1,0:T(8,128)(2,1)S(1)}, u32[]{:S(2)}, u32[]{:S(2)}) collective-permute-start(bf16[120,2176]{1,0:T(8,128)(2,1)} %get-tuple-element.506), channel_id=1, source_target_pairs={{0,8},{8,0},{16,24},{24,16},{1,9},{9,1},{17,25},{25,17},{2,10},{10... | collective-permute-start | bytes 1566728 | tf_op jit(solution)/shard_map/ppermute | solution.py:129
  316.8 25.5 %collective-permute-start.51 = (bf16[120,2176]{1,0:T(8,128)(2,1)}, bf16[120,2176]{1,0:T(8,128)(2,1)S(1)}, u32[]{:S(2)}, u32[]{:S(2)}) collective-permute-start(bf16[120,2176]{1,0:T(8,128)(2,1)} %get-tuple-element.507), channel_id=1, source_target_pairs={{0,16},{8,24},{16,0},{24,8},{1,17},{9,25},{17,1},{25,9},{2,18},{10... | collective-permute-start | bytes 1566728 | tf_op jit(solution)/shard_map/ppermute | solution.py:129
  317.3 25.0 %collective-permute-start.52 = (bf16[120,2176]{1,0:T(8,128)(2,1)}, bf16[120,2176]{1,0:T(8,128)(2,1)S(1)}, u32[]{:S(2)}, u32[]{:S(2)}) collective-permute-start(bf16[120,2176]{1,0:T(8,128)(2,1)} %get-tuple-element.508), channel_id=1, source_target_pairs={{0,24},{8,16},{16,8},{24,0},{1,25},{9,17},{17,9},{25,1},{2,26},{10... | collective-permute-start | bytes 1566728 | tf_op jit(solution)/shard_map/ppermute | solution.py:129
  338.7 21.6 %collective-permute-start.57 = (bf16[120,2176]{1,0:T(8,128)(2,1)}, bf16[120,2176]{1,0:T(8,128)(2,1)S(1)}, u32[]{:S(2)}, u32[]{:S(2)}) collective-permute-start(bf16[120,2176]{1,0:T(8,128)(2,1)} %get-tuple-element.531), channel_id=1, source_target_pairs={{0,8},{8,0},{16,24},{24,16},{1,9},{9,1},{17,25},{25,17},{2,10},{10... | collective-permute-start | bytes 1566728 | tf_op jit(solution)/shard_map/ppermute | solution.py:129
  339.0 21.3 %collective-permute-start.58 = (bf16[120,2176]{1,0:T(8,128)(2,1)}, bf16[120,2176]{1,0:T(8,128)(2,1)S(1)}, u32[]{:S(2)}, u32[]{:S(2)}) collective-permute-start(bf16[120,2176]{1,0:T(8,128)(2,1)} %get-tuple-element.532), channel_id=1, source_target_pairs={{0,16},{8,24},{16,0},{24,8},{1,17},{9,25},{17,1},{25,9},{2,18},{10... | collective-permute-start | bytes 1566728 | tf_op jit(solution)/shard_map/ppermute | solution.py:129
  339.5 24.7 %collective-permute-start.59 = (bf16[120,2176]{1,0:T(8,128)(2,1)}, bf16[120,2176]{1,0:T(8,128)(2,1)S(1)}, u32[]{:S(2)}, u32[]{:S(2)}) collective-permute-start(bf16[120,2176]{1,0:T(8,128)(2,1)} %get-tuple-element.533), channel_id=1, source_target_pairs={{0,24},{8,16},{16,8},{24,0},{1,25},{9,17},{17,9},{25,1},{2,26},{10... | collective-permute-start | bytes 1566728 | tf_op jit(solution)/shard_map/ppermute | solution.py:129
  408.7 27.5 %collective-permute-start.73 = (bf16[144,2048]{1,0:T(8,128)(2,1)S(1)}, bf16[144,2048]{1,0:T(8,128)(2,1)S(1)}, u32[]{:S(2)}, u32[]{:S(2)}) collective-permute-start(bf16[144,2048]{1,0:T(8,128)(2,1)S(1)} %copy-done.91), channel_id=1, source_target_pairs={{0,24},{8,16},{16,8},{24,0},{1,25},{9,17},{17,9},{25,1},{2,26},{10... | collective-permute-start | bytes 1769480 | tf_op jit(solution)/shard_map/ppermute | solution.py:129
  522.3 94.3 %all-to-all-start.1 = ((bf16[4,200,2048]{2,1,0:T(8,128)(2,1)}), bf16[4,200,2048]{2,1,0:T(8,128)(2,1)S(1)}, u32[]{:S(2)}, u32[]{:S(2)}) async-start(bf16[4,200,2048]{2,1,0:T(8,128)(2,1)} %get-tuple-element.602), calls=%async_computation.1 | async-start | bytes 6553600 | tf_op jit(solution)/shard_map/all_to_all | solution.py:610
  554.4 35.7 %collective-permute-start.89 = (bf16[128,2048]{1,0:T(8,128)(2,1)}, bf16[128,2048]{1,0:T(8,128)(2,1)S(1)}, u32[]{:S(2)}, u32[]{:S(2)}) collective-permute-start(bf16[128,2048]{1,0:T(8,128)(2,1)} %get-tuple-element.645), channel_id=1, source_target_pairs={{0,8},{1,9},{2,24},{3,25},{4,0},{5,1},{6,16},{7,17},{8,10},{9,11},... | collective-permute-start | bytes 1572872 | tf_op jit(solution)/shard_map/ppermute | solution.py:1338
  574.4 24.6 %collective-permute-start.94 = (bf16[264,1280]{1,0:T(8,128)(2,1)}, bf16[264,1280]{1,0:T(8,128)(2,1)}, u32[]{:S(2)}, u32[]{:S(2)}) collective-permute-start(bf16[264,1280]{1,0:T(8,128)(2,1)} %get-tuple-element.670), channel_id=1, source_target_pairs={{0,2},{2,4},{4,6},{6,7},{7,5},{5,3},{3,1},{1,0},{8,10},{10,12},{12... | collective-permute-start | bytes 2027528 | tf_op jit(solution)/shard_map/ppermute | solution.py:55
  574.5 24.5 %collective-permute-start.95 = (bf16[264,1280]{1,0:T(8,128)(2,1)}, bf16[264,1280]{1,0:T(8,128)(2,1)}, u32[]{:S(2)}, u32[]{:S(2)}) collective-permute-start(bf16[264,1280]{1,0:T(8,128)(2,1)} %get-tuple-element.672), channel_id=1, source_target_pairs={{2,0},{4,2},{6,4},{7,6},{5,7},{3,5},{1,3},{0,1},{10,8},{12,10},{14... | collective-permute-start | bytes 2027528 | tf_op jit(solution)/shard_map/ppermute | solution.py:58
  602.3 30.6 %collective-permute-start.100 = (bf16[264,1280]{1,0:T(8,128)(2,1)}, bf16[264,1280]{1,0:T(8,128)(2,1)}, u32[]{:S(2)}, u32[]{:S(2)}) collective-permute-start(bf16[264,1280]{1,0:T(8,128)(2,1)} %get-tuple-element.693), channel_id=1, source_target_pairs={{0,2},{2,4},{4,6},{6,7},{7,5},{5,3},{3,1},{1,0},{8,10},{10,12},{12... | collective-permute-start | bytes 2027528 | tf_op jit(solution)/shard_map/ppermute | solution.py:55
  603.6 29.4 %collective-permute-start.101 = (bf16[264,1280]{1,0:T(8,128)(2,1)}, bf16[264,1280]{1,0:T(8,128)(2,1)}, u32[]{:S(2)}, u32[]{:S(2)}) collective-permute-start(bf16[264,1280]{1,0:T(8,128)(2,1)} %get-tuple-element.694), channel_id=1, source_target_pairs={{2,0},{4,2},{6,4},{7,6},{5,7},{3,5},{1,3},{0,1},{10,8},{12,10},{14... | collective-permute-start | bytes 2027528 | tf_op jit(solution)/shard_map/ppermute | solution.py:58
  637.4 38.5 %collective-permute-start.112 = (bf16[264,1280]{1,0:T(8,128)(2,1)}, bf16[264,1280]{1,0:T(8,128)(2,1)S(1)}, u32[]{:S(2)}, u32[]{:S(2)}) collective-permute-start(bf16[264,1280]{1,0:T(8,128)(2,1)} %get-tuple-element.714.refs_1_), channel_id=1, source_target_pairs={{0,8},{8,0},{16,24},{24,16},{1,9},{9,1},{17,25},{25,17},{2,10},{10... | collective-permute-start | bytes 2027528 | tf_op jit(solution)/shard_map/ppermute | solution.py:129
  653.1 22.9 %collective-permute-start.113 = (bf16[264,1280]{1,0:T(8,128)(2,1)S(1)}, bf16[264,1280]{1,0:T(8,128)(2,1)S(1)}, u32[]{:S(2)}, u32[]{:S(2)}) collective-permute-start(bf16[264,1280]{1,0:T(8,128)(2,1)S(1)} %collective-permute-done.109.refs_3_), channel_id=1, source_target_pairs={{0,8},{8,0},{16,24},{24,16},{1,9},{9,1},{17,25},{25,17},{2,10},{10... | collective-permute-start | bytes 2027528 | tf_op jit(solution)/shard_map/ppermute | solution.py:129
  (184 other events, 1787.0 us)

commit v4 on v3

--- a/solution.py
+++ b/solution.py
@@ -18,6 +18,7 @@
 BF = jnp.bfloat16
 F32 = jnp.float32
 I32 = jnp.int32
+LIMIT = 8
 
 
 def ring_order(count):
@@ -160,7 +161,7 @@
         *arrays, self.token = lax.optimization_barrier(tuple(arrays) + (self.token,))
         return arrays
 
-    def run(self, body, outs, operands, scratch=()):
+    def run(self, body, outs, operands, scratch=(), alone=False):
         spaces = {"s": pltpu.SMEM, "a": pl.ANY, "v": pltpu.VMEM}
         specs, arrays = [], []
         for item in list(operands) + [("a", self.token)]:
@@ -168,6 +169,14 @@
             specs.append(pl.BlockSpec(memory_space=spaces[kind]))
             arrays.append(array)
         given, made = len(operands), len(outs)
+        need = 0
+        for spec, array in list(zip(specs, arrays)) + [(None, o) for o in outs]:
+            if spec is None or spec.memory_space == pltpu.VMEM:
+                need += array.size * array.dtype.itemsize
+        for item in scratch:
+            if getattr(item, "memory_space", None) == pltpu.VMEM:
+                need += int(np.prod(item.shape)) * jnp.dtype(item.dtype).itemsize
+        limit = 60 << 20 if alone else min(60 << 20, need * 3 // 2 + (LIMIT << 20))
 
         def call(*refs):
             rest = refs[given + 1 :]
@@ -181,7 +190,7 @@
             + [pl.BlockSpec(memory_space=pl.ANY)],
             scratch_shapes=list(scratch),
             input_output_aliases={given: made},
-            compiler_params=pltpu.CompilerParams(vmem_limit_bytes=60 << 20),
+            compiler_params=pltpu.CompilerParams(vmem_limit_bytes=limit),
             cost_estimate=pl.CostEstimate(
                 flops=1 << 20, bytes_accessed=1 << 16, transcendentals=0
             ),
@@ -378,6 +387,7 @@
             routes[0].T,
         ],
         [pltpu.SemaphoreType.DMA((3,))],
+        alone=True,
     )
     first = Gather(ring, chain, block)
     IR = 16
@@ -543,6 +553,7 @@
             pltpu.SemaphoreType.DMA((N, 2)),
             pltpu.SemaphoreType.DMA((N,)),
         ],
+        alone=True,
     )
 
     def attend_body(raw, krot, vlow, bias_, gq, cos, sin, rot, out):
@@ -717,8 +728,6 @@
     x2_own, x2_got = seq_reduce(make_output)
     (dy_near,) = gate(dy_near)
     dy.step()
-    dy.finish()
-    picked = select(dy.blocks, [far], longer)
     (x2_got,) = gate(x2_got)
 
     def second_body(x, own, got, g2, x2_out, h2_out):
@@ -732,27 +741,183 @@
         [inputs[0], x2_own, x2_got, gain_two],
     )
 
+    dy.finish()
+    (h2,) = gate(h2)
     walk = Gather(ring, chain, h2)
-    dy_far = exchange(picked)
+    dy_far = exchange(select(dy.blocks, [far], longer))
     h2_near = [None] * (len(near_pairs))
-    for j in range(1, half):
+    walk.step()
+    picked = select(walk.blocks, [near_pairs[-1], [0]], longer)
+    arrive(dy_far)
+    moving = h2_near[-1] = exchange(picked)
+    for j in range(2, half):
         walk.step()
-        if j == 1:
-            picked = select(walk.blocks, [near_pairs[-1], [0]], longer)
-            arrive(dy_far)
-            moving = h2_near[-1] = exchange(picked)
-        elif j < half - 1:
-            picked = select(walk.blocks, [[j, N - j]])
-            arrive(moving)
-            moving = h2_near[half - 2 - j] = exchange(picked)
+        if j < half - 1:
+            (picked,) = select(walk.blocks, [[j, N - j]], joint=True)
+            if j == half - 2:
+                walk.step()
+            if j == 2:
+                arrive(moving)
+            else:
+                (h2_near[half - 1 - j],) = gate(h2_near[half - 1 - j])
+            (picked,) = gate(picked)
+            h2_near[half - 2 - j] = all_to_all(picked)
+            if j == half - 2:
+                break
     walk.finish()
-    picked = select(walk.blocks, [far])
+    h2_far = exchange(gate(*select(walk.blocks, [far])))
+
+    gate_w, up_w, down_w = w_gate[0], w_up[0], w_down[0]
+
+    def expert(x_parts, y_parts, back_sizes, front_rows=0, joint=False):
+        x_used = [slice(low, low + used) for _, used, low in x_parts]
+        y_used = [slice(low, low + used) for _, used, low in y_parts]
+        size = sum(used for _, used, _ in x_parts)
+        x_parts = [part for part, _, _ in x_parts]
+        y_parts = [part for part, _, _ in y_parts]
+        pad = -(-size // 16) * 16
+        rows = S * pad
+        starts = np.cumsum([0] + list(back_sizes))
+        front_count = 1 if joint else S
+
+        def body(*refs):
+            mt, rest = refs[0], refs[1:]
+            xs = regroup(rest, x_parts)
+            rest = rest[sum(len(p) for p in x_parts) :]
+            ys = regroup(rest, y_parts)
+            rest = rest[sum(len(p) for p in y_parts) :]
+            wg_in, wu_in, wd_in = rest[:3]
+            rest = rest[3:]
+            outs = [rest[i * S : (i + 1) * S] for i in range(len(back_sizes))]
+            rest = rest[S * len(back_sizes) :]
+            fronts, rest = rest[:front_count], rest[front_count:]
+            xp, yp, hid, dg_out, du_out, sums, wg, wu, wd, sems = rest
+
+            def copies(i):
+                lanes = at(i * 256, 256)
+                return [
+                    pltpu.make_async_copy(wg_in.at[:, lanes], wg.at[:, lanes], sems.at[0, i]),
+                    pltpu.make_async_copy(wu_in.at[:, lanes], wu.at[:, lanes], sems.at[1, i]),
+                    pltpu.make_async_copy(wd_in.at[lanes, :], wd.at[lanes, :], sems.at[2, i]),
+                ]
+
+            for i in range(FF // 256):
+                for c in copies(i):
+                    c.start()
+            for k in range(S):
+                for sources_, used, target in ((xs, x_used, xp), (ys, y_used, yp)):
+                    values = [
+                        part[0][mt[SRC + k], n, :] if len(part) == 1 else part[k][n, :]
+                        for part, n in zip(sources_, used)
+                    ]
+                    if pad > size:
+                        values.append(jnp.zeros((pad - size, D), BF))
+                    value = values[0] if len(values) == 1 else jnp.concatenate(values, axis=0)
+                    target[k * pad : (k + 1) * pad, :] = value
+            sums[...] = jnp.zeros_like(sums)
+
+            def first(i, carry):
+                lanes = at(i * 256, 256)
+                for c in copies(i):
+                    c.wait()
+                g = dot(xp[...], wg[:, lanes])
+                u = dot(xp[...], wu[:, lanes])
+                z = dot_nt(yp[...], wd[lanes, :])
+                sig = 1.0 / (1.0 + jnp.exp(-g))
+                silu = g * sig
+                hidden = (silu * u).astype(BF)
+                hid[:, lanes] = hidden
+                du_out[:, lanes] = (z * silu).astype(BF)
+                dg_out[:, lanes] = (z * u * sig * (1.0 + g * (1.0 - sig))).astype(BF)
+                sums[...] += jnp.sum(z * hidden.astype(F32), axis=1, keepdims=True)
+                return carry
+
+            lax.fori_loop(0, FF // 256, first, 0)
+
+            def second(i, carry):
+                cols = at(i * 512, 512)
+                back = dot_nt(dg_out[...], wg[cols, :]) + dot_nt(du_out[...], wu[cols, :])
+                front = dot(hid[...], wd[:, cols])
+                for k in range(S):
+                    for n, part in enumerate(outs):
+                        low = k * pad + int(starts[n])
+                        high = k * pad + int(starts[n + 1])
+                        part[k][:, cols] = back[low:high].astype(BF)
+                    part = front[k * pad : k * pad + size].astype(BF)
+                    if joint:
+                        fronts[0][mt[SRC + k], :, cols] = part
+                    else:
+                        fronts[k][0:size, cols] = part
+                    if front_rows > size:
+                        fronts[k][size:, cols] = jnp.zeros((front_rows - size, 512), BF)
+                return carry
+
+            lax.fori_loop(0, D // 512, second, 0)
+            mine = iota((pad, 128), 1) == mt[EXP]
+            for k in range(S):
+                term = jnp.where(mine, sums[k * pad : (k + 1) * pad, 0:1], 0.0)
+                for n, part in enumerate(outs):
+                    part[k][:, D:] = term[int(starts[n]) : int(starts[n + 1])].astype(BF)
+
+        result = run(
+            body,
+            [shaped((b, W), BF) for b in back_sizes for _ in range(S)]
+            + (
+                [shaped((S, size, D), BF)]
+                if joint
+                else [shaped((max(size, front_rows), D), BF)] * S
+            )
+            + [shaped((rows, D), BF)] * 2
+            + [shaped((rows, FF), BF)] * 3,
+            [meta_s]
+            + flat(x_parts)
+            + flat(y_parts)
+            + [("a", gate_w), ("a", up_w), ("a", down_w)],
+            [
+                pltpu.VMEM((rows, 128), F32),
+                pltpu.VMEM((D, FF), BF),
+                pltpu.VMEM((D, FF), BF),
+                pltpu.VMEM((FF, D), BF),
+                pltpu.SemaphoreType.DMA((3, FF // 256)),
+            ],
+            alone=True,
+        )
+        count = len(back_sizes)
+        returned = [result[i * S : (i + 1) * S] for i in range(count)]
+        rest = result[S * count :]
+        return returned, rest[:front_count], rest[front_count:]
+
+    pair = 2 * cap
+    rest = flat(near_pairs[:-1])
+    rest_rows = pair * (len(near_pairs) - 1)
+    (last_back,), last_front, last_kept = expert(
+        [(h2_near[-1], pair + cap, 0)],
+        [([dy_near], pair + cap, rest_rows)],
+        [pair + cap],
+        0,
+        True,
+    )
+    (h2_near[0],) = gate(h2_near[0])
+    near_back, rest_front, rest_kept = expert(
+        [([part], pair, 0) for part in h2_near[:-1]],
+        [([dy_near], rest_rows, 0)],
+        [pair] * (len(near_pairs) - 1),
+        0,
+        True,
+    )
+    arrive(h2_far)
+    last_back = exchange(gate(*last_back))
+    (far_back,), far_front, far_kept = expert(
+        [(h2_far, 3 * cap, 0)], [(dy_far, 3 * cap, 0)], [3 * cap], T + 16
+    )
+    arrive(last_back)
+    far_back = exchange(gate(*far_back))
 
     def gate_body(*refs):
         m, rest = refs[0], refs[1:]
         tokens = regroup(rest, walk.blocks)
         rest = rest[sum(len(b) for b in walk.blocks) :]
-        router, table, key, gates_k, own, slots = rest
+        router, table, key, gates_k, own, *slots = rest
         line = iota((E, T), 0).astype(F32)
         for r in range(N):
             logits = [dot_nt(router[...], t[...]) for t in tokens[r]]
@@ -775,155 +940,15 @@
                 )
                 gates_k[r, k : k + 1, :] = value
                 pick = jnp.where(iota((cap, T), 0).astype(F32) == key[r, k : k + 1, :], 1.0, 0.0)
-                slots[k, r : r + 1, :] = dot_nt(
+                slots[k][r : r + 1, :] = dot_nt(
                     jnp.broadcast_to(value, (8, T)), pick, EXACT
                 )[0:1]
 
-    gate_k, gate_own, slot_gates = run(
+    gate_k, gate_own, *slot_gates = run(
         gate_body,
-        [shaped((N, SP, T), F32), shaped((T, 128), F32), shaped((S, N, cap), F32)],
+        [shaped((N, SP, T), F32), shaped((T, 128), F32)] + [shaped((N, cap), F32)] * S,
         [meta_s] + flat(walk.blocks) + [router_t, route_t, keys],
     )
-
-    slot_pieces = [slot_gates[0]] + [swap(slot_gates[k], k, S) for k in range(1, 3)]
-    arrive(moving)
-    arrive(slot_pieces)
-    h2_far = exchange(picked)
-    slot_pieces += [swap(slot_gates[k], k, S) for k in range(3, S)]
-
-    gate_w, up_w, down_w = w_gate[0], w_up[0], w_down[0]
-
-    def expert(x_parts, y_parts, back_sizes, front_rows=0, joint=False):
-        x_used = [used for _, used in x_parts]
-        y_used = [used for _, used in y_parts]
-        x_parts = [part for part, _ in x_parts]
-        y_parts = [part for part, _ in y_parts]
-        size = sum(x_used)
-        pad = -(-size // 16) * 16
-        rows = S * pad
-        starts = np.cumsum([0] + list(back_sizes))
-        front_count = 1 if joint else S
-
-        def body(*refs):
-            mt, rest = refs[0], refs[1:]
-            xs = regroup(rest, x_parts)
-            rest = rest[S * len(x_parts) :]
-            ys = regroup(rest, y_parts)
-            rest = rest[sum(len(p) for p in y_parts) :]
-            wg_in, wu_in, wd_in = rest[:3]
-            rest = rest[3:]
-            outs = [rest[i * S : (i + 1) * S] for i in range(len(back_sizes))]
-            rest = rest[S * len(back_sizes) :]
-            fronts, rest = rest[:front_count], rest[front_count:]
-            xp, yp, hid, dg_out, du_out, sums, wg, wu, wd, sems = rest
-
-            def copies(i):
-                lanes = at(i * 256, 256)
-                return [
-                    pltpu.make_async_copy(wg_in.at[:, lanes], wg.at[:, lanes], sems.at[0, i]),
-                    pltpu.make_async_copy(wu_in.at[:, lanes], wu.at[:, lanes], sems.at[1, i]),
-                    pltpu.make_async_copy(wd_in.at[lanes, :], wd.at[lanes, :], sems.at[2, i]),
-                ]
-
-            for i in range(FF // 256):
-                for c in copies(i):
-                    c.start()
-            for k in range(S):
-                for sources_, used, target in ((xs, x_used, xp), (ys, y_used, yp)):
-                    values = [
-                        part[0][mt[SRC + k], 0:n, :] if len(part) == 1 else part[k][0:n, :]
-                        for part, n in zip(sources_, used)
-                    ]
-                    if pad > size:
-                        values.append(jnp.zeros((pad - size, D), BF))
-                    value = values[0] if len(values) == 1 else jnp.concatenate(values, axis=0)
-                    target[k * pad : (k + 1) * pad, :] = value
-            sums[...] = jnp.zeros_like(sums)
-
-            def first(i, carry):
-                lanes = at(i * 256, 256)
-                for c in copies(i):
-                    c.wait()
-                g = dot(xp[...], wg[:, lanes])
-                u = dot(xp[...], wu[:, lanes])
-                z = dot_nt(yp[...], wd[lanes, :])
-                sig = 1.0 / (1.0 + jnp.exp(-g))
-                silu = g * sig
-                hidden = (silu * u).astype(BF)
-                hid[:, lanes] = hidden
-                du_out[:, lanes] = (z * silu).astype(BF)
-                dg_out[:, lanes] = (z * u * sig * (1.0 + g * (1.0 - sig))).astype(BF)
-                sums[...] += jnp.sum(z * hidden.astype(F32), axis=1, keepdims=True)
-                return carry
-
-            lax.fori_loop(0, FF // 256, first, 0)
-
-            def second(i, carry):
-                cols = at(i * 512, 512)
-                back = dot_nt(dg_out[...], wg[cols, :]) + dot_nt(du_out[...], wu[cols, :])
-                front = dot(hid[...], wd[:, cols])
-                for k in range(S):
-                    for n, part in enumerate(outs):
-                        low = k * pad + int(starts[n])
-                        high = k * pad + int(starts[n + 1])
-                        part[k][:, cols] = back[low:high].astype(BF)
-                    part = front[k * pad : k * pad + size].astype(BF)
-                    if joint:
-                        fronts[0][mt[SRC + k], :, cols] = part
-                    else:
-                        fronts[k][0:size, cols] = part
-                    if front_rows > size:
-                        fronts[k][size:, cols] = jnp.zeros((front_rows - size, 512), BF)
-                return carry
-
-            lax.fori_loop(0, D // 512, second, 0)
-            mine = iota((pad, 128), 1) == mt[EXP]
-            for k in range(S):
-                term = jnp.where(mine, sums[k * pad : (k + 1) * pad, 0:1], 0.0)
-                for n, part in enumerate(outs):
-                    part[k][:, D:] = term[int(starts[n]) : int(starts[n + 1])].astype(BF)
-
-        result = run(
-            body,
-            [shaped((b, W), BF) for b in back_sizes for _ in range(S)]
-            + (
-                [shaped((S, size, D), BF)]
-                if joint
-                else [shaped((max(size, front_rows), D), BF)] * S
-            )
-            + [shaped((rows, D), BF)] * 2
-            + [shaped((rows, FF), BF)] * 3,
-            [meta_s]
-            + flat(x_parts)
-            + flat(y_parts)
-            + [("a", gate_w), ("a", up_w), ("a", down_w)],
-            [
-                pltpu.VMEM((rows, 128), F32),
-                pltpu.VMEM((D, FF), BF),
-                pltpu.VMEM((D, FF), BF),
-                pltpu.VMEM((FF, D), BF),
-                pltpu.SemaphoreType.DMA((3, FF // 256)),
-            ],
-        )
-        count = len(back_sizes)
-        returned = [result[i * S : (i + 1) * S] for i in range(count)]
-        rest = result[S * count :]
-        return returned, rest[:front_count], rest[front_count:]
-
-    pair = 2 * cap
-    near_sizes = [pair] * (len(near_pairs) - 1) + [pair + cap]
-    near_used = [pair] * (len(near_pairs) - 1) + [pair + cap]
-    near_back, near_front, near_kept = expert(
-        list(zip(h2_near, near_used)), [([dy_near], sum(near_used))], near_sizes, 0, True
-    )
-    arrive(h2_far)
-    slot_pieces[3:] = gate(*slot_pieces[3:])
-    near_back[-1] = exchange(near_back[-1])
-    (far_back,), far_front, far_kept = expert(
-        [(h2_far, 3 * cap)], [(dy_far, 3 * cap)], [3 * cap], T + 16
-    )
-    arrive(near_back[-1])
-    far_back = exchange(far_back)
 
     def mix(group, pieces, split=False, first=0):
         m = len(group)
@@ -976,25 +1001,20 @@
         walk_.left -= 1
         walk_.ahead, walk_.behind = ring.forward(a), ring.backward(b)
 
-    def as_rows(values, group):
-        return jnp.stack([jnp.stack([v[r] for r in group]).reshape(-1) for v in values])
-
-    row_gates = [as_rows(slot_pieces, near), as_rows(slot_pieces, far)]
-
     def row_grad(left, right, scale_left, shape, by_column):
         def body(*refs):
-            gates, lefts, rights = refs[:2], refs[2:4], refs[4:6]
-            out, scaled = refs[6:]
+            gates, lefts, rights = refs[:S], refs[S : S + 3], refs[S + 3 : S + 6]
+            out, scaled = refs[S + 6 :]
             offset = 0
             source = lefts if scale_left else rights
-            for i, g in enumerate(gates):
-                size, rows = g.shape[1], source[i].shape[0] // S
+            for i, group in enumerate((rest, last_pair, far)):
+                rows = source[i].shape[0] // S
+                spare_rows = rows - len(group) * cap
                 for k in range(S):
-                    column = as_column(g[k : k + 1, :])
-                    if rows > size:
-                        column = jnp.concatenate(
-                            [column, jnp.zeros((rows - size, 1), F32)], axis=0
-                        )
+                    columns = [as_column(gates[k][r : r + 1, :]) for r in group]
+                    if spare_rows:
+                        columns.append(jnp.zeros((spare_rows, 1), F32))
+                    column = jnp.concatenate(columns, axis=0)
                     scaled[offset : offset + rows, :] = (
                         source[i][k * rows : (k + 1) * rows, :].astype(F32) * column
                     ).astype(BF)
@@ -1016,30 +1036,32 @@
         (result,) = run(
             body,
             [shaped(shape, F32)],
-            row_gates + list(left) + list(right),
+            slot_pieces + list(left) + list(right),
             [pltpu.VMEM((total, FF), BF)],
         )
         return result
 
-    kept = list(zip(near_kept, far_kept))
+    kept = list(zip(rest_kept, last_kept, far_kept))
     x_kept, y_kept, hid_kept, dg_kept, du_kept = kept
 
     back_parts = {}
     a, b, c = last_pair
-    back_parts[a], back_parts[b], back_parts[c] = mix(last_pair, near_back[-1])
-    grad_gate = row_grad(x_kept, dg_kept, False, (D, FF), False)
+    back_parts[a], back_parts[b], back_parts[c] = mix(last_pair, last_back)
     arrive(far_back)
+    slot_gates[1:] = gate(*slot_gates[1:])
     far_top, far_bottom = mix(far[2:], far_back, split=True, first=2)
     back = Reduce(ring, chain, far_top, far_bottom)
+    slot_pieces = [slot_gates[0]] + [swap(slot_gates[k], k, S) for k in range(1, S)]
     back_parts[far[0]], back_parts[far[1]] = mix(far[:2], far_back)
 
     def back_step():
         back.step(back_parts[back.left], back_parts[N - back.left])
 
     back_step()
+    arrive(slot_pieces)
     grads = [
+        lambda: row_grad(x_kept, dg_kept, False, (D, FF), False),
         lambda: row_grad(x_kept, du_kept, False, (D, FF), False),
-        lambda: row_grad(hid_kept, y_kept, True, (FF, D), True),
     ]
     done_grads = []
     for i in range(len(near_pairs) - 1):
@@ -1054,7 +1076,7 @@
         done_grads.append(grads.pop(0)())
     while back.left > 0:
         back_step()
-    grad_up, grad_down = done_grads
+    grad_gate, grad_up = done_grads
     arrive(far_front)
     y_parts = {}
     y_parts[far[0]], y_parts[far[1]], y_top, y_bottom = mix(far, far_front, split=True)
@@ -1107,7 +1129,8 @@
         if bit == S // 2:
             front.step(y_parts[half - 1], y_parts[N - half + 1])
         elif not front_sent:
-            near_front = [all_to_all(gate(near_front[0])[0])]
+            (near_front,) = gate(jnp.concatenate(rest_front + last_front, axis=1))
+            near_front = [all_to_all(near_front)]
             front_sent = True
         bit //= 2
     da_rows = [da_have[k] for k in range(S)]
@@ -1259,9 +1282,8 @@
             x2[...] + own[...] + ahead[...].astype(F32) + behind[...].astype(F32)
         ).astype(BF)
 
-    grad_k, grad_v = grad_k.astype(BF), grad_v.astype(BF)
     if replicas > 1:
-        both = jnp.concatenate([grad_k, grad_v], axis=1).astype(F32)
+        both = jnp.concatenate([grad_k, grad_v], axis=1).astype(BF).astype(F32)
         bit = 1
         while bit < replicas:
             both = both + swap(both.astype(BF), bit, S).astype(F32)
@@ -1275,7 +1297,7 @@
         k_raw = raw[...]
         factor = row_scale(k_raw)
         nk = k_raw * factor
-        dkn = turn(dk[...].astype(F32), cos[...], -sin[...])
+        dkn = turn(dk[...].astype(BF).astype(F32), cos[...], -sin[...])
         k_part = jnp.sum(dkn * nk, axis=0, keepdims=True) * (1.0 / replicas)
         dn = dkn * gq[1:2, :]
         dk_raw = factor * (dn - nk * jnp.mean(dn * nk, axis=-1, keepdims=True))
@@ -1409,6 +1431,7 @@
         y_parts[r] = part
     while block_walk.left > 0 or bits:
         tail_step()
+    front.step(y_parts[front.left], y_parts[N - front.left])
     out_pieces = [out_have[k] for k in range(S)]
     tail_pieces = [tail_have[k] for k in range(S)]
     out_pieces[1:] = gate(*out_pieces[1:])
@@ -1452,7 +1475,9 @@
     for k in sorted(block_have):
         block_have[k ^ bit] = swap(block_have[k], bit, S)
 
-    front.step(y_parts[front.left], y_parts[N - front.left])
+    grad_down = row_grad(hid_kept, y_kept, True, (FF, D), True)
+    while front.left > 0:
+        front.step(y_parts[front.left], y_parts[N - front.left])
     while bit > 1:
         bit //= 2
         for k in sorted(block_have):
@@ -1460,8 +1485,6 @@
                 (block_have[k],) = gate(block_have[k])
             block_have[k ^ bit] = swap(block_have[k], bit, S)
     block_pieces = [block_have[k] for k in range(S)]
-    while front.left > 0:
-        front.step(y_parts[front.left], y_parts[N - front.left])
     block_pieces[1:] = gate(*block_pieces[1:])
 
     def join_body(*refs):

time: 706 us -> 651 us (0.922)
  Pallas kernels: 308 us -> 207 us
  local copies, waits for them, and re-layouts: 33 us -> 50 us
  waiting for transfers between devices: 203 us -> 220 us
  starting transfers between devices: 136 us -> 150 us
    pallas_call x52 -> x53, Pallas kernels: 308 us -> 207 us  [run(): pl.pallas_call(call, out_shape=list(outs) + [shaped((8, 128), F32)], in_s...]
    unnamed x200 -> x338, local copies, waits for them, and re-layouts: 21.2 us -> 44.4 us
    ppermute x32, waiting for transfers between devices: 96.8 us -> 111 us  [forward(): return lax.ppermute(value, 'shard', self.up)]
    ppermute x48 -> x45, starting transfers between devices: 62.9 us -> 71.2 us  [swap(): return lax.ppermute(value, 'seq', [(i, i ^ bit) for i in range(count)])]
    all_to_all x2 -> x3, starting transfers between devices: 14.6 us -> 22 us  [all_to_all(): return lax.all_to_all(rows, 'seq', 0, 0, tiled=True)]
    ppermute x48 -> x45, waiting for transfers between devices: 77.9 us -> 80 us  [swap(): return lax.ppermute(value, 'seq', [(i, i ^ bit) for i in range(count)])]
  transfers between devices with their start and end apart: 116 -> 114, of which waited for: 49 -> 60; matrix products, arithmetic and copies ran while one was open for 3% -> 2% of each run, Pallas kernels for 39% -> 30%
where the time goes in v4:
time: 651 us; the launch traced here: 638 us
  waiting for transfers between devices  220 us (34%)
  Pallas kernels  207 us (32%)
  starting transfers between devices  150 us (23%)
  local copies, waits for them, and re-layouts  50 us (8%)
  other arithmetic  8.78 us (1%)
    pallas_call x53, Pallas kernels, run(): pl.pallas_call(call, out_shape=list(outs) + [shaped((8, 128), F32)], in_s...  207 us
    ppermute x32, waiting for transfers between devices, forward(): return lax.ppermute(value, 'shard', self.up)  111 us
    ppermute x45, waiting for transfers between devices, swap(): return lax.ppermute(value, 'seq', [(i, i ^ bit) for i in range(count)])  80 us
    ppermute x45, starting transfers between devices, swap(): return lax.ppermute(value, 'seq', [(i, i ^ bit) for i in range(count)])  71.2 us
    unnamed x338, local copies, waits for them, and re-layouts  44.4 us
    ppermute x32, starting transfers between devices, forward(): return lax.ppermute(value, 'shard', self.up)  31.2 us
    ppermute x32, starting transfers between devices, backward(): return lax.ppermute(value, 'shard', self.down)  24.3 us
    all_to_all x3, starting transfers between devices, all_to_all(): return lax.all_to_all(rows, 'seq', 0, 0, tiled=True)  22 us
  transfers between devices with their start and end apart: 114, of which 60 were waited for; matrix products, arithmetic and copies ran while one was open for 2% of the time, Pallas kernels for 30%

profile of v4, /device:TPU:5, one launch (start us, length us, event | category | flops | bytes accessed | tf_op | source)
XLA Modules:
  0.0 638.0 jit_solution(15101067289562366732)
XLA Ops:
  11.1 13.2 %collective-permute-done.2.refs_15_.refs_12_ = bf16[272,1280]{1,0:T(8,128)(2,1)S(1)} collective-permute-done((bf16[272,1280]{1,0:T(8,128)(2,1)}, bf16[272,1280]{1,0:T(8,128)(2,1)S(1)}, u32[]{:S(2)}, u32[]{:S(2)}) %collective-permute-start.2) | collective-permute-done | bytes 696352 | tf_op jit(solution)/shard_map/ppermute | solution.py:56
  27.3 11.6 %collective-permute-done.1.refs_3_ = bf16[144,2048]{1,0:T(8,128)(2,1)} collective-permute-done((bf16[144,2048]{1,0:T(8,128)(2,1)}, bf16[144,2048]{1,0:T(8,128)(2,1)}, u32[]{:S(2)}, u32[]{:S(2)}) %collective-permute-start.1) | collective-permute-done | bytes 589856 | tf_op jit(solution)/shard_map/ppermute | solution.py:130
  47.1 7.9 %collective-permute-done.7.refs_13_.refs_10_ = bf16[272,1280]{1,0:T(8,128)(2,1)S(1)} collective-permute-done((bf16[272,1280]{1,0:T(8,128)(2,1)}, bf16[272,1280]{1,0:T(8,128)(2,1)S(1)}, u32[]{:S(2)}, u32[]{:S(2)}) %collective-permute-start.7) | collective-permute-done | bytes 696352 | tf_op jit(solution)/shard_map/ppermute | solution.py:56
  59.7 15.6 %collective-permute-done.9.refs_2_.refs_5_ = bf16[128,2048]{1,0:T(8,128)(2,1)} collective-permute-done((bf16[128,2048]{1,0:T(8,128)(2,1)S(1)}, bf16[128,2048]{1,0:T(8,128)(2,1)}, u32[]{:S(2)}, u32[]{:S(2)}) %collective-permute-start.9) | collective-permute-done | bytes 524320 | tf_op jit(solution)/shard_map/ppermute | solution.py:415
  75.2 5.5 collective-permute-done.10.refs_11_.refs_8_
  85.4 11.2 %shard_map.292 = (bf16[512,2048]{1,0:T(8,128)(2,1)}, f32[512,1280]{1,0:T(8,128)}, bf16[512,128]{1,0:T(8,128)(2,1)}, bf16[512,128]{1,0:T(8,128)(2,1)}, f32[512,51...) custom-call(s32[28]{0:T(128)} %concatenate.15.refs_0_, ...), custom_call_target="tpu_custom_call", output_to_operand_aliasing={{11}: (16, {})} | custom-call | flops 1048576 | bytes 65536 | tf_op jit(solution)/shard_map/pallas_call | solution.py:185
  104.3 12.4 %shard_map.293 = (bf16[512,1024]{1,0:T(8,128)(2,1)S(1)}, bf16[512,1024]{1,0:T(8,128)(2,1)S(1)}, f32[8,128]{1,0:T(8,128)S(1)}) custom-call(f32[512,1280]{1,0:T(8,128)S(1)} %copy-done.2, bf16[512,128]{1,0:T(8,128)(2,1)S(1)} %copy-done.80, bf16[512,128]{1,0:T(8,128)(2,1)S(1)} %copy-done.82, f32[512,512]{1,0:T(8,128)S(1)} %copy-done.24, ...), custom_call_target="tpu_custom_call", output_to_operand_aliasing={{2}: (7, {})} | custom-call | flops 1048576 | bytes 65536 | tf_op jit(solution)/shard_map/pallas_call | solution.py:185
  125.2 8.7 %all-to-all-start = ((bf16[4,200,2048]{2,1,0:T(8,128)(2,1)}), bf16[4,200,2048]{2,1,0:T(8,128)(2,1)}, u32[]{:S(2)}, u32[]{:S(2)}) async-start(bf16[4,200,2048]{2,1,0:T(8,128)(2,1)} %copy-done.51), calls=%async_computation | async-start | bytes 6553600 | tf_op jit(solution)/shard_map/all_to_all | solution.py:621
  135.6 12.0 %collective-permute-done.18.refs_9_.refs_12_ = bf16[128,2048]{1,0:T(8,128)(2,1)S(1)} collective-permute-done((bf16[128,2048]{1,0:T(8,128)(2,1)}, bf16[128,2048]{1,0:T(8,128)(2,1)S(1)}, u32[]{:S(2)}, u32[]{:S(2)}) %collective-permute-start.18) | collective-permute-done | bytes 524320 | tf_op jit(solution)/shard_map/ppermute | solution.py:56
  150.5 10.9 %collective-permute-done.20.refs_8_.refs_11_ = bf16[128,2048]{1,0:T(8,128)(2,1)S(1)} collective-permute-done((bf16[128,2048]{1,0:T(8,128)(2,1)S(1)}, bf16[128,2048]{1,0:T(8,128)(2,1)S(1)}, u32[]{:S(2)}, u32[]{:S(2)}) %collective-permute-start.20) | collective-permute-done | bytes 524320 | tf_op jit(solution)/shard_map/ppermute | solution.py:56
  181.2 8.5 %collective-permute-done.27.refs_3_ = bf16[128,2048]{1,0:T(8,128)(2,1)S(1)} collective-permute-done((bf16[128,2048]{1,0:T(8,128)(2,1)S(1)}, bf16[128,2048]{1,0:T(8,128)(2,1)S(1)}, u32[]{:S(2)}, u32[]{:S(2)}) %collective-permute-start.27) | collective-permute-done | bytes 524320 | tf_op jit(solution)/shard_map/ppermute | solution.py:56
  220.5 12.2 %collective-permute-done.37.refs_8_ = bf16[136,2048]{1,0:T(8,128)(2,1)S(1)} collective-permute-done((bf16[136,2048]{1,0:T(8,128)(2,1)S(1)}, bf16[136,2048]{1,0:T(8,128)(2,1)S(1)}, u32[]{:S(2)}, u32[]{:S(2)}) %collective-permute-start.37) | collective-permute-done | bytes 557088 | tf_op jit(solution)/shard_map/ppermute | solution.py:130
  235.7 10.6 %collective-permute-done.38.refs_3_.refs_7_ = bf16[128,2048]{1,0:T(8,128)(2,1)S(1)} collective-permute-done((bf16[128,2048]{1,0:T(8,128)(2,1)S(1)}, bf16[128,2048]{1,0:T(8,128)(2,1)S(1)}, u32[]{:S(2)}, u32[]{:S(2)}) %collective-permute-start.38) | collective-permute-done | bytes 524320 | tf_op jit(solution)/shard_map/ppermute | solution.py:56
  246.6 9.6 %collective-permute-done.44.refs_4_ = bf16[136,2048]{1,0:T(8,128)(2,1)S(1)} collective-permute-done((bf16[136,2048]{1,0:T(8,128)(2,1)S(1)}, bf16[136,2048]{1,0:T(8,128)(2,1)S(1)}, u32[]{:S(2)}, u32[]{:S(2)}) %collective-permute-start.44) | collective-permute-done | bytes 557088 | tf_op jit(solution)/shard_map/ppermute | solution.py:130
  264.1 5.5 collective-permute-done.40.refs_4_.refs_5_
  278.2 19.9 %shard_map.302 = (bf16[120,2176]{1,0:T(8,128)(2,1)}, bf16[120,2176]{1,0:T(8,128)(2,1)}, bf16[120,2176]{1,0:T(8,128)(2,1)}, bf16[120,2176]{1,0:T(8,128)(2,1)}, bf...) custom-call(s32[28]{0:T(128)} %concatenate.15.refs_0_, ...), custom_call_target="tpu_custom_call", output_to_operand_aliasing={{10}: (9, {})} | custom-call | flops 1048576 | bytes 65536 | tf_op jit(solution)/shard_map/pallas_call | solution.py:185
  298.1 14.6 %shard_map.303 = (bf16[80,2176]{1,0:T(8,128)(2,1)}, bf16[80,2176]{1,0:T(8,128)(2,1)}, bf16[80,2176]{1,0:T(8,128)(2,1)}, bf16[80,2176]{1,0:T(8,128)(2,1)}, bf16[4...) custom-call(s32[28]{0:T(128)} %concatenate.15.refs_0_, ...), custom_call_target="tpu_custom_call", output_to_operand_aliasing={{10}: (6, {})} | custom-call | flops 1048576 | bytes 65536 | tf_op jit(solution)/shard_map/pallas_call | solution.py:185
  314.9 19.4 %shard_map.304 = (bf16[120,2176]{1,0:T(8,128)(2,1)}, bf16[120,2176]{1,0:T(8,128)(2,1)}, bf16[120,2176]{1,0:T(8,128)(2,1)}, bf16[120,2176]{1,0:T(8,128)(2,1)}, bf...) custom-call(s32[28]{0:T(128)} %concatenate.15.refs_0_, ...), custom_call_target="tpu_custom_call", output_to_operand_aliasing={{13}: (12, {})} | custom-call | flops 1048576 | bytes 65536 | tf_op jit(solution)/shard_map/pallas_call | solution.py:185
  346.8 5.7 shard_map.305
  357.3 5.7 collective-permute-done.53.refs_6_
  383.8 9.3 %shard_map.310 = (f32[2048,768]{1,0:T(8,128)}, f32[8,128]{1,0:T(8,128)S(1)}) custom-call(f32[8,40]{1,0:T(8,128)S(1)} %get-tuple-element.585.refs_0_, f32[8,40]{1,0:T(8,128)S(1)} %collective-permute-done.61.refs_1_, f32[8,40]{1,0:T(8,128)S(1)} %collective-permute-done.62.refs_2_, ...), custom_call_target="tpu_custom_call", output_to_operand_aliasing={{1}: (10, {})} | custom-call | flops 1048576 | bytes 65536 | tf_op jit(solution)/shard_map/pallas_call | solution.py:185
  403.0 9.2 %shard_map.312 = (f32[2048,768]{1,0:T(8,128)}, f32[8,128]{1,0:T(8,128)S(1)}) custom-call(f32[8,40]{1,0:T(8,128)S(1)} %get-tuple-element.585.refs_0_, f32[8,40]{1,0:T(8,128)S(1)} %collective-permute-done.61.refs_1_, f32[8,40]{1,0:T(8,128)S(1)} %collective-permute-done.62.refs_2_, ...), custom_call_target="tpu_custom_call", output_to_operand_aliasing={{1}: (10, {})} | custom-call | flops 1048576 | bytes 65536 | tf_op jit(solution)/shard_map/pallas_call | solution.py:185
  416.1 13.1 %collective-permute-done.70.refs_6_ = bf16[144,2048]{1,0:T(8,128)(2,1)S(1)} collective-permute-done((bf16[144,2048]{1,0:T(8,128)(2,1)S(1)}, bf16[144,2048]{1,0:T(8,128)(2,1)S(1)}, u32[]{:S(2)}, u32[]{:S(2)}) %collective-permute-start.70) | collective-permute-done | bytes 589856 | tf_op jit(solution)/shard_map/ppermute | solution.py:130
  438.4 5.5 collective-permute-done.72.refs_1_
  458.7 5.3 shard_map.318
  471.5 7.6 %shard_map.320 = (bf16[512,512]{1,0:T(8,128)(2,1)S(1)}, f32[512,128]{1,0:T(8,128)S(1)}, f32[512,128]{1,0:T(8,128)S(1)}, f32[8,128]{1,0:T(8,128)S(1)}, f32[8,128]{1,0:T(8,128)S(1)}) custom-call(f32[512,1280]{1,0:T(8,128)S(1)} %copy-done.3, bf16[512,1024]{1,0:T(8,128)(2,1)S(1)} %copy-done.48, ...), custom_call_target="tpu_custom_call", output_to_operand_aliasing={{4}: (12, {})} | custom-call | flops 1048576 | bytes 65536 | tf_op jit(solution)/shard_map/pallas_call | solution.py:185
  486.0 7.6 %shard_map.322 = (bf16[512,512]{1,0:T(8,128)(2,1)S(1)}, f32[512,128]{1,0:T(8,128)S(1)}, f32[512,128]{1,0:T(8,128)S(1)}, f32[8,128]{1,0:T(8,128)S(1)}, f32[8,128]{1,0:T(8,128)S(1)}) custom-call(f32[512,1280]{1,0:T(8,128)S(1)} %copy-done.3, bf16[512,1024]{1,0:T(8,128)(2,1)S(1)} %copy-done.48, ...), custom_call_target="tpu_custom_call", output_to_operand_aliasing={{4}: (12, {})} | custom-call | flops 1048576 | bytes 65536 | tf_op jit(solution)/shard_map/pallas_call | solution.py:185
  499.3 8.7 %all-to-all-start.2 = ((bf16[4,200,2048]{2,1,0:T(8,128)(2,1)}), bf16[4,200,2048]{2,1,0:T(8,128)(2,1)}, u32[]{:S(2)}, u32[]{:S(2)}) async-start(bf16[4,200,2048]{2,1,0:T(8,128)(2,1)} %pad_maximum_fusion), calls=%async_computation.2 | async-start | bytes 6553600 | tf_op jit(solution)/shard_map/all_to_all | solution.py:621
  524.5 6.2 shard_map.330
  535.3 22.6 %collective-permute-start.95 = (bf16[128,2048]{1,0:T(8,128)(2,1)S(1)}, bf16[128,2048]{1,0:T(8,128)(2,1)S(1)}, u32[]{:S(2)}, u32[]{:S(2)}) collective-permute-start(bf16[128,2048]{1,0:T(8,128)(2,1)S(1)} %get-tuple-element.712), channel_id=1, source_target_pairs={{0,8},{8,0},{16,24},{24,16},{1,9},{9,1},{17,25},{25,17},{2,10},{10... | collective-permute-start | bytes 1572872 | tf_op jit(solution)/shard_map/ppermute | solution.py:130
  572.2 9.2 %collective-permute-start.103 = (bf16[128,2048]{1,0:T(8,128)(2,1)S(1)}, bf16[128,2048]{1,0:T(8,128)(2,1)S(1)}, u32[]{:S(2)}, u32[]{:S(2)}) collective-permute-start(bf16[128,2048]{1,0:T(8,128)(2,1)S(1)} %collective-permute-done.94.refs_3_), channel_id=1, source_target_pairs={{0,8},{8,0},{16,24},{24,16},{1,9},{9,1},{17,25},{25,17},{2,10},{10... | collective-permute-start | bytes 1572872 | tf_op jit(solution)/shard_map/ppermute | solution.py:130
  605.2 9.0 %shard_map.339 = (f32[768,2048]{1,0:T(8,128)}, f32[8,128]{1,0:T(8,128)S(1)}) custom-call(f32[8,40]{1,0:T(8,128)S(1)} %get-tuple-element.585.refs_0_, f32[8,40]{1,0:T(8,128)S(1)} %collective-permute-done.61.refs_1_, f32[8,40]{1,0:T(8,128)S(1)} %collective-permute-done.62.refs_2_, ...), custom_call_target="tpu_custom_call", output_to_operand_aliasing={{1}: (10, {})} | custom-call | flops 1048576 | bytes 65536 | tf_op jit(solution)/shard_map/pallas_call | solution.py:185
  (629 shorter events, 301.5 us)
Async XLA Ops:
  45.9 29.3 %collective-permute-start.9 = (bf16[128,2048]{1,0:T(8,128)(2,1)S(1)}, bf16[128,2048]{1,0:T(8,128)(2,1)}, u32[]{:S(2)}, u32[]{:S(2)}) collective-permute-start(bf16[128,2048]{1,0:T(8,128)(2,1)S(1)} %constant_dynamic-slice_fusion), channel_id=1, source_target_pairs={{8,0},{9,1},{24,2},{25,3},{0,4},{1,5},{16,6},{17,7},{10,8},{11,9},... | collective-permute-start | bytes 1572872 | tf_op jit(solution)/shard_map/ppermute | solution.py:415
  56.0 24.7 %collective-permute-start.10 = (bf16[128,1280]{1,0:T(8,128)(2,1)S(1)}, bf16[128,1280]{1,0:T(8,128)(2,1)S(1)}, u32[]{:S(2)}, u32[]{:S(2)}) collective-permute-start(bf16[128,1280]{1,0:T(8,128)(2,1)S(1)} %slice.54), channel_id=1, source_target_pairs={{0,2},{2,4},{4,6},{6,7},{7,5},{5,3},{3,1},{1,0},{8,10},{10,12},{12... | collective-permute-start | bytes 983048 | tf_op jit(solution)/shard_map/ppermute | solution.py:56
  57.4 23.4 %collective-permute-start.11 = (bf16[144,1280]{1,0:T(8,128)(2,1)S(1)}, bf16[144,1280]{1,0:T(8,128)(2,1)S(1)}, u32[]{:S(2)}, u32[]{:S(2)}) collective-permute-start(bf16[144,1280]{1,0:T(8,128)(2,1)S(1)} %slice.55), channel_id=1, source_target_pairs={{2,0},{4,2},{6,4},{7,6},{5,7},{3,5},{1,3},{0,1},{10,8},{12,10},{14... | collective-permute-start | bytes 1105928 | tf_op jit(solution)/shard_map/ppermute | solution.py:59
  96.6 20.7 %collective-permute-start.14 = (bf16[128,2048]{1,0:T(8,128)(2,1)}, bf16[128,2048]{1,0:T(8,128)(2,1)S(1)}, u32[]{:S(2)}, u32[]{:S(2)}) collective-permute-start(bf16[128,2048]{1,0:T(8,128)(2,1)} %collective-permute-done.12.refs_5_), channel_id=1, source_target_pairs={{0,2},{2,4},{4,6},{6,7},{7,5},{5,3},{3,1},{1,0},{8,10},{10,12},{12... | collective-permute-start | bytes 1572872 | tf_op jit(solution)/shard_map/ppermute | solution.py:56
  125.2 56.0 %all-to-all-start = ((bf16[4,200,2048]{2,1,0:T(8,128)(2,1)}), bf16[4,200,2048]{2,1,0:T(8,128)(2,1)}, u32[]{:S(2)}, u32[]{:S(2)}) async-start(bf16[4,200,2048]{2,1,0:T(8,128)(2,1)} %copy-done.51), calls=%async_computation | async-start | bytes 6553600 | tf_op jit(solution)/shard_map/all_to_all | solution.py:621
  206.0 26.7 %collective-permute-start.37 = (bf16[136,2048]{1,0:T(8,128)(2,1)S(1)}, bf16[136,2048]{1,0:T(8,128)(2,1)S(1)}, u32[]{:S(2)}, u32[]{:S(2)}) collective-permute-start(bf16[136,2048]{1,0:T(8,128)(2,1)S(1)} %get-tuple-element.490), channel_id=1, source_target_pairs={{0,24},{8,16},{16,8},{24,0},{1,25},{9,17},{17,9},{25,1},{2,26},{10... | collective-permute-start | bytes 1671176 | tf_op jit(solution)/shard_map/ppermute | solution.py:130
  209.2 23.5 %collective-permute-start.33 = (bf16[128,2048]{1,0:T(8,128)(2,1)S(1)}, bf16[128,2048]{1,0:T(8,128)(2,1)S(1)}, u32[]{:S(2)}, u32[]{:S(2)}) collective-permute-start(bf16[128,2048]{1,0:T(8,128)(2,1)S(1)} %collective-permute-done.31.refs_3_.refs_9_), channel_id=1, source_target_pairs={{0,2},{2,4},{4,6},{6,7},{7,5},{5,3},{3,1},{1,0},{8,10},{10,12},{12... | collective-permute-start | bytes 1572872 | tf_op jit(solution)/shard_map/ppermute | solution.py:56
  210.1 22.6 %collective-permute-start.34 = (bf16[128,2048]{1,0:T(8,128)(2,1)S(1)}, bf16[128,2048]{1,0:T(8,128)(2,1)S(1)}, u32[]{:S(2)}, u32[]{:S(2)}) collective-permute-start(bf16[128,2048]{1,0:T(8,128)(2,1)S(1)} %collective-permute-done.32.refs_2_), channel_id=1, source_target_pairs={{2,0},{4,2},{6,4},{7,6},{5,7},{3,5},{1,3},{0,1},{10,8},{12,10},{14... | collective-permute-start | bytes 1572872 | tf_op jit(solution)/shard_map/ppermute | solution.py:59
  213.1 33.4 %collective-permute-start.42 = (bf16[136,2048]{1,0:T(8,128)(2,1)S(1)}, bf16[136,2048]{1,0:T(8,128)(2,1)S(1)}, u32[]{:S(2)}, u32[]{:S(2)}) collective-permute-start(bf16[136,2048]{1,0:T(8,128)(2,1)S(1)} %get-tuple-element.501), channel_id=1, source_target_pairs={{0,8},{8,0},{16,24},{24,16},{1,9},{9,1},{17,25},{25,17},{2,10},{10... | collective-permute-start | bytes 1671176 | tf_op jit(solution)/shard_map/ppermute | solution.py:130
  220.3 26.3 %collective-permute-start.43 = (bf16[136,2048]{1,0:T(8,128)(2,1)S(1)}, bf16[136,2048]{1,0:T(8,128)(2,1)S(1)}, u32[]{:S(2)}, u32[]{:S(2)}) collective-permute-start(bf16[136,2048]{1,0:T(8,128)(2,1)S(1)} %get-tuple-element.502), channel_id=1, source_target_pairs={{0,16},{8,24},{16,0},{24,8},{1,17},{9,25},{17,1},{25,9},{2,18},{10... | collective-permute-start | bytes 1671176 | tf_op jit(solution)/shard_map/ppermute | solution.py:130
  232.7 23.5 %collective-permute-start.44 = (bf16[136,2048]{1,0:T(8,128)(2,1)S(1)}, bf16[136,2048]{1,0:T(8,128)(2,1)S(1)}, u32[]{:S(2)}, u32[]{:S(2)}) collective-permute-start(bf16[136,2048]{1,0:T(8,128)(2,1)S(1)} %get-tuple-element.503), channel_id=1, source_target_pairs={{0,24},{8,16},{16,8},{24,0},{1,25},{9,17},{17,9},{25,1},{2,26},{10... | collective-permute-start | bytes 1671176 | tf_op jit(solution)/shard_map/ppermute | solution.py:130
  257.0 41.0 %all-to-all-start.1 = ((bf16[4,80,2048]{2,1,0:T(8,128)(2,1)}), bf16[4,80,2048]{2,1,0:T(8,128)(2,1)}, u32[]{:S(2)}, u32[]{:S(2)}) async-start(bf16[4,80,2048]{2,1,0:T(8,128)(2,1)} %copy-done.75), calls=%async_computation.1 | async-start | bytes 2621440 | tf_op jit(solution)/shard_map/all_to_all | solution.py:621
  275.4 37.2 %collective-permute-start.45 = (bf16[120,2048]{1,0:T(8,128)(2,1)}, bf16[120,2048]{1,0:T(8,128)(2,1)}, u32[]{:S(2)}, u32[]{:S(2)}) collective-permute-start(bf16[120,2048]{1,0:T(8,128)(2,1)} %get-tuple-element.513), channel_id=1, source_target_pairs={{0,8},{8,0},{16,24},{24,16},{1,9},{9,1},{17,25},{25,17},{2,10},{10... | collective-permute-start | bytes 1474568 | tf_op jit(solution)/shard_map/ppermute | solution.py:130
  276.5 36.2 %collective-permute-start.46 = (bf16[120,2048]{1,0:T(8,128)(2,1)}, bf16[120,2048]{1,0:T(8,128)(2,1)}, u32[]{:S(2)}, u32[]{:S(2)}) collective-permute-start(bf16[120,2048]{1,0:T(8,128)(2,1)} %get-tuple-element.514), channel_id=1, source_target_pairs={{0,16},{8,24},{16,0},{24,8},{1,17},{9,25},{17,1},{25,9},{2,18},{10... | collective-permute-start | bytes 1474568 | tf_op jit(solution)/shard_map/ppermute | solution.py:130
  277.9 34.8 %collective-permute-start.47 = (bf16[120,2048]{1,0:T(8,128)(2,1)}, bf16[120,2048]{1,0:T(8,128)(2,1)}, u32[]{:S(2)}, u32[]{:S(2)}) collective-permute-start(bf16[120,2048]{1,0:T(8,128)(2,1)} %get-tuple-element.515), channel_id=1, source_target_pairs={{0,24},{8,16},{16,8},{24,0},{1,25},{9,17},{17,9},{25,1},{2,26},{10... | collective-permute-start | bytes 1474568 | tf_op jit(solution)/shard_map/ppermute | solution.py:130
  312.7 21.6 %collective-permute-start.48 = (bf16[120,2176]{1,0:T(8,128)(2,1)}, bf16[120,2176]{1,0:T(8,128)(2,1)}, u32[]{:S(2)}, u32[]{:S(2)}) collective-permute-start(bf16[120,2176]{1,0:T(8,128)(2,1)} %get-tuple-element.544), channel_id=1, source_target_pairs={{0,8},{8,0},{16,24},{24,16},{1,9},{9,1},{17,25},{25,17},{2,10},{10... | collective-permute-start | bytes 1566728 | tf_op jit(solution)/shard_map/ppermute | solution.py:130
  312.9 21.4 %collective-permute-start.49 = (bf16[120,2176]{1,0:T(8,128)(2,1)}, bf16[120,2176]{1,0:T(8,128)(2,1)}, u32[]{:S(2)}, u32[]{:S(2)}) collective-permute-start(bf16[120,2176]{1,0:T(8,128)(2,1)} %get-tuple-element.545), channel_id=1, source_target_pairs={{0,16},{8,24},{16,0},{24,8},{1,17},{9,25},{17,1},{25,9},{2,18},{10... | collective-permute-start | bytes 1566728 | tf_op jit(solution)/shard_map/ppermute | solution.py:130
  314.3 23.7 %collective-permute-start.50 = (bf16[120,2176]{1,0:T(8,128)(2,1)}, bf16[120,2176]{1,0:T(8,128)(2,1)}, u32[]{:S(2)}, u32[]{:S(2)}) collective-permute-start(bf16[120,2176]{1,0:T(8,128)(2,1)} %get-tuple-element.546), channel_id=1, source_target_pairs={{0,24},{8,16},{16,8},{24,0},{1,25},{9,17},{17,9},{25,1},{2,26},{10... | collective-permute-start | bytes 1566728 | tf_op jit(solution)/shard_map/ppermute | solution.py:130
  338.0 19.3 %collective-permute-start.51 = (bf16[120,2176]{1,0:T(8,128)(2,1)}, bf16[120,2176]{1,0:T(8,128)(2,1)S(1)}, u32[]{:S(2)}, u32[]{:S(2)}) collective-permute-start(bf16[120,2176]{1,0:T(8,128)(2,1)} %get-tuple-element.561), channel_id=1, source_target_pairs={{0,8},{8,0},{16,24},{24,16},{1,9},{9,1},{17,25},{25,17},{2,10},{10... | collective-permute-start | bytes 1566728 | tf_op jit(solution)/shard_map/ppermute | solution.py:130
  338.0 19.3 %collective-permute-start.52 = (bf16[120,2176]{1,0:T(8,128)(2,1)}, bf16[120,2176]{1,0:T(8,128)(2,1)S(1)}, u32[]{:S(2)}, u32[]{:S(2)}) collective-permute-start(bf16[120,2176]{1,0:T(8,128)(2,1)} %get-tuple-element.562), channel_id=1, source_target_pairs={{0,16},{8,24},{16,0},{24,8},{1,17},{9,25},{17,1},{25,9},{2,18},{10... | collective-permute-start | bytes 1566728 | tf_op jit(solution)/shard_map/ppermute | solution.py:130
  339.4 23.6 %collective-permute-start.53 = (bf16[120,2176]{1,0:T(8,128)(2,1)}, bf16[120,2176]{1,0:T(8,128)(2,1)S(1)}, u32[]{:S(2)}, u32[]{:S(2)}) collective-permute-start(bf16[120,2176]{1,0:T(8,128)(2,1)} %get-tuple-element.563), channel_id=1, source_target_pairs={{0,24},{8,16},{16,8},{24,0},{1,25},{9,17},{17,9},{25,1},{2,26},{10... | collective-permute-start | bytes 1566728 | tf_op jit(solution)/shard_map/ppermute | solution.py:130
  374.7 23.2 %collective-permute-start.56 = (bf16[128,2176]{1,0:T(8,128)(2,1)S(1)}, bf16[128,2176]{1,0:T(8,128)(2,1)S(1)}, u32[]{:S(2)}, u32[]{:S(2)}) collective-permute-start(bf16[128,2176]{1,0:T(8,128)(2,1)S(1)} %get-tuple-element.579), channel_id=1, source_target_pairs={{0,2},{2,4},{4,6},{6,7},{7,5},{5,3},{3,1},{1,0},{8,10},{10,12},{12... | collective-permute-start | bytes 1671176 | tf_op jit(solution)/shard_map/ppermute | solution.py:56
  375.4 22.5 %collective-permute-start.57 = (bf16[128,2176]{1,0:T(8,128)(2,1)S(1)}, bf16[128,2176]{1,0:T(8,128)(2,1)S(1)}, u32[]{:S(2)}, u32[]{:S(2)}) collective-permute-start(bf16[128,2176]{1,0:T(8,128)(2,1)S(1)} %get-tuple-element.580), channel_id=1, source_target_pairs={{2,0},{4,2},{6,4},{7,6},{5,7},{3,5},{1,3},{0,1},{10,8},{12,10},{14... | collective-permute-start | bytes 1671176 | tf_op jit(solution)/shard_map/ppermute | solution.py:59
  402.3 27.0 %collective-permute-start.70 = (bf16[144,2048]{1,0:T(8,128)(2,1)S(1)}, bf16[144,2048]{1,0:T(8,128)(2,1)S(1)}, u32[]{:S(2)}, u32[]{:S(2)}) collective-permute-start(bf16[144,2048]{1,0:T(8,128)(2,1)S(1)} %copy-done.160), channel_id=1, source_target_pairs={{0,24},{8,16},{16,8},{24,0},{1,25},{9,17},{17,9},{25,1},{2,26},{10... | collective-permute-start | bytes 1769480 | tf_op jit(solution)/shard_map/ppermute | solution.py:130
  499.3 85.8 %all-to-all-start.2 = ((bf16[4,200,2048]{2,1,0:T(8,128)(2,1)}), bf16[4,200,2048]{2,1,0:T(8,128)(2,1)}, u32[]{:S(2)}, u32[]{:S(2)}) async-start(bf16[4,200,2048]{2,1,0:T(8,128)(2,1)} %pad_maximum_fusion), calls=%async_computation.2 | async-start | bytes 6553600 | tf_op jit(solution)/shard_map/all_to_all | solution.py:621
  521.6 36.3 %collective-permute-start.86 = (bf16[128,2048]{1,0:T(8,128)(2,1)S(1)}, bf16[128,2048]{1,0:T(8,128)(2,1)S(1)}, u32[]{:S(2)}, u32[]{:S(2)}) collective-permute-start(bf16[128,2048]{1,0:T(8,128)(2,1)S(1)} %get-tuple-element.682), channel_id=1, source_target_pairs={{0,8},{1,9},{2,24},{3,25},{4,0},{5,1},{6,16},{7,17},{8,10},{9,11},... | collective-permute-start | bytes 1572872 | tf_op jit(solution)/shard_map/ppermute | solution.py:1360
  533.8 32.8 %collective-permute-start.91 = (bf16[264,1280]{1,0:T(8,128)(2,1)S(1)}, bf16[264,1280]{1,0:T(8,128)(2,1)S(1)}, u32[]{:S(2)}, u32[]{:S(2)}) collective-permute-start(bf16[264,1280]{1,0:T(8,128)(2,1)S(1)} %get-tuple-element.707), channel_id=1, source_target_pairs={{0,2},{2,4},{4,6},{6,7},{7,5},{5,3},{3,1},{1,0},{8,10},{10,12},{12... | collective-permute-start | bytes 2027528 | tf_op jit(solution)/shard_map/ppermute | solution.py:56
  534.3 32.2 %collective-permute-start.92 = (bf16[264,1280]{1,0:T(8,128)(2,1)S(1)}, bf16[264,1280]{1,0:T(8,128)(2,1)S(1)}, u32[]{:S(2)}, u32[]{:S(2)}) collective-permute-start(bf16[264,1280]{1,0:T(8,128)(2,1)S(1)} %get-tuple-element.709), channel_id=1, source_target_pairs={{2,0},{4,2},{6,4},{7,6},{5,7},{3,5},{1,3},{0,1},{10,8},{12,10},{14... | collective-permute-start | bytes 2027528 | tf_op jit(solution)/shard_map/ppermute | solution.py:59
  535.3 24.1 %collective-permute-start.95 = (bf16[128,2048]{1,0:T(8,128)(2,1)S(1)}, bf16[128,2048]{1,0:T(8,128)(2,1)S(1)}, u32[]{:S(2)}, u32[]{:S(2)}) collective-permute-start(bf16[128,2048]{1,0:T(8,128)(2,1)S(1)} %get-tuple-element.712), channel_id=1, source_target_pairs={{0,8},{8,0},{16,24},{24,16},{1,9},{9,1},{17,25},{25,17},{2,10},{10... | collective-permute-start | bytes 1572872 | tf_op jit(solution)/shard_map/ppermute | solution.py:130
  567.9 31.3 %collective-permute-start.99 = (bf16[264,1280]{1,0:T(8,128)(2,1)}, bf16[264,1280]{1,0:T(8,128)(2,1)}, u32[]{:S(2)}, u32[]{:S(2)}) collective-permute-start(bf16[264,1280]{1,0:T(8,128)(2,1)} %get-tuple-element.740), channel_id=1, source_target_pairs={{0,2},{2,4},{4,6},{6,7},{7,5},{5,3},{3,1},{1,0},{8,10},{10,12},{12... | collective-permute-start | bytes 2027528 | tf_op jit(solution)/shard_map/ppermute | solution.py:56
  569.6 29.6 %collective-permute-start.100 = (bf16[264,1280]{1,0:T(8,128)(2,1)}, bf16[264,1280]{1,0:T(8,128)(2,1)}, u32[]{:S(2)}, u32[]{:S(2)}) collective-permute-start(bf16[264,1280]{1,0:T(8,128)(2,1)} %get-tuple-element.741), channel_id=1, source_target_pairs={{2,0},{4,2},{6,4},{7,6},{5,7},{3,5},{1,3},{0,1},{10,8},{12,10},{14... | collective-permute-start | bytes 2027528 | tf_op jit(solution)/shard_map/ppermute | solution.py:59
  604.1 19.4 %collective-permute-start.108 = (bf16[264,1280]{1,0:T(8,128)(2,1)S(1)}, bf16[264,1280]{1,0:T(8,128)(2,1)S(1)}, u32[]{:S(2)}, u32[]{:S(2)}) collective-permute-start(bf16[264,1280]{1,0:T(8,128)(2,1)S(1)} %get-tuple-element.761.refs_1_), channel_id=1, source_target_pairs={{0,8},{8,0},{16,24},{24,16},{1,9},{9,1},{17,25},{25,17},{2,10},{10... | collective-permute-start | bytes 2027528 | tf_op jit(solution)/shard_map/ppermute | solution.py:130
  (251 other events, 2861.6 us)

commit v5 on v4

--- a/solution.py
+++ b/solution.py
@@ -161,14 +161,15 @@
         *arrays, self.token = lax.optimization_barrier(tuple(arrays) + (self.token,))
         return arrays
 
-    def run(self, body, outs, operands, scratch=(), alone=False):
+    def run(self, body, outs, operands, scratch=(), alone=False, streamed=False):
         spaces = {"s": pltpu.SMEM, "a": pl.ANY, "v": pltpu.VMEM}
         specs, arrays = [], []
-        for item in list(operands) + [("a", self.token)]:
+        for item in operands:
             kind, array = item if isinstance(item, tuple) else ("v", item)
             specs.append(pl.BlockSpec(memory_space=spaces[kind]))
             arrays.append(array)
-        given, made = len(operands), len(outs)
+        first = max(range(len(arrays)), key=lambda i: arrays[i].ndim > 1)
+        (arrays[first],) = self.gate(arrays[first])
         need = 0
         for spec, array in list(zip(specs, arrays)) + [(None, o) for o in outs]:
             if spec is None or spec.memory_space == pltpu.VMEM:
@@ -177,24 +178,21 @@
             if getattr(item, "memory_space", None) == pltpu.VMEM:
                 need += int(np.prod(item.shape)) * jnp.dtype(item.dtype).itemsize
         limit = 60 << 20 if alone else min(60 << 20, need * 3 // 2 + (LIMIT << 20))
-
-        def call(*refs):
-            rest = refs[given + 1 :]
-            body(*refs[:given], *rest[:made], *rest[made + 1 :])
-
-        *results, self.token = pl.pallas_call(
-            call,
-            out_shape=list(outs) + [shaped((8, 128), F32)],
-            in_specs=specs,
-            out_specs=[pl.BlockSpec(memory_space=pltpu.VMEM)] * made
-            + [pl.BlockSpec(memory_space=pl.ANY)],
-            scratch_shapes=list(scratch),
-            input_output_aliases={given: made},
-            compiler_params=pltpu.CompilerParams(vmem_limit_bytes=limit),
-            cost_estimate=pl.CostEstimate(
-                flops=1 << 20, bytes_accessed=1 << 16, transcendentals=0
-            ),
-        )(*arrays)
+        results = list(
+            pl.pallas_call(
+                body,
+                out_shape=list(outs),
+                in_specs=specs,
+                out_specs=[pl.BlockSpec(memory_space=pl.ANY if streamed else pltpu.VMEM)]
+                * len(outs),
+                scratch_shapes=list(scratch),
+                compiler_params=pltpu.CompilerParams(vmem_limit_bytes=limit),
+                cost_estimate=pl.CostEstimate(
+                    flops=1 << 20, bytes_accessed=1 << 16, transcendentals=0
+                ),
+            )(*arrays)
+        )
+        (results[-1],) = self.gate(results[-1])
         return results
 
 
@@ -556,17 +554,26 @@
         alone=True,
     )
 
-    def attend_body(raw, krot, vlow, bias_, gq, cos, sin, rot, out):
-        def head(h, carry):
-            lanes = at(h * HD, HD)
-            q_raw = raw[:, lanes]
-            q = turn(q_raw * row_scale(q_raw) * gq[0:1, :], cos[...], sin[...]).astype(BF)
-            rot[:, lanes] = q
-            p = weights_of(q, krot[...], bias_[...]).astype(BF)
-            out[:, lanes] = dot(p, vlow[...]).astype(BF)
-            return carry
-
-        lax.fori_loop(0, heads, head, 0)
+    def attend_body(first_head, count):
+        def body(raw_in, krot, vlow, bias_, gq, cos, sin, rot, out, raw, sem):
+            c = pltpu.make_async_copy(
+                raw_in.at[:, pl.ds(first_head * HD, count * HD)], raw, sem
+            )
+            c.start()
+            c.wait()
+
+            def head(h, carry):
+                lanes = at(h * HD, HD)
+                q_raw = raw[:, lanes]
+                q = turn(q_raw * row_scale(q_raw) * gq[0:1, :], cos[...], sin[...]).astype(BF)
+                rot[:, lanes] = q
+                p = weights_of(q, krot[...], bias_[...]).astype(BF)
+                out[:, lanes] = dot(p, vlow[...]).astype(BF)
+                return carry
+
+            lax.fori_loop(0, count, head, 0)
+
+        return body
 
     near_pairs = [[j, N - j] for j in range(half - 2, 0, -1)]
     near = flat(near_pairs) + [0]
@@ -623,17 +630,28 @@
     last_pair = near_pairs[-1] + [0]
     longer = T + 8
     dy.step()
-    q_rot, attended = run(
-        attend_body,
-        [shaped((L, QC), BF), shaped((L, QC), BF)],
-        [qkv, k_rot, v_low, bias, gain_qk, cosines, sines],
-    )
+    calls = 2
+    per_call = heads // calls
+    q_rot, attended = [], []
+
+    def attend(i):
+        rot, out = run(
+            attend_body(i * per_call, per_call),
+            [shaped((L, per_call * HD), BF)] * 2,
+            [("a", qkv), k_rot, v_low, bias, gain_qk, cosines, sines],
+            [pltpu.VMEM((L, per_call * HD), F32), pltpu.SemaphoreType.DMA],
+        )
+        q_rot.append(rot)
+        attended.append(out)
+
+    attend(0)
     for j in range(2, half - 1):
         dy.arrive()
         if j + 1 < half - 1:
             dy.step()
     (piece,) = gate(piece)
     out_ring = Gather(ring, chain, piece)
+    attend(1)
     (dy_near,) = select(dy.blocks, near_pairs + [[0]], joint=True)
     dy_near = all_to_all(dy_near)
     while out_ring.done < half:
@@ -699,7 +717,8 @@
 
     def make_output():
         def body(*refs):
-            m, o, rest = refs[0], refs[1], refs[2:]
+            m, os, rest = refs[0], refs[1 : 1 + calls], refs[1 + calls :]
+            o = jnp.concatenate([x[...] for x in os], axis=1)
             parts = regroup(rest, out_blocks)
             rest = rest[sum(len(b) for b in out_blocks) :]
             outs, (full, sems) = rest[:S], rest[S:]
@@ -708,7 +727,7 @@
 
             def tile(i, carry):
                 lanes = at(i * 512, 512)
-                value = dot(o[...], full[:, lanes])
+                value = dot(o, full[:, lanes])
                 for j, k in enumerate(range(1, S, 2)):
                     outs[j][:, lanes] = value[k * T : (k + 1) * T].astype(BF)
                 for j, k in enumerate(range(0, S, 2)):
@@ -720,7 +739,7 @@
         result = run(
             body,
             reduce_shapes,
-            [meta_s, attended] + [("a", b) for b in flat(out_blocks)],
+            [meta_s] + attended + [("a", b) for b in flat(out_blocks)],
             [pltpu.VMEM((QC, D), BF), pltpu.SemaphoreType.DMA((N, 2))],
         )
         return result[: S // 2], result[S // 2 :]
@@ -756,6 +775,8 @@
             (picked,) = select(walk.blocks, [[j, N - j]], joint=True)
             if j == half - 2:
                 walk.step()
+                walk.finish()
+                far_rows = select(walk.blocks, [far])
             if j == 2:
                 arrive(moving)
             else:
@@ -764,8 +785,7 @@
             h2_near[half - 2 - j] = all_to_all(picked)
             if j == half - 2:
                 break
-    walk.finish()
-    h2_far = exchange(gate(*select(walk.blocks, [far])))
+    h2_far = exchange(gate(*far_rows))
 
     gate_w, up_w, down_w = w_gate[0], w_up[0], w_down[0]
 
@@ -1137,17 +1157,20 @@
     da_rows[1:] = gate(*da_rows[1:])
 
     def out_grad_body(*refs):
-        m, o, das, small = refs[0], refs[1], refs[2 : 2 + S], refs[2 + S]
-        outs, full = refs[3 + S : 4 + S + N], refs[4 + S + N]
+        m, os, rest = refs[0], refs[1 : 1 + calls], refs[1 + calls :]
+        das, small, outs, full = rest[:S], rest[S], rest[S + 1 : S + N + 2], rest[S + N + 2]
         da = jnp.concatenate([a[...] for a in das], axis=0)
         if PR % 128:
-            full[...] = dot_tn(o[...], da)
+            full[...] = dot_tn(jnp.concatenate([o[...] for o in os], axis=1), da)
+        else:
+            for i, o in enumerate(os):
+                full[:, i * per_call * HD : (i + 1) * per_call * HD] = o[...]
         cut = halfway(PR + extra_rows)
         for r in range(N):
             if PR % 128:
                 value = full[at(m[SPOT + r] * PR, PR), :]
             else:
-                value = dot_tn(o[:, at(m[SPOT + r] * PR, PR)], da)
+                value = dot_tn(full[:, at(m[SPOT + r] * PR, PR)], da)
             place = at(m[r] * slab, slab)
             tail = [small[8 * g : 8 * (g + 1), place] for g in range(E // 8 + 1)]
             used = len(tail) * slab
@@ -1171,8 +1194,8 @@
         out_grad_body,
         [shaped((PR + extra_rows, D), F32)] * (N - 1)
         + [shaped((out_cut, D), BF), shaped((PR + extra_rows - out_cut, D), BF)],
-        [meta_s, attended] + da_rows + [small_two],
-        [pltpu.VMEM((QC, D) if PR % 128 else (8, 128), F32)],
+        [meta_s] + attended + da_rows + [small_two],
+        [pltpu.VMEM((QC, D), F32) if PR % 128 else pltpu.VMEM((L, QC), BF)],
     )
     out_parts = {r: out_list[r - (r > half)] for r in range(N) if r != half}
     out_walk = Reduce(ring, chain, out_top, out_bottom)
@@ -1211,7 +1234,7 @@
             lanes_here = pl.ds(first_head * HD, count * HD)
             copies = [
                 pltpu.make_async_copy(raw_in.at[:, lanes_here], raw, sems.at[0]),
-                pltpu.make_async_copy(rot_in.at[:, lanes_here], rot, sems.at[1]),
+                pltpu.make_async_copy(rot_in, rot, sems.at[1]),
                 pltpu.make_async_copy(do_in.at[:, lanes_here], do, sems.at[2]),
             ]
             for c in copies:
@@ -1249,8 +1272,6 @@
 
         return body
 
-    calls = 2
-    per_call = heads // calls
     grad_k, grad_v = jnp.zeros((L, HD), F32), jnp.zeros((L, HD), F32)
     gain_sum = jnp.zeros((8, 128), F32)
     grad_q = []
@@ -1263,7 +1284,7 @@
                 shaped((L, HD), F32),
                 shaped((8, 128), F32),
             ],
-            [("a", qkv), ("a", q_rot), ("a", grad_heads)]
+            [("a", qkv), ("a", q_rot[i]), ("a", grad_heads)]
             + [k_rot, v_low, bias, gain_qk, cosines, sines, grad_k, grad_v, gain_sum],
             [
                 pltpu.VMEM((L, per_call * HD), F32),
@@ -1357,7 +1378,6 @@
     )
     block_top, block_bottom = weight_grad([half], split=True)
     block_walk = Reduce(ring, chain, block_top, block_bottom)
-    out_piece = lax.ppermute(out_piece, ("seq", "shard"), [(b, a) for a, b in spread])
     block_parts = {}
 
     def more_blocks(offsets):
@@ -1405,49 +1425,17 @@
         )
         return result[: S // 2], result[S // 2 :]
 
-    out_have = {0: out_piece}
-    tail_have = {0: out_tail}
-    bits = []
-    while not bits or bits[-1] > 1:
-        bits.append(bits[-1] // 2 if bits else S // 2)
-
-    def tail_step():
-        bit_ = bits.pop(0) if bits else 0
-        pairs = [(have, k) for have in (out_have, tail_have) for k in sorted(have)]
-        for have, k in pairs:
-            if bit_ and k:
-                (have[k],) = gate(have[k])
-        if block_walk.left > 0:
-            block_step()
-        for have, k in pairs:
-            if bit_:
-                if not k:
-                    (have[k],) = gate(have[k])
-                have[k ^ bit_] = swap(have[k], bit_, S)
-
-    one_own, one_got = seq_reduce(make_first, tail_step)
+    def send_pieces():
+        (moved,) = gate(out_piece)
+        return lax.ppermute(moved, ("seq", "shard"), [(b, a) for a, b in spread])
+
+    one_own, one_got = seq_reduce(make_first, block_step)
+    while block_walk.left > 0:
+        block_step()
     near_front[:] = gate(*near_front)
     for r, part in zip(near, mix(near, near_front)):
         y_parts[r] = part
-    while block_walk.left > 0 or bits:
-        tail_step()
     front.step(y_parts[front.left], y_parts[N - front.left])
-    out_pieces = [out_have[k] for k in range(S)]
-    tail_pieces = [tail_have[k] for k in range(S)]
-    out_pieces[1:] = gate(*out_pieces[1:])
-
-    def out_join_body(*refs):
-        m, pieces, tails = refs[0], refs[1 : 1 + S], refs[1 + S : 1 + 2 * S]
-        out, small = refs[1 + 2 * S :]
-        for k in range(S):
-            out[at(m[QUA + k] * PR, PR), :] = pieces[k][...].astype(F32)
-        small[...] = tree_sum([t_[...].astype(F32) for t_ in tails])
-
-    grad_out_w, tail_two = run(
-        out_join_body,
-        [shaped((S * PR, D), F32), shaped((extra_rows, D), F32)],
-        [meta_s] + out_pieces + tail_pieces,
-    )
 
     def inputs_body(x_ref, own, got, g1, dx2, out):
         x = x_ref[...].astype(F32)
@@ -1470,22 +1458,25 @@
         [shaped((block_rows, C), BF)],
         [block_parts[0], block_walk.ahead, block_walk.behind],
     )
-    block_have = {0: block_sum}
     bit = S // 2
-    for k in sorted(block_have):
-        block_have[k ^ bit] = swap(block_have[k], bit, S)
-
+    block_have = {0: block_sum, bit: swap(block_sum, bit, S)}
+    out_piece = send_pieces()
     grad_down = row_grad(hid_kept, y_kept, True, (FF, D), True)
     while front.left > 0:
         front.step(y_parts[front.left], y_parts[N - front.left])
+    tail_have = {0: out_tail, bit: swap(out_tail, bit, S)}
     while bit > 1:
         bit //= 2
-        for k in sorted(block_have):
-            if k:
-                (block_have[k],) = gate(block_have[k])
-            block_have[k ^ bit] = swap(block_have[k], bit, S)
+        for have in (block_have, tail_have):
+            for k in sorted(have):
+                if k:
+                    (have[k],) = gate(have[k])
+                have[k ^ bit] = swap(have[k], bit, S)
     block_pieces = [block_have[k] for k in range(S)]
-    block_pieces[1:] = gate(*block_pieces[1:])
+    tail_pieces = [tail_have[k] for k in range(S)]
+    bit = S // 2
+    (out_piece,) = gate(out_piece)
+    out_have = {0: out_piece, bit: swap(out_piece, bit, S)}
 
     def join_body(*refs):
         m, pieces = refs[0], refs[1 : 1 + S]
@@ -1521,6 +1512,26 @@
         [shaped((T, D), BF)],
         [x_second, y_parts[0], front.ahead, front.behind],
     )
+    while bit > 1:
+        bit //= 2
+        for k in sorted(out_have):
+            if k:
+                (out_have[k],) = gate(out_have[k])
+            out_have[k ^ bit] = swap(out_have[k], bit, S)
+    out_pieces = [out_have[k] for k in range(S)]
+
+    def out_join_body(*refs):
+        m, pieces, tails = refs[0], refs[1 : 1 + S], refs[1 + S : 1 + 2 * S]
+        out, small = refs[1 + 2 * S :]
+        for k in range(S):
+            out[at(m[QUA + k] * PR, PR), :] = pieces[k][...].astype(F32)
+        small[...] = tree_sum([t_[...].astype(F32) for t_ in tails])
+
+    grad_out_w, tail_two = run(
+        out_join_body,
+        [shaped((S * PR, D), F32), shaped((extra_rows, D), F32)],
+        [meta_s] + out_pieces + tail_pieces,
+    )
 
     grad_gain_one = one_rows[0] / norm1_gain.astype(F32)
     share = HD // N
@@ -1534,6 +1545,8 @@
     ]
     grad_router = jnp.concatenate(lines[: E // 8], axis=0).T
     grad_gain_two = lines[E // 8][0]
+
+    grad_gain_two = grad_gain_two + chain.token[0, 0]
 
     return (
         result[None],

time: 651 us -> 628 us (0.965)
  local copies, waits for them, and re-layouts: 50 us -> 30.6 us
    unnamed x338 -> x284, local copies, waits for them, and re-layouts: 44.4 us -> 26.6 us
    pallas_call x53 -> x54, Pallas kernels: 207 us -> 210 us  [run(): pl.pallas_call(body, out_shape=list(outs), in_specs=specs, out_specs=[pl....]
  transfers between devices with their start and end apart: 114 -> 114, of which waited for: 60 -> 58; matrix products, arithmetic and copies ran while one was open for 2% -> 1% of each run, Pallas kernels for 30% -> 32%
where the time goes in v5:
time: 628 us; the launch traced here: 616 us
  waiting for transfers between devices  217 us (35%)
  Pallas kernels  210 us (33%)
  starting transfers between devices  146 us (23%)
  local copies, waits for them, and re-layouts  30.6 us (5%)
  other arithmetic  9.87 us (2%)
    pallas_call x54, Pallas kernels, run(): pl.pallas_call(body, out_shape=list(outs), in_specs=specs, out_specs=[pl....  210 us
    ppermute x32, waiting for transfers between devices, forward(): return lax.ppermute(value, 'shard', self.up)  111 us
    ppermute x45, waiting for transfers between devices, swap(): return lax.ppermute(value, 'seq', [(i, i ^ bit) for i in range(count)])  79.3 us
    ppermute x45, starting transfers between devices, swap(): return lax.ppermute(value, 'seq', [(i, i ^ bit) for i in range(count)])  65.4 us
    ppermute x32, starting transfers between devices, backward(): return lax.ppermute(value, 'shard', self.down)  29 us
    ppermute x32, starting transfers between devices, forward(): return lax.ppermute(value, 'shard', self.up)  28.4 us
    unnamed x284, local copies, waits for them, and re-layouts  26.6 us
    all_to_all x3, starting transfers between devices, all_to_all(): return lax.all_to_all(rows, 'seq', 0, 0, tiled=True)  22.4 us
  transfers between devices with their start and end apart: 114, of which 58 were waited for; matrix products, arithmetic and copies ran while one was open for 1% of the time, Pallas kernels for 32%

profile of v5, /device:TPU:5, one launch (start us, length us, event | category | flops | bytes accessed | tf_op | source)
XLA Modules:
  0.0 616.2 jit_solution(14974844332658652444)
XLA Ops:
  9.1 14.5 %collective-permute-done.refs_15_.refs_12_ = bf16[272,1280]{1,0:T(8,128)(2,1)S(1)} collective-permute-done((bf16[272,1280]{1,0:T(8,128)(2,1)}, bf16[272,1280]{1,0:T(8,128)(2,1)S(1)}, u32[]{:S(2)}, u32[]{:S(2)}) %collective-permute-start) | collective-permute-done | bytes 696352 | tf_op jit(solution)/shard_map/ppermute | solution.py:56
  26.6 11.6 %collective-permute-done.4.refs_3_ = bf16[144,2048]{1,0:T(8,128)(2,1)} collective-permute-done((bf16[144,2048]{1,0:T(8,128)(2,1)}, bf16[144,2048]{1,0:T(8,128)(2,1)}, u32[]{:S(2)}, u32[]{:S(2)}) %collective-permute-start.4) | collective-permute-done | bytes 589856 | tf_op jit(solution)/shard_map/ppermute | solution.py:130
  47.4 6.9 %collective-permute-done.5.refs_13_.refs_10_ = bf16[272,1280]{1,0:T(8,128)(2,1)S(1)} collective-permute-done((bf16[272,1280]{1,0:T(8,128)(2,1)}, bf16[272,1280]{1,0:T(8,128)(2,1)S(1)}, u32[]{:S(2)}, u32[]{:S(2)}) %collective-permute-start.5) | collective-permute-done | bytes 696352 | tf_op jit(solution)/shard_map/ppermute | solution.py:56
  59.0 15.5 %collective-permute-done.9.refs_3_.refs_5_ = bf16[128,2048]{1,0:T(8,128)(2,1)S(1)} collective-permute-done((bf16[128,2048]{1,0:T(8,128)(2,1)S(1)}, bf16[128,2048]{1,0:T(8,128)(2,1)S(1)}, u32[]{:S(2)}, u32[]{:S(2)}) %collective-permute-start.9) | collective-permute-done | bytes 524320 | tf_op jit(solution)/shard_map/ppermute | solution.py:413
  74.5 5.7 collective-permute-done.7.refs_11_.refs_8_
  84.8 10.9 %shard_map.292 = (bf16[512,2048]{1,0:T(8,128)(2,1)}, f32[512,1280]{1,0:T(8,128)}, bf16[512,128]{1,0:T(8,128)(2,1)}, bf16[512,128]{1,0:T(8,128)(2,1)}, f32[512,51...) custom-call(s32[28]{0:T(128)} %concatenate.15.refs_0_.m, ...), custom_call_target="tpu_custom_call" | custom-call | flops 1048576 | bytes 65536 | tf_op jit(solution)/shard_map/pallas_call | solution.py:182
  102.7 6.4 %shard_map.293 = (bf16[512,512]{1,0:T(8,128)(2,1)S(1)}, bf16[512,512]{1,0:T(8,128)(2,1)S(1)}) custom-call(f32[512,1280]{1,0:T(8,128)S(1)} %copy-done.2, bf16[512,128]{1,0:T(8,128)(2,1)S(1)} %copy-done.33, bf16[512,128]{1,0:T(8,128)(2,1)S(1)} %copy-done.35, f32[512,512]{1,0:T(8,128)S(1)} %copy-done.5, f32[8,128]{1,0:T(8,128)S(1)} %copy-done.112, ...), custom_call_target="tpu_custom_call" | custom-call | flops 1048576 | bytes 65536 | tf_op jit(solution)/shard_map/pallas_call | solution.py:182
  111.4 6.4 %shard_map.294 = (bf16[512,512]{1,0:T(8,128)(2,1)S(1)}, bf16[512,512]{1,0:T(8,128)(2,1)S(1)}) custom-call(f32[512,1280]{1,0:T(8,128)S(1)} %copy-done.2, bf16[512,128]{1,0:T(8,128)(2,1)S(1)} %copy-done.33, bf16[512,128]{1,0:T(8,128)(2,1)S(1)} %copy-done.35, f32[512,512]{1,0:T(8,128)S(1)} %copy-done.5, f32[8,128]{1,0:T(8,128)S(1)} %copy-done.112, ...), custom_call_target="tpu_custom_call" | custom-call | flops 1048576 | bytes 65536 | tf_op jit(solution)/shard_map/pallas_call | solution.py:182
  124.0 8.5 %all-to-all-start = ((bf16[4,200,2048]{2,1,0:T(8,128)(2,1)}), bf16[4,200,2048]{2,1,0:T(8,128)(2,1)}, u32[]{:S(2)}, u32[]{:S(2)}) async-start(bf16[4,200,2048]{2,1,0:T(8,128)(2,1)} %shard_map.295), calls=%async_computation | async-start | bytes 6553600 | tf_op jit(solution)/shard_map/all_to_all | solution.py:628
  134.2 12.0 %collective-permute-done.18.refs_10_.refs_12_ = bf16[128,2048]{1,0:T(8,128)(2,1)S(1)} collective-permute-done((bf16[128,2048]{1,0:T(8,128)(2,1)}, bf16[128,2048]{1,0:T(8,128)(2,1)S(1)}, u32[]{:S(2)}, u32[]{:S(2)}) %collective-permute-start.18) | collective-permute-done | bytes 524320 | tf_op jit(solution)/shard_map/ppermute | solution.py:56
  149.1 10.9 %collective-permute-done.20.refs_9_.refs_11_ = bf16[128,2048]{1,0:T(8,128)(2,1)S(1)} collective-permute-done((bf16[128,2048]{1,0:T(8,128)(2,1)S(1)}, bf16[128,2048]{1,0:T(8,128)(2,1)S(1)}, u32[]{:S(2)}, u32[]{:S(2)}) %collective-permute-start.20) | collective-permute-done | bytes 524320 | tf_op jit(solution)/shard_map/ppermute | solution.py:56
  179.8 8.7 %collective-permute-done.27.refs_3_ = bf16[128,2048]{1,0:T(8,128)(2,1)S(1)} collective-permute-done((bf16[128,2048]{1,0:T(8,128)(2,1)}, bf16[128,2048]{1,0:T(8,128)(2,1)S(1)}, u32[]{:S(2)}, u32[]{:S(2)}) %collective-permute-start.27) | collective-permute-done | bytes 524320 | tf_op jit(solution)/shard_map/ppermute | solution.py:56
  210.7 8.1 %collective-permute-done.36.refs_7_ = bf16[136,2048]{1,0:T(8,128)(2,1)S(1)} collective-permute-done((bf16[136,2048]{1,0:T(8,128)(2,1)S(1)}, bf16[136,2048]{1,0:T(8,128)(2,1)S(1)}, u32[]{:S(2)}, u32[]{:S(2)}) %collective-permute-start.36) | collective-permute-done | bytes 557088 | tf_op jit(solution)/shard_map/ppermute | solution.py:130
  218.9 12.0 %collective-permute-done.37.refs_8_ = bf16[136,2048]{1,0:T(8,128)(2,1)S(1)} collective-permute-done((bf16[136,2048]{1,0:T(8,128)(2,1)S(1)}, bf16[136,2048]{1,0:T(8,128)(2,1)S(1)}, u32[]{:S(2)}, u32[]{:S(2)}) %collective-permute-start.37) | collective-permute-done | bytes 557088 | tf_op jit(solution)/shard_map/ppermute | solution.py:130
  237.4 6.8 %collective-permute-done.38.refs_3_.refs_7_ = bf16[128,2048]{1,0:T(8,128)(2,1)S(1)} collective-permute-done((bf16[128,2048]{1,0:T(8,128)(2,1)S(1)}, bf16[128,2048]{1,0:T(8,128)(2,1)S(1)}, u32[]{:S(2)}, u32[]{:S(2)}) %collective-permute-start.38) | collective-permute-done | bytes 524320 | tf_op jit(solution)/shard_map/ppermute | solution.py:56
  267.0 19.6 %shard_map.303 = (bf16[120,2176]{1,0:T(8,128)(2,1)}, bf16[120,2176]{1,0:T(8,128)(2,1)}, bf16[120,2176]{1,0:T(8,128)(2,1)}, bf16[120,2176]{1,0:T(8,128)(2,1)}, bf...) custom-call(s32[28]{0:T(128)} %concatenate.15.refs_0_.m, ...), custom_call_target="tpu_custom_call" | custom-call | flops 1048576 | bytes 65536 | tf_op jit(solution)/shard_map/pallas_call | solution.py:182
  286.7 14.6 %shard_map.304 = (bf16[80,2176]{1,0:T(8,128)(2,1)}, bf16[80,2176]{1,0:T(8,128)(2,1)}, bf16[80,2176]{1,0:T(8,128)(2,1)}, bf16[80,2176]{1,0:T(8,128)(2,1)}, bf16[4...) custom-call(s32[28]{0:T(128)} %concatenate.15.refs_0_.m, ...), custom_call_target="tpu_custom_call" | custom-call | flops 1048576 | bytes 65536 | tf_op jit(solution)/shard_map/pallas_call | solution.py:182
  304.7 19.5 %shard_map.305 = (bf16[120,2176]{1,0:T(8,128)(2,1)}, bf16[120,2176]{1,0:T(8,128)(2,1)}, bf16[120,2176]{1,0:T(8,128)(2,1)}, bf16[120,2176]{1,0:T(8,128)(2,1)}, bf...) custom-call(s32[28]{0:T(128)} %concatenate.15.refs_0_.m, ...), custom_call_target="tpu_custom_call" | custom-call | flops 1048576 | bytes 65536 | tf_op jit(solution)/shard_map/pallas_call | solution.py:182
  343.7 9.2 %collective-permute-done.56.refs_6_ = bf16[120,2176]{1,0:T(8,128)(2,1)S(1)} collective-permute-done((bf16[120,2176]{1,0:T(8,128)(2,1)}, bf16[120,2176]{1,0:T(8,128)(2,1)S(1)}, u32[]{:S(2)}, u32[]{:S(2)}) %collective-permute-start.56) | collective-permute-done | bytes 522272 | tf_op jit(solution)/shard_map/ppermute | solution.py:130
  371.5 9.3 %shard_map.311 = f32[2048,768]{1,0:T(8,128)} custom-call(f32[8,40]{1,0:T(8,128)S(1)} %get-tuple-element.1024.refs_0_, f32[8,40]{1,0:T(8,128)S(1)} %collective-permute-done.57.refs_1_, f32[8,40]{1,0:T(8,128)S(1)} %collective-permute-done.58.refs_2_, f32[8,40]{1,0:T(8,128)S(1)} %collective-permute-done.59.refs_3_, bf16[320,2048]{1,0:T(8,128)(2,1)S(1)} %copy-done.17, ...), custom_call_target="tpu_custom_call" | custom-call | flops 1048576 | bytes 65536 | tf_op jit(solution)/shard_map/pallas_call | solution.py:182
  391.4 9.3 %shard_map.313 = f32[2048,768]{1,0:T(8,128)} custom-call(f32[8,40]{1,0:T(8,128)S(1)} %get-tuple-element.1024.refs_0_, f32[8,40]{1,0:T(8,128)S(1)} %collective-permute-done.57.refs_1_, f32[8,40]{1,0:T(8,128)S(1)} %collective-permute-done.58.refs_2_, f32[8,40]{1,0:T(8,128)S(1)} %collective-permute-done.59.refs_3_, bf16[320,2048]{1,0:T(8,128)(2,1)S(1)} %copy-done.17, ...), custom_call_target="tpu_custom_call" | custom-call | flops 1048576 | bytes 65536 | tf_op jit(solution)/shard_map/pallas_call | solution.py:182
  404.8 12.4 %collective-permute-done.70.refs_6_ = bf16[144,2048]{1,0:T(8,128)(2,1)S(1)} collective-permute-done((bf16[144,2048]{1,0:T(8,128)(2,1)S(1)}, bf16[144,2048]{1,0:T(8,128)(2,1)S(1)}, u32[]{:S(2)}, u32[]{:S(2)}) %collective-permute-start.70) | collective-permute-done | bytes 589856 | tf_op jit(solution)/shard_map/ppermute | solution.py:130
  425.4 6.3 %collective-permute-done.73.a_in = bf16[64,2048]{1,0:T(8,128)(2,1)S(1)} collective-permute-done((bf16[64,2048]{1,0:T(8,128)(2,1)S(1)}, bf16[64,2048]{1,0:T(8,128)(2,1)S(1)}, u32[]{:S(2)}, u32[]{:S(2)}) %collective-permute-start.73) | collective-permute-done | bytes 262176 | tf_op jit(solution)/shard_map/ppermute | solution.py:56
  459.2 7.6 %shard_map.321 = (bf16[512,512]{1,0:T(8,128)(2,1)S(1)}, f32[512,128]{1,0:T(8,128)S(1)}, f32[512,128]{1,0:T(8,128)S(1)}, f32[8,128]{1,0:T(8,128)S(1)}) custom-call(f32[512,1280]{1,0:T(8,128)S(1)} %copy-done.3, bf16[512,512]{1,0:T(8,128)(2,1)S(1)} %copy-done.95, bf16[512,1024]{1,0:T(8,128)(2,1)S(1)} %shard_map.319.do_in, bf16[512,128]{1,0:T(8,128)(2,1)S(1)} %copy-done.34, ...), custom_call_target="tpu_custom_call" | custom-call | flops 1048576 | bytes 65536 | tf_op jit(solution)/shard_map/pallas_call | solution.py:182
  473.2 7.6 %shard_map.323 = (bf16[512,512]{1,0:T(8,128)(2,1)S(1)}, f32[512,128]{1,0:T(8,128)S(1)}, f32[512,128]{1,0:T(8,128)S(1)}, f32[8,128]{1,0:T(8,128)S(1)}) custom-call(f32[512,1280]{1,0:T(8,128)S(1)} %copy-done.3, bf16[512,512]{1,0:T(8,128)(2,1)S(1)} %copy-done.93, bf16[512,1024]{1,0:T(8,128)(2,1)S(1)} %shard_map.319.do_in, bf16[512,128]{1,0:T(8,128)(2,1)S(1)} %copy-done.34, ...), custom_call_target="tpu_custom_call" | custom-call | flops 1048576 | bytes 65536 | tf_op jit(solution)/shard_map/pallas_call | solution.py:182
  486.7 8.7 %all-to-all-start.2 = ((bf16[4,200,2048]{2,1,0:T(8,128)(2,1)}), bf16[4,200,2048]{2,1,0:T(8,128)(2,1)}, u32[]{:S(2)}, u32[]{:S(2)}) async-start(bf16[4,200,2048]{2,1,0:T(8,128)(2,1)} %pad_maximum_fusion), calls=%async_computation.2 | async-start | bytes 6553600 | tf_op jit(solution)/shard_map/all_to_all | solution.py:628
  511.1 6.2 %shard_map.331 = (bf16[128,2048]{1,0:T(8,128)(2,1)S(1)}, bf16[128,2048]{1,0:T(8,128)(2,1)S(1)}, f32[128,2048]{1,0:T(8,128)S(1)}, f32[128,2048]{1,0:T(8,128)S(1)}) custom-call(s32[28]{0:T(128)S(1)} %copy-done.109, bf16[512,512]{1,0:T(8,128)(2,1)S(1)} %copy-done.13, bf16[512,512]{1,0:T(8,128)(2,1)S(1)} %copy-done.15, ...), custom_call_target="tpu_custom_call" | custom-call | flops 1048576 | bytes 65536 | tf_op jit(solution)/shard_map/pallas_call | solution.py:182
  522.4 8.9 %collective-permute-start.90 = (bf16[128,2048]{1,0:T(8,128)(2,1)S(1)}, bf16[128,2048]{1,0:T(8,128)(2,1)S(1)}, u32[]{:S(2)}, u32[]{:S(2)}) collective-permute-start(bf16[128,2048]{1,0:T(8,128)(2,1)S(1)} %get-tuple-element.980), channel_id=1, source_target_pairs={{0,8},{8,0},{16,24},{24,16},{1,9},{9,1},{17,25},{25,17},{2,10},{10... | collective-permute-start | bytes 1572872 | tf_op jit(solution)/shard_map/ppermute | solution.py:130
  555.4 9.0 %collective-permute-start.102 = (bf16[264,1280]{1,0:T(8,128)(2,1)S(1)}, bf16[264,1280]{1,0:T(8,128)(2,1)}, u32[]{:S(2)}, u32[]{:S(2)}) collective-permute-start(bf16[264,1280]{1,0:T(8,128)(2,1)S(1)} %shard_map.338.refs_1_), channel_id=1, source_target_pairs={{0,8},{8,0},{16,24},{24,16},{1,9},{9,1},{17,25},{25,17},{2,10},{10... | collective-permute-start | bytes 2027528 | tf_op jit(solution)/shard_map/ppermute | solution.py:130
  564.4 9.0 %shard_map.339 = f32[768,2048]{1,0:T(8,128)} custom-call(f32[8,40]{1,0:T(8,128)S(1)} %get-tuple-element.1024.refs_0_, f32[8,40]{1,0:T(8,128)S(1)} %collective-permute-done.57.refs_1_, f32[8,40]{1,0:T(8,128)S(1)} %collective-permute-done.58.refs_2_, f32[8,40]{1,0:T(8,128)S(1)} %collective-permute-done.59.refs_3_, bf16[320,768]{1,0:T(8,128)(2,1)S(1)} %copy-done.103, ...), custom_call_target="tpu_custom_call" | custom-call | flops 1048576 | bytes 65536 | tf_op jit(solution)/shard_map/pallas_call | solution.py:182
  574.5 7.1 %collective-permute-start.98 = (bf16[8,2048]{1,0:T(8,128)(2,1)S(1)}, bf16[8,2048]{1,0:T(8,128)(2,1)S(1)}, u32[]{:S(2)}, u32[]{:S(2)}) collective-permute-start(bf16[8,2048]{1,0:T(8,128)(2,1)S(1)} %get-tuple-element.1021.refs_5_), channel_id=1, source_target_pairs={{0,16},{8,24},{16,0},{24,8},{1,17},{9,25},{17,1},{25,9},{2,18},{10... | collective-permute-start | bytes 98312 | tf_op jit(solution)/shard_map/ppermute | solution.py:130
  583.4 7.9 %collective-permute-start.105 = (bf16[128,2048]{1,0:T(8,128)(2,1)}, bf16[128,2048]{1,0:T(8,128)(2,1)}, u32[]{:S(2)}, u32[]{:S(2)}) collective-permute-start(bf16[128,2048]{1,0:T(8,128)(2,1)} %get-tuple-element.1051), channel_id=1, source_target_pairs={{2,0},{4,2},{6,4},{7,6},{5,7},{3,5},{1,3},{0,1},{10,8},{12,10},{14... | collective-permute-start | bytes 1572872 | tf_op jit(solution)/shard_map/ppermute | solution.py:59
  (576 shorter events, 296.7 us)
Async XLA Ops:
  45.2 29.2 %collective-permute-start.9 = (bf16[128,2048]{1,0:T(8,128)(2,1)S(1)}, bf16[128,2048]{1,0:T(8,128)(2,1)S(1)}, u32[]{:S(2)}, u32[]{:S(2)}) collective-permute-start(bf16[128,2048]{1,0:T(8,128)(2,1)S(1)} %constant_dynamic-slice_fusion), channel_id=1, source_target_pairs={{8,0},{9,1},{24,2},{25,3},{0,4},{1,5},{16,6},{17,7},{10,8},{11,9},... | collective-permute-start | bytes 1572872 | tf_op jit(solution)/shard_map/ppermute | solution.py:413
  55.3 24.8 %collective-permute-start.7 = (bf16[128,1280]{1,0:T(8,128)(2,1)S(1)}, bf16[128,1280]{1,0:T(8,128)(2,1)}, u32[]{:S(2)}, u32[]{:S(2)}) collective-permute-start(bf16[128,1280]{1,0:T(8,128)(2,1)S(1)} %slice.57), channel_id=1, source_target_pairs={{0,2},{2,4},{4,6},{6,7},{7,5},{5,3},{3,1},{1,0},{8,10},{10,12},{12... | collective-permute-start | bytes 983048 | tf_op jit(solution)/shard_map/ppermute | solution.py:56
  56.7 23.5 %collective-permute-start.8 = (bf16[144,1280]{1,0:T(8,128)(2,1)S(1)}, bf16[144,1280]{1,0:T(8,128)(2,1)}, u32[]{:S(2)}, u32[]{:S(2)}) collective-permute-start(bf16[144,1280]{1,0:T(8,128)(2,1)S(1)} %slice.58), channel_id=1, source_target_pairs={{2,0},{4,2},{6,4},{7,6},{5,7},{3,5},{1,3},{0,1},{10,8},{12,10},{14... | collective-permute-start | bytes 1105928 | tf_op jit(solution)/shard_map/ppermute | solution.py:59
  109.9 22.6 %collective-permute-start.16 = (bf16[128,2048]{1,0:T(8,128)(2,1)S(1)}, bf16[128,2048]{1,0:T(8,128)(2,1)}, u32[]{:S(2)}, u32[]{:S(2)}) collective-permute-start(bf16[128,2048]{1,0:T(8,128)(2,1)S(1)} %collective-permute-done.9.refs_3_.refs_5_), channel_id=1, source_target_pairs={{0,2},{2,4},{4,6},{6,7},{7,5},{5,3},{3,1},{1,0},{8,10},{10,12},{12... | collective-permute-start | bytes 1572872 | tf_op jit(solution)/shard_map/ppermute | solution.py:56
  111.4 21.1 %collective-permute-start.17 = (bf16[128,2048]{1,0:T(8,128)(2,1)S(1)}, bf16[128,2048]{1,0:T(8,128)(2,1)}, u32[]{:S(2)}, u32[]{:S(2)}) collective-permute-start(bf16[128,2048]{1,0:T(8,128)(2,1)S(1)} %collective-permute-done.9.refs_3_.refs_5_), channel_id=1, source_target_pairs={{2,0},{4,2},{6,4},{7,6},{5,7},{3,5},{1,3},{0,1},{10,8},{12,10},{14... | collective-permute-start | bytes 1572872 | tf_op jit(solution)/shard_map/ppermute | solution.py:59
  124.0 55.8 %all-to-all-start = ((bf16[4,200,2048]{2,1,0:T(8,128)(2,1)}), bf16[4,200,2048]{2,1,0:T(8,128)(2,1)}, u32[]{:S(2)}, u32[]{:S(2)}) async-start(bf16[4,200,2048]{2,1,0:T(8,128)(2,1)} %shard_map.295), calls=%async_computation | async-start | bytes 6553600 | tf_op jit(solution)/shard_map/all_to_all | solution.py:628
  204.6 26.3 %collective-permute-start.37 = (bf16[136,2048]{1,0:T(8,128)(2,1)S(1)}, bf16[136,2048]{1,0:T(8,128)(2,1)S(1)}, u32[]{:S(2)}, u32[]{:S(2)}) collective-permute-start(bf16[136,2048]{1,0:T(8,128)(2,1)S(1)} %get-tuple-element.666), channel_id=1, source_target_pairs={{0,24},{8,16},{16,8},{24,0},{1,25},{9,17},{17,9},{25,1},{2,26},{10... | collective-permute-start | bytes 1671176 | tf_op jit(solution)/shard_map/ppermute | solution.py:130
  207.6 23.3 %collective-permute-start.33 = (bf16[128,2048]{1,0:T(8,128)(2,1)S(1)}, bf16[128,2048]{1,0:T(8,128)(2,1)S(1)}, u32[]{:S(2)}, u32[]{:S(2)}) collective-permute-start(bf16[128,2048]{1,0:T(8,128)(2,1)S(1)} %collective-permute-done.31.refs_3_.refs_9_), channel_id=1, source_target_pairs={{0,2},{2,4},{4,6},{6,7},{7,5},{5,3},{3,1},{1,0},{8,10},{10,12},{12... | collective-permute-start | bytes 1572872 | tf_op jit(solution)/shard_map/ppermute | solution.py:56
  207.9 23.0 %collective-permute-start.34 = (bf16[128,2048]{1,0:T(8,128)(2,1)S(1)}, bf16[128,2048]{1,0:T(8,128)(2,1)S(1)}, u32[]{:S(2)}, u32[]{:S(2)}) collective-permute-start(bf16[128,2048]{1,0:T(8,128)(2,1)S(1)} %collective-permute-done.32.refs_2_), channel_id=1, source_target_pairs={{2,0},{4,2},{6,4},{7,6},{5,7},{3,5},{1,3},{0,1},{10,8},{12,10},{14... | collective-permute-start | bytes 1572872 | tf_op jit(solution)/shard_map/ppermute | solution.py:59
  232.5 22.6 %collective-permute-start.42 = (bf16[136,2048]{1,0:T(8,128)(2,1)S(1)}, bf16[136,2048]{1,0:T(8,128)(2,1)S(1)}, u32[]{:S(2)}, u32[]{:S(2)}) collective-permute-start(bf16[136,2048]{1,0:T(8,128)(2,1)S(1)} %get-tuple-element.693), channel_id=1, source_target_pairs={{0,8},{8,0},{16,24},{24,16},{1,9},{9,1},{17,25},{25,17},{2,10},{10... | collective-permute-start | bytes 1671176 | tf_op jit(solution)/shard_map/ppermute | solution.py:130
  233.3 21.7 %collective-permute-start.43 = (bf16[136,2048]{1,0:T(8,128)(2,1)S(1)}, bf16[136,2048]{1,0:T(8,128)(2,1)S(1)}, u32[]{:S(2)}, u32[]{:S(2)}) collective-permute-start(bf16[136,2048]{1,0:T(8,128)(2,1)S(1)} %get-tuple-element.694), channel_id=1, source_target_pairs={{0,16},{8,24},{16,0},{24,8},{1,17},{9,25},{17,1},{25,9},{2,18},{10... | collective-permute-start | bytes 1671176 | tf_op jit(solution)/shard_map/ppermute | solution.py:130
  233.5 26.2 %collective-permute-start.44 = (bf16[136,2048]{1,0:T(8,128)(2,1)S(1)}, bf16[136,2048]{1,0:T(8,128)(2,1)}, u32[]{:S(2)}, u32[]{:S(2)}) collective-permute-start(bf16[136,2048]{1,0:T(8,128)(2,1)S(1)} %get-tuple-element.695), channel_id=1, source_target_pairs={{0,24},{8,16},{16,8},{24,0},{1,25},{9,17},{17,9},{25,1},{2,26},{10... | collective-permute-start | bytes 1671176 | tf_op jit(solution)/shard_map/ppermute | solution.py:130
  259.7 26.9 %all-to-all-start.1 = ((bf16[4,80,2048]{2,1,0:T(8,128)(2,1)}), bf16[4,80,2048]{2,1,0:T(8,128)(2,1)}, u32[]{:S(2)}, u32[]{:S(2)}) async-start(bf16[4,80,2048]{2,1,0:T(8,128)(2,1)} %shard_map.301), calls=%async_computation.1 | async-start | bytes 2621440 | tf_op jit(solution)/shard_map/all_to_all | solution.py:628
  264.8 36.4 %collective-permute-start.45 = (bf16[120,2048]{1,0:T(8,128)(2,1)}, bf16[120,2048]{1,0:T(8,128)(2,1)}, u32[]{:S(2)}, u32[]{:S(2)}) collective-permute-start(bf16[120,2048]{1,0:T(8,128)(2,1)} %copy-done.122), channel_id=1, source_target_pairs={{0,8},{8,0},{16,24},{24,16},{1,9},{9,1},{17,25},{25,17},{2,10},{10... | collective-permute-start | bytes 1474568 | tf_op jit(solution)/shard_map/ppermute | solution.py:130
  264.9 36.4 %collective-permute-start.46 = (bf16[120,2048]{1,0:T(8,128)(2,1)}, bf16[120,2048]{1,0:T(8,128)(2,1)}, u32[]{:S(2)}, u32[]{:S(2)}) collective-permute-start(bf16[120,2048]{1,0:T(8,128)(2,1)} %copy-done.121), channel_id=1, source_target_pairs={{0,16},{8,24},{16,0},{24,8},{1,17},{9,25},{17,1},{25,9},{2,18},{10... | collective-permute-start | bytes 1474568 | tf_op jit(solution)/shard_map/ppermute | solution.py:130
  266.6 35.9 %collective-permute-start.47 = (bf16[120,2048]{1,0:T(8,128)(2,1)}, bf16[120,2048]{1,0:T(8,128)(2,1)}, u32[]{:S(2)}, u32[]{:S(2)}) collective-permute-start(bf16[120,2048]{1,0:T(8,128)(2,1)} %copy-done.120), channel_id=1, source_target_pairs={{0,24},{8,16},{16,8},{24,0},{1,25},{9,17},{17,9},{25,1},{2,26},{10... | collective-permute-start | bytes 1474568 | tf_op jit(solution)/shard_map/ppermute | solution.py:130
  302.5 21.7 %collective-permute-start.48 = (bf16[120,2176]{1,0:T(8,128)(2,1)}, bf16[120,2176]{1,0:T(8,128)(2,1)}, u32[]{:S(2)}, u32[]{:S(2)}) collective-permute-start(bf16[120,2176]{1,0:T(8,128)(2,1)} %get-tuple-element.736), channel_id=1, source_target_pairs={{0,8},{8,0},{16,24},{24,16},{1,9},{9,1},{17,25},{25,17},{2,10},{10... | collective-permute-start | bytes 1566728 | tf_op jit(solution)/shard_map/ppermute | solution.py:130
  302.7 21.5 %collective-permute-start.49 = (bf16[120,2176]{1,0:T(8,128)(2,1)}, bf16[120,2176]{1,0:T(8,128)(2,1)}, u32[]{:S(2)}, u32[]{:S(2)}) collective-permute-start(bf16[120,2176]{1,0:T(8,128)(2,1)} %get-tuple-element.737), channel_id=1, source_target_pairs={{0,16},{8,24},{16,0},{24,8},{1,17},{9,25},{17,1},{25,9},{2,18},{10... | collective-permute-start | bytes 1566728 | tf_op jit(solution)/shard_map/ppermute | solution.py:130
  303.1 24.8 %collective-permute-start.50 = (bf16[120,2176]{1,0:T(8,128)(2,1)}, bf16[120,2176]{1,0:T(8,128)(2,1)}, u32[]{:S(2)}, u32[]{:S(2)}) collective-permute-start(bf16[120,2176]{1,0:T(8,128)(2,1)} %get-tuple-element.738), channel_id=1, source_target_pairs={{0,24},{8,16},{16,8},{24,0},{1,25},{9,17},{17,9},{25,1},{2,26},{10... | collective-permute-start | bytes 1566728 | tf_op jit(solution)/shard_map/ppermute | solution.py:130
  328.3 24.6 %collective-permute-start.56 = (bf16[120,2176]{1,0:T(8,128)(2,1)}, bf16[120,2176]{1,0:T(8,128)(2,1)S(1)}, u32[]{:S(2)}, u32[]{:S(2)}) collective-permute-start(bf16[120,2176]{1,0:T(8,128)(2,1)} %get-tuple-element.769), channel_id=1, source_target_pairs={{0,24},{8,16},{16,8},{24,0},{1,25},{9,17},{17,9},{25,1},{2,26},{10... | collective-permute-start | bytes 1566728 | tf_op jit(solution)/shard_map/ppermute | solution.py:130
  363.3 23.0 %collective-permute-start.62 = (bf16[128,2176]{1,0:T(8,128)(2,1)S(1)}, bf16[128,2176]{1,0:T(8,128)(2,1)S(1)}, u32[]{:S(2)}, u32[]{:S(2)}) collective-permute-start(bf16[128,2176]{1,0:T(8,128)(2,1)S(1)} %get-tuple-element.811), channel_id=1, source_target_pairs={{0,2},{2,4},{4,6},{6,7},{7,5},{5,3},{3,1},{1,0},{8,10},{10,12},{12... | collective-permute-start | bytes 1671176 | tf_op jit(solution)/shard_map/ppermute | solution.py:56
  364.0 22.3 %collective-permute-start.63 = (bf16[128,2176]{1,0:T(8,128)(2,1)S(1)}, bf16[128,2176]{1,0:T(8,128)(2,1)S(1)}, u32[]{:S(2)}, u32[]{:S(2)}) collective-permute-start(bf16[128,2176]{1,0:T(8,128)(2,1)S(1)} %get-tuple-element.812), channel_id=1, source_target_pairs={{2,0},{4,2},{6,4},{7,6},{5,7},{3,5},{1,3},{0,1},{10,8},{12,10},{14... | collective-permute-start | bytes 1671176 | tf_op jit(solution)/shard_map/ppermute | solution.py:59
  389.7 27.5 %collective-permute-start.70 = (bf16[144,2048]{1,0:T(8,128)(2,1)S(1)}, bf16[144,2048]{1,0:T(8,128)(2,1)S(1)}, u32[]{:S(2)}, u32[]{:S(2)}) collective-permute-start(bf16[144,2048]{1,0:T(8,128)(2,1)S(1)} %copy-done.133), channel_id=1, source_target_pairs={{0,24},{8,16},{16,8},{24,0},{1,25},{9,17},{17,9},{25,1},{2,26},{10... | collective-permute-start | bytes 1769480 | tf_op jit(solution)/shard_map/ppermute | solution.py:130
  486.7 51.8 %all-to-all-start.2 = ((bf16[4,200,2048]{2,1,0:T(8,128)(2,1)}), bf16[4,200,2048]{2,1,0:T(8,128)(2,1)}, u32[]{:S(2)}, u32[]{:S(2)}) async-start(bf16[4,200,2048]{2,1,0:T(8,128)(2,1)} %pad_maximum_fusion), calls=%async_computation.2 | async-start | bytes 6553600 | tf_op jit(solution)/shard_map/all_to_all | solution.py:628
  552.5 22.0 %collective-permute-start.99 = (bf16[264,1280]{1,0:T(8,128)(2,1)S(1)}, bf16[264,1280]{1,0:T(8,128)(2,1)}, u32[]{:S(2)}, u32[]{:S(2)}) collective-permute-start(bf16[264,1280]{1,0:T(8,128)(2,1)S(1)} %shard_map.338.refs_1_), channel_id=1, source_target_pairs={{0,16},{8,24},{16,0},{24,8},{1,17},{9,25},{17,1},{25,9},{2,18},{10... | collective-permute-start | bytes 2027528 | tf_op jit(solution)/shard_map/ppermute | solution.py:130
  553.3 20.0 %collective-permute-start.100 = (bf16[128,2048]{1,0:T(8,128)(2,1)S(1)}, bf16[128,2048]{1,0:T(8,128)(2,1)S(1)}, u32[]{:S(2)}, u32[]{:S(2)}) collective-permute-start(bf16[128,2048]{1,0:T(8,128)(2,1)S(1)} %get-tuple-element.1034), channel_id=1, source_target_pairs={{0,2},{2,4},{4,6},{6,7},{7,5},{5,3},{3,1},{1,0},{8,10},{10,12},{12... | collective-permute-start | bytes 1572872 | tf_op jit(solution)/shard_map/ppermute | solution.py:56
  554.2 19.2 %collective-permute-start.101 = (bf16[128,2048]{1,0:T(8,128)(2,1)S(1)}, bf16[128,2048]{1,0:T(8,128)(2,1)S(1)}, u32[]{:S(2)}, u32[]{:S(2)}) collective-permute-start(bf16[128,2048]{1,0:T(8,128)(2,1)S(1)} %get-tuple-element.1036), channel_id=1, source_target_pairs={{2,0},{4,2},{6,4},{7,6},{5,7},{3,5},{1,3},{0,1},{10,8},{12,10},{14... | collective-permute-start | bytes 1572872 | tf_op jit(solution)/shard_map/ppermute | solution.py:59
  554.8 36.5 %collective-permute-start.97 = (bf16[128,2048]{1,0:T(8,128)(2,1)S(1)}, bf16[128,2048]{1,0:T(8,128)(2,1)}, u32[]{:S(2)}, u32[]{:S(2)}) collective-permute-start(bf16[128,2048]{1,0:T(8,128)(2,1)S(1)} %copy-done.119), channel_id=1, source_target_pairs={{0,8},{1,9},{2,24},{3,25},{4,0},{5,1},{6,16},{7,17},{8,10},{9,11},... | collective-permute-start | bytes 1572872 | tf_op jit(solution)/shard_map/ppermute | solution.py:1430
  555.4 36.4 %collective-permute-start.102 = (bf16[264,1280]{1,0:T(8,128)(2,1)S(1)}, bf16[264,1280]{1,0:T(8,128)(2,1)}, u32[]{:S(2)}, u32[]{:S(2)}) collective-permute-start(bf16[264,1280]{1,0:T(8,128)(2,1)S(1)} %shard_map.338.refs_1_), channel_id=1, source_target_pairs={{0,8},{8,0},{16,24},{24,16},{1,9},{9,1},{17,25},{25,17},{2,10},{10... | collective-permute-start | bytes 2027528 | tf_op jit(solution)/shard_map/ppermute | solution.py:130
  574.5 22.6 %collective-permute-start.103 = (bf16[264,1280]{1,0:T(8,128)(2,1)}, bf16[264,1280]{1,0:T(8,128)(2,1)}, u32[]{:S(2)}, u32[]{:S(2)}) collective-permute-start(bf16[264,1280]{1,0:T(8,128)(2,1)} %collective-permute-done.99.refs_3_), channel_id=1, source_target_pairs={{0,8},{8,0},{16,24},{24,16},{1,9},{9,1},{17,25},{25,17},{2,10},{10... | collective-permute-start | bytes 2027528 | tf_op jit(solution)/shard_map/ppermute | solution.py:130
  581.6 23.6 %collective-permute-start.104 = (bf16[128,2048]{1,0:T(8,128)(2,1)}, bf16[128,2048]{1,0:T(8,128)(2,1)}, u32[]{:S(2)}, u32[]{:S(2)}) collective-permute-start(bf16[128,2048]{1,0:T(8,128)(2,1)} %get-tuple-element.1050), channel_id=1, source_target_pairs={{0,2},{2,4},{4,6},{6,7},{7,5},{5,3},{3,1},{1,0},{8,10},{10,12},{12... | collective-permute-start | bytes 1572872 | tf_op jit(solution)/shard_map/ppermute | solution.py:56
  583.4 22.2 %collective-permute-start.105 = (bf16[128,2048]{1,0:T(8,128)(2,1)}, bf16[128,2048]{1,0:T(8,128)(2,1)}, u32[]{:S(2)}, u32[]{:S(2)}) collective-permute-start(bf16[128,2048]{1,0:T(8,128)(2,1)} %get-tuple-element.1051), channel_id=1, source_target_pairs={{2,0},{4,2},{6,4},{7,6},{5,7},{3,5},{1,3},{0,1},{10,8},{12,10},{14... | collective-permute-start | bytes 1572872 | tf_op jit(solution)/shard_map/ppermute | solution.py:59
  (224 other events, 2940.6 us)
